TPU v7x, 128 devices: a whole 4x4x4 slice. The times are simulated.
128 devices in a mesh: row: 8 (over y, x_hi), col: 16 (over x_lo, z, core).
Axes of the slice: x: 4 (x_hi: 2, x_lo: 2; x = x_hi * 2 + x_lo), y: 4, z: 4, core: 2. Of those that a mesh axis runs over, the one named last changes fastest.
Arguments:
- a_blocks: float32 [8, 16, 4, 128, 128], P('row', 'col'), may hold values from -1.2 to 1.2
- a_index: int32 [8, 16, 4], P('row', 'col'), may hold values from -1 to 63, as said below
- b_blocks: float32 [8, 16, 2, 8, 128, 128], P('row', 'col'), may hold values from -1.2 to 1.2
- b_index: int32 [8, 16, 2, 8], P('row', 'col'), may hold values from -1 to 63, as said below
- c_index: int32 [8, 16, 16], P('row', 'col'), may hold values from -1 to 63, as said below
Outputs:
- c_blocks: float32 [8, 16, 16, 128, 128], P('row', 'col')
Inputs may be any that keep to these rules, and one draw needn't show every extreme that they name: `a_index`: within each tile the non-negative entries are distinct and come before the entries -1, which mark empty slots; every tile has at least one block and some tile has all 4 slots filled. `b_index`: within each panel of a device the non-negative entries are distinct and come before the entries -1, which mark empty slots; every panel has at least one block and some panel has all 8 slots filled. `c_index`: within each tile the non-negative entries are distinct and come before the entries -1, which mark empty slots; every tile keeps at least one block and some tile has all 16 slots filled.
All inputs are finite; a program needn't handle non-finite values.
Results may differ from a plain program's by a relative error of at most 0.0003.
Values sent between devices are 32-bit elements; how exact they have to be, the bound alone decides.
No kernel may reach another device: no remote copies, remote signals or barrier semaphores. Data moves between devices by JAX's collectives and lax.ppermute only.
A program may use at most 192 MiB of HBM per device.

v0:
```python
import functools

import jax
import jax.numpy as jnp
from jax import lax
from jax.experimental import pallas as pl
from jax.experimental.pallas import tpu as pltpu
from jax.sharding import Mesh
from jax.sharding import PartitionSpec as P

SA = 4
PK = 8
NBD = 8
NEAR = 6
FAR = 3
COL = ("x_lo", "z", "core")
VMEM_LIMIT = 16 << 20
A_PARTS = 8
LIST = 512
AHEAD = 8


def matmul(a, b):
    return jnp.dot(a.astype(jnp.bfloat16), b, preferred_element_type=jnp.float32)


def lands_at(a_line, b):
    meet = (a_line >= 0) & (b >= 0) & ((a_line & (PK - 1)) == (b >> 3))
    return jnp.where(meet, (a_line >> 3) * NBD + (b & (NBD - 1)), -2)


def needed(a, b, c):
    need = jnp.zeros(b.shape, jnp.bool_)
    for s in range(SA):
        lands = lands_at(a[s : s + 1], b)
        for n in range(c.shape[0]):
            need = need | (lands == c[n : n + 1])
    return need


def lane_facts(shape, axis=1):
    lane = lax.broadcasted_iota(jnp.int32, shape, axis)
    r, p = lane >> 4, lane & 15
    owner = p >> 1
    far = (((owner >> 1) - (r >> 1)) & 3) == 2
    way = ((owner ^ r) & 1) + jnp.where(far, 2, 0)
    return r, p, owner, way


def code(a_slot, part, at, c_slot):
    return ((a_slot * 16 + part) * 128 + at) * 16 + c_slot


def a_of(word):
    return word >> 15


def part_of(word):
    return (word >> 11) & 15


def at_of(word):
    return (word >> 4) & 127


def c_of(word):
    return word & 15


def fetch_a(word, a_refs, dst, sem):
    a = a_of(word)
    fetch_block(a >> 3, a & 7, a_refs, dst, sem)


def fetch_block(part, at, refs, dst, sem):
    for i, ref in enumerate(refs):

        def start(ref=ref):
            pltpu.make_async_copy(ref.at[at], dst, sem).start()

        if len(refs) == 1:
            start()
        else:
            pl.when(part == i)(start)


def make_maps(maps_ref):
    shape = maps_ref.shape[1:]
    lane = lax.broadcasted_iota(jnp.int32, shape, 1)
    down = lax.broadcasted_iota(jnp.int32, shape, 0)
    r, p, owner, way = lane_facts(shape)
    r_down, p_down, _, way_down = lane_facts(shape, 0)
    holder = (p_down == 0) & (r_down == owner)
    alike = (r == r_down) & (way == way_down)
    y, xh, xl, z, core = lane >> 5, (lane >> 4) & 1, (lane >> 3) & 1, (lane >> 1) & 3, lane & 1
    listed_at = (((core * 2 + xh) * 2 + xl) * 4 + z) * 4 + y
    for n, flags in enumerate(
        [
            holder & ((p & 1) == 0),
            holder & ((p & 1) == 1),
            (p_down == 0) & (r == r_down),
            alike,
            alike & (down < lane),
            down == listed_at,
        ]
    ):
        maps_ref[n] = jnp.where(flags, 1.0, 0.0).astype(jnp.bfloat16)


def positions(spots_ref, maps_ref):
    spots = spots_ref[...].astype(jnp.float32).astype(jnp.bfloat16)
    return lax.dot_general(
        spots, maps_ref[5], (((0,), (0,)), ((), ())), preferred_element_type=jnp.float32
    )


def plan_kernel(sends, me_ref, spots_ref, pack_list, product_list, info_ref, maps_ref):
    row, column = me_ref[0], me_ref[1]
    make_maps(maps_ref)
    held = positions(spots_ref, maps_ref)
    a = held[:8].astype(jnp.int32)
    turned = pltpu.roll(held[8:40], (128 - column) & 127, 1)
    b = matmul(turned[:8], maps_ref[0]) + matmul(turned[8:16], maps_ref[1])
    b = b.astype(jnp.int32)
    c = matmul(turned[16:32], maps_ref[2]).astype(jnp.int32)
    need = needed(a, b, c)

    r, p, owner, way = lane_facts(b.shape)
    t = lax.broadcasted_iota(jnp.int32, b.shape, 0)
    flags = jnp.where(need, 1.0, 0.0)
    alike = matmul(flags, maps_ref[3])
    upto = alike
    for step in (1, 2, 4):
        upto = upto + jnp.where(t >= step, pltpu.roll(upto, step, 0), 0.0)
    rank = (upto - alike + matmul(flags, maps_ref[4])).astype(jnp.int32)
    order = jnp.where(need, way * 128 + rank, -1)

    steps = ((owner >> 1) - (row >> 1)) & 3
    part = jnp.where(steps == 0, 0, jnp.where(steps == 3, 1, 2))
    word = (part * 16 + (p & 1) * 8 + t).astype(jnp.float32)
    n = 0
    for slots, which, there in sends:
        for e in range(slots):
            hit = (order == which * 128 + e) & (r == there(row))
            pack_list[n] = jnp.max(jnp.where(hit, word, -1.0)).astype(jnp.int32)
            n += 1

    info_ref[0:8] = a
    info_ref[8:16] = b
    info_ref[16:32] = c
    info_ref[32:40] = order
    extract(entries_of(info_ref, me_ref)[0], product_list)


def plan(me, spots, sends):
    smem = pl.BlockSpec(memory_space=pltpu.SMEM)
    vmem = pl.BlockSpec(memory_space=pltpu.VMEM)
    return pl.pallas_call(
        functools.partial(plan_kernel, sends),
        in_specs=[smem, vmem],
        out_specs=[smem, smem, vmem, vmem],
        out_shape=[
            jax.ShapeDtypeStruct((sum(n for n, *_ in sends),), jnp.int32),
            jax.ShapeDtypeStruct((LIST + 1,), jnp.int32),
            jax.ShapeDtypeStruct((40, 128), jnp.int32),
            jax.ShapeDtypeStruct((6, 128, 128), jnp.bfloat16),
        ],
        compiler_params=pltpu.CompilerParams(vmem_limit_bytes=16 << 20),
        name="plan",
    )(me, spots)


def pack_kernel(sizes, list_ref, *rest):
    near, packed, sems = rest[:3], rest[3:-1], rest[-1]
    places = [(i, e) for i, size in enumerate(sizes) for e in range(size)]
    for n, (i, e) in enumerate(places):
        word = list_ref[n]

        @pl.when(word >= 0)
        def _():
            fetch_block(word >> 4, word & 15, near, packed[i].at[e], sems.at[n])

    for n, (i, e) in enumerate(places):

        @pl.when(list_ref[n] >= 0)
        def _():
            pltpu.make_async_copy(near[0].at[0], packed[i].at[e], sems.at[n]).wait()


def pack(listing, near, sizes):
    size = near[0].shape[-1]
    return pl.pallas_call(
        functools.partial(pack_kernel, sizes),
        in_specs=[pl.BlockSpec(memory_space=pltpu.SMEM)]
        + [pl.BlockSpec(memory_space=pl.ANY)] * 3,
        out_specs=[pl.BlockSpec(memory_space=pltpu.VMEM)] * len(sizes),
        scratch_shapes=[pltpu.SemaphoreType.DMA((sum(sizes),))],
        out_shape=[jax.ShapeDtypeStruct((n, size, size), jnp.float32) for n in sizes],
        compiler_params=pltpu.CompilerParams(vmem_limit_bytes=16 << 20),
        name="pack",
    )(listing, *near)


def overflow_kernel(spots_ref, maps_ref, over_ref):
    held = positions(spots_ref, maps_ref)
    a = held[:8].astype(jnp.int32)
    turned = [held[8:40]] + [pltpu.roll(held[8:40], 128 - q, 1) for q in range(1, 16)]
    b = matmul(jnp.concatenate([x[:8] for x in turned]), maps_ref[0])
    b = b + matmul(jnp.concatenate([x[8:16] for x in turned]), maps_ref[1])
    b = b.astype(jnp.int32)
    c = matmul(jnp.concatenate([x[16:32] for x in turned]), maps_ref[2]).astype(jnp.int32)
    flags = [
        jnp.where(needed(a, b[q * 8 : q * 8 + 8], c[q * 16 : q * 16 + 16]), 1.0, 0.0)
        for q in range(16)
    ]
    alike = matmul(jnp.concatenate(flags), maps_ref[3])
    most = jnp.sum(alike[:8], axis=0, keepdims=True)
    for q in range(1, 16):
        most = jnp.maximum(most, jnp.sum(alike[q * 8 : q * 8 + 8], axis=0, keepdims=True))
    *_, way = lane_facts(most.shape)
    slots = jnp.where(way == 0, 128, jnp.where(way == 1, NEAR, FAR))
    over_ref[0] = jnp.max(jnp.where(most > slots.astype(jnp.float32), 1.0, 0.0)).astype(jnp.int32)


def overflow(spots, maps):
    vmem = pl.BlockSpec(memory_space=pltpu.VMEM)
    return pl.pallas_call(
        overflow_kernel,
        in_specs=[vmem] * 2,
        out_specs=pl.BlockSpec(memory_space=pltpu.SMEM),
        out_shape=jax.ShapeDtypeStruct((1,), jnp.int32),
        compiler_params=pltpu.CompilerParams(vmem_limit_bytes=16 << 20),
        cost_estimate=pl.CostEstimate(flops=10**9, bytes_accessed=10**5, transcendentals=0),
        name="overflow",
    )(spots, maps)


def halves(x):
    high = x.astype(jnp.bfloat16)
    return high, (x - high.astype(jnp.float32)).astype(jnp.bfloat16)


def block_product(a, b):
    a_high, a_low = halves(a)
    b_high, b_low = halves(b)
    dot = functools.partial(jnp.dot, preferred_element_type=jnp.float32)
    return dot(a_high, b_high) + (dot(a_high, b_low) + dot(a_low, b_high))


def extract(entries, list_ref):
    def more(state):
        n, word, left = state
        list_ref[n] = word.astype(jnp.int32)
        left = jnp.where(left == word, -1.0, left)
        return n + 1, jnp.max(left), left

    n, *_ = lax.while_loop(
        lambda state: state[1] >= 0, more, (jnp.int32(0), jnp.max(entries), entries)
    )
    list_ref[LIST] = n


def entries_of(info_ref, me_ref):
    row, column = me_ref[0], me_ref[1]
    b, c, order = info_ref[8:16], info_ref[16:32], info_ref[32:40]
    r, p, owner, way = lane_facts(b.shape)
    t = lax.broadcasted_iota(jnp.int32, b.shape, 0)
    rank = order & 127
    steps = ((owner >> 1) - (row >> 1)) & 3
    part = jnp.where(steps == 0, 0, jnp.where(steps == 3, 1, 2))
    sent = (way > 0) & (rank < jnp.where(way == 1, NEAR, FAR))
    along = ((p >> 1) - (column >> 1)) & 3
    beside = ((p ^ column) >> 3) & 1
    a_part = jnp.where(along == 0, 0, jnp.where(along == 3, 1, jnp.where(along == 1, 2, 3)))
    a_at = (a_part + 4 * ((p ^ column) & 1)) * 8 + beside * SA
    found = [[], []]
    for s in range(SA):
        lands = lands_at(info_ref[s : s + 1], b)
        c_slot = jnp.full(b.shape, -1, jnp.int32)
        for n in range(c.shape[0]):
            c_slot = jnp.where(lands == c[n : n + 1], n, c_slot)
        live = (c_slot >= 0) & (r == row)
        a_slot = a_at + s
        at_hand = jnp.where(
            way == 0,
            code(a_slot, part, (p & 1) * 8 + t, c_slot),
            code(a_slot, 2 + way, rank, c_slot),
        )
        elsewhere = code(a_slot, owner ^ row, (p & 1) * 8 + t, c_slot)
        found[0].append(jnp.where(live & ((way == 0) | sent), at_hand, -1).astype(jnp.float32))
        found[1].append(jnp.where(live & (way > 0) & ~sent, elsewhere, -1).astype(jnp.float32))
    return [jnp.concatenate(x) for x in found]


def multiply_listed(list_ref, a_refs, b_refs, acc, a_buf, b_buf, a_sem, b_sem, meanwhile):
    count = list_ref[LIST]

    def fetch(n):
        slot = n % AHEAD
        word = list_ref[n]
        fetch_a(word, a_refs, a_buf.at[slot], a_sem.at[slot])
        fetch_block(part_of(word), at_of(word), b_refs, b_buf.at[slot], b_sem.at[slot])

    for n in range(AHEAD):

        @pl.when(n < count)
        def _():
            fetch(n)

    meanwhile()

    def step(n, carry):
        slot = n % AHEAD
        pltpu.make_async_copy(a_refs[0].at[0], a_buf.at[slot], a_sem.at[slot]).wait()
        pltpu.make_async_copy(b_refs[0].at[0], b_buf.at[slot], b_sem.at[slot]).wait()
        acc[c_of(list_ref[n])] += block_product(a_buf[slot], b_buf[slot])

        @pl.when(n + AHEAD < count)
        def _():
            fetch(n + AHEAD)

        return carry

    lax.fori_loop(0, count, step, 0)


def all_kernel(parts, list_ref, *rest):
    a_refs, b_refs = rest[:A_PARTS], rest[A_PARTS:parts]
    out_ref, acc, c_sem, _, *buffers = rest[parts:]

    def meanwhile():
        acc[...] = jnp.zeros_like(acc)

    multiply_listed(list_ref, a_refs, b_refs, acc, *buffers, meanwhile)
    copy = pltpu.make_async_copy(acc, out_ref, c_sem.at[0])
    copy.start()
    copy.wait()


def add_listed(list_ref, a_refs, b_refs, total_ref, out_ref, acc, c_sem, stage, *buffers):
    count = list_ref[LIST]

    def touched(was, act):
        def step(n, carry):
            c = c_of(list_ref[n])

            @pl.when(stage[c] == was)
            def _():
                stage[c] = was + 1
                act(c)

            return carry

        lax.fori_loop(0, count, step, 0)

    def fetched(c):
        return pltpu.make_async_copy(total_ref.at[c], acc.at[c], c_sem.at[c])

    def stored(c):
        return pltpu.make_async_copy(acc.at[c], out_ref.at[c], c_sem.at[c])

    for c in range(acc.shape[0]):
        stage[c] = 0

    def meanwhile():
        touched(0, lambda c: fetched(c).start())
        touched(1, lambda c: fetched(c).wait())

    multiply_listed(list_ref, a_refs, b_refs, acc, *buffers, meanwhile)
    touched(2, lambda c: stored(c).start())
    touched(3, lambda c: stored(c).wait())


def rest_kernel(parts, me_ref, info_ref, *rest):
    a_refs, b_refs = rest[:A_PARTS], rest[A_PARTS:parts]
    total_ref, out_ref, rest_list, *buffers = rest[parts:]
    extract(entries_of(info_ref, me_ref)[1], rest_list)
    add_listed(rest_list, a_refs, b_refs, total_ref, out_ref, *buffers)


def products(kernel, leading, a_parts, b_parts, total, slots, own_list=False):
    size = a_parts[0].shape[-1]
    parts = len(a_parts) + len(b_parts)
    smem = pl.BlockSpec(memory_space=pltpu.SMEM)
    vmem = pl.BlockSpec(memory_space=pltpu.VMEM)
    hbm = pl.BlockSpec(memory_space=pltpu.HBM)
    operands = [*leading, *a_parts, *b_parts] + ([] if total is None else [total])
    return pl.pallas_call(
        functools.partial(kernel, parts),
        in_specs=[smem if x.ndim == 1 else vmem for x in leading]
        + [pl.BlockSpec(memory_space=pl.ANY)] * parts
        + ([] if total is None else [hbm]),
        out_specs=hbm,
        out_shape=jax.ShapeDtypeStruct((slots, size, size), jnp.float32),
        scratch_shapes=([pltpu.SMEM((LIST + 1,), jnp.int32)] if own_list else [])
        + [
            pltpu.VMEM((slots, size, size), jnp.float32),
            pltpu.SemaphoreType.DMA((slots,)),
            pltpu.SMEM((slots,), jnp.int32),
            pltpu.VMEM((AHEAD, size, size), jnp.float32),
            pltpu.VMEM((AHEAD, size, size), jnp.float32),
            pltpu.SemaphoreType.DMA((AHEAD,)),
            pltpu.SemaphoreType.DMA((AHEAD,)),
        ],
        input_output_aliases={} if total is None else {len(operands) - 1: 0},
        compiler_params=pltpu.CompilerParams(vmem_limit_bytes=VMEM_LIMIT),
        cost_estimate=pl.CostEstimate(
            flops=8 * 3 * 2 * size**3, bytes_accessed=24 * size * size * 4, transcendentals=0
        ),
        name="products",
    )(*operands)


def to_row(block, rows, there):
    return lax.ppermute(block, "row", [(i, there(i)) for i in range(rows)])


def on_z(i):
    return (i & 9) | ((i + 2) & 6)


def back_z(i):
    return (i & 9) | ((i - 2) & 6)


def moved(block, there, columns):
    return lax.ppermute(block, COL, [(i, there(i)) for i in range(columns)])


def pair_kernel(tile_ref, beside_ref, _, pair_ref, __, sems):
    n = tile_ref.shape[0]
    copies = [
        pltpu.make_async_copy(tile_ref, pair_ref.at[pl.ds(0, n)], sems.at[0]),
        pltpu.make_async_copy(beside_ref, pair_ref.at[pl.ds(n, n)], sems.at[1]),
    ]
    for copy in copies:
        copy.start()
    for copy in copies:
        copy.wait()


def paired(tile, beside, passing):
    n, size = tile.shape[0], tile.shape[-1]
    anywhere = pl.BlockSpec(memory_space=pl.ANY)
    return pl.pallas_call(
        pair_kernel,
        in_specs=[anywhere] * 3,
        out_specs=[pl.BlockSpec(memory_space=pltpu.VMEM), anywhere],
        out_shape=[
            jax.ShapeDtypeStruct((2 * n, size, size), tile.dtype),
            jax.ShapeDtypeStruct(passing.shape, passing.dtype),
        ],
        scratch_shapes=[pltpu.SemaphoreType.DMA((2,))],
        input_output_aliases={2: 1},
        compiler_params=pltpu.CompilerParams(vmem_limit_bytes=16 << 20),
        name="pair",
    )(tile, beside, passing)


def hold_kernel(*refs):
    pass


def held_for(arrays, later):
    anywhere = pl.BlockSpec(memory_space=pl.ANY)
    return pl.pallas_call(
        hold_kernel,
        in_specs=[anywhere] * (len(arrays) + len(later)),
        out_specs=[anywhere] * len(arrays),
        out_shape=[jax.ShapeDtypeStruct(x.shape, x.dtype) for x in arrays],
        input_output_aliases={i: i for i in range(len(arrays))},
        name="hold",
    )(*arrays, *later)


def among(held, bits, rows, columns):
    me = lax.axis_index("row") * columns + lax.axis_index(COL)
    group = jnp.zeros((2 ** len(bits),) + held.shape, held.dtype)
    for move in range(2 ** len(bits)):
        flip = sum(((move >> n) & 1) << bit for n, bit in enumerate(bits))
        got = held
        if move:
            pairs = [(i ^ flip, i) for i in range(rows * columns)]
            got = lax.ppermute(held, ("row", *COL), pairs)
        spot = sum((((me ^ flip) >> bit) & 1) << n for n, bit in enumerate(bits))
        group = lax.dynamic_update_index_in_dim(group, got, spot, 0)
    return group


def per_device(a_blocks, a_index, b_blocks, b_index, c_index):
    rows = lax.axis_size("row")
    columns = lax.axis_size(COL)
    row = lax.axis_index("row")
    me = jnp.stack([row, lax.axis_index(COL)])
    hold = columns // rows
    sa, sb, sc = a_blocks.shape[2], b_blocks.shape[3], c_index.shape[2]
    held = hold * sb
    size = a_blocks.shape[-1]

    own = b_blocks[0, 0].reshape(held, size, size)
    behind = to_row(own, rows, lambda i: (i + 2) % rows)
    ahead = to_row(own, rows, lambda i: (i - 2) % rows)
    near = [own, behind, ahead]

    blank = jnp.full((8 - sa,), -1, jnp.int32)
    mine = jnp.concatenate([a_index[0, 0], blank, b_index[0, 0].reshape(-1), c_index[0, 0]])
    spots = among(jnp.pad(mine, (0, 128 - mine.shape[0])), (5, 6), rows, columns)
    spots = among(spots, (1, 2), rows, columns)
    tile = a_blocks[0, 0]
    pair, spots = paired(tile, moved(tile, lambda i: i ^ 8, columns), spots)
    spots = among(spots, (3,), rows, columns)
    spots = among(spots, (4,), rows, columns)
    spots = among(spots, (0,), rows, columns).reshape(rows * columns, 128)
    a_behind = moved(pair, on_z, columns)
    a_ahead = moved(pair, back_z, columns)

    sends = [
        (FAR, 2, lambda i: (i + 2) & 7),
        (FAR, 3, lambda i: ((i + 2) & 7) ^ 1),
        (NEAR, 1, lambda i: i ^ 1),
    ]
    pack_list, product_list, info, maps = plan(me, spots, sends)
    packed = pack(pack_list, near, [n for n, *_ in sends])

    far_own, far_other, cross = [
        to_row(block, rows, there) for block, (*_, there) in zip(packed, sends)
    ]

    (a_far,) = held_for([moved(a_behind, on_z, columns)], [far_own, far_other, cross])
    a_mine = [pair, a_behind, a_ahead, a_far]
    a_parts = a_mine + [moved(block, lambda i: i ^ 1, columns) for block in a_mine]

    b_parts = near + [cross, far_own, far_other]
    total = products(all_kernel, [product_list], a_parts, b_parts, None, sc)

    trips = overflow(spots, maps)[0]

    def trip(state):
        done, total = state
        sent = jnp.where(done >= 0, own, 0)
        whole = [own] + [to_row(sent, rows, lambda i, n=n: i ^ n) for n in range(1, rows)]
        rest = products(rest_kernel, [me, info], a_parts, whole, total, sc, own_list=True)
        return done + 1, rest

    _, total = lax.while_loop(lambda state: state[0] < trips, trip, (jnp.int32(0), total))
    return total[None, None]


def solution(mesh):
    rows, columns = mesh.devices.shape
    mesh = Mesh(mesh.devices.reshape(rows, 2, columns // 4, 2), ("row", *COL))
    in_specs = (
        P("row", COL, None, None, None),
        P("row", COL, None),
        P("row", COL, None, None, None, None),
        P("row", COL, None, None),
        P("row", COL, None),
    )
    out_specs = P("row", COL, None, None, None)
    return jax.shard_map(
        per_device, mesh=mesh, in_specs=in_specs, out_specs=out_specs, check_vma=False
    )
```

profile of v0, /device:TPU:1, one launch (start us, length us, event | category | flops | bytes accessed | tf_op | source)
XLA Modules:
  0.0 64.9 jit_solution(4084921726873218158)
XLA Ops:
  0.0 0.0 copy-start.6
  0.0 0.8 %reshape_squeeze.6 = s32[16]{0:T(128)S(1)} reshape(s32[1,1,2,8]{3,2,1,0:T(2,128)} %param.10) | data formatting | bytes 128 | tf_op jit(solution)/shard_map/reshape;squeeze | solution.py:506
  0.8 0.7 %pad_add_fusion.1 = s32[40]{0:T(128)S(1)} fusion(s32[16]{0:T(128)} %bitcast.38, s32[16]{0:T(128)S(1)} %reshape_squeeze.6, s32[4]{0:T(128)S(1)} %broadcast.5, s32[4]{0:T(128)} %bitcast.39), kind=kLoop, calls=%fused_computation.12 | loop fusion | flops 120 | bytes 320 | tf_op jit(solution)/shard_map/concatenate | solution.py:506
  1.6 3.8 %collective-permute-start.9 = (s32[128]{0:T(128)S(1)}, s32[128]{0:T(128)S(1)}, u32[]{:S(2)}, u32[]{:S(2)}) collective-permute-start(s32[128]{0:T(128)S(1)} %get-tuple-element.215), channel_id=1, source_target_pairs={{64,0},{65,1},{66,2},{67,3},{68,4},{69,5},{70,6},{71,7},{72,8},{73... | collective-permute-start | bytes 1544 | tf_op jit(solution)/shard_map/ppermute | solution.py:484
  5.3 0.4 collective-permute-start.8
  5.7 0.4 collective-permute-start.10
  6.1 2.3 %collective-permute-start.21 = (f32[16,128,128]{2,1,0:T(8,128)}, f32[16,128,128]{2,1,0:T(8,128)S(1)}, u32[]{:S(2)}, u32[]{:S(2)}) collective-permute-start(f32[16,128,128]{2,1,0:T(8,128)} %bitcast.20.rest_0_.rest_8_), channel_id=1, source_target_pairs={{0,96},{16,112},{32,0},{48,16},{64,32},{80,48},{96,64},{112,80},{1... | collective-permute-start | bytes 3145736 | tf_op jit(solution)/shard_map/ppermute | solution.py:415
  8.4 0.1 pad_add_fusion.me_ref
  8.5 0.1 collective-permute-start.20
  8.6 0.0 collective-permute-done.8
  8.6 0.0 copy-done.6
  8.6 1.3 %collective-permute-start.7 = (f32[4,128,128]{2,1,0:T(8,128)S(1)}, f32[4,128,128]{2,1,0:T(8,128)S(1)}, u32[]{:S(2)}, u32[]{:S(2)}) collective-permute-start(f32[4,128,128]{2,1,0:T(8,128)S(1)} %bitcast.34), channel_id=1, source_target_pairs={{0,8},{1,9},{2,10},{3,11},{4,12},{5,13},{6,14},{7,15},{8,0},{9,1},... | collective-permute-start | bytes 786440 | tf_op jit(solution)/shard_map/ppermute | solution.py:427
  9.9 0.0 collective-permute-done.9
  10.0 0.0 collective-permute-done.10
  10.0 1.7 %collective-permute-start.11 = (s32[4,128]{1,0:T(4,128)S(1)}, s32[4,128]{1,0:T(4,128)S(1)}, u32[]{:S(2)}, u32[]{:S(2)}) collective-permute-start(s32[4,128]{1,0:T(4,128)S(1)} %dynamic_update_slice.50), channel_id=1, source_target_pairs={{2,0},{3,1},{0,2},{1,3},{6,4},{7,5},{4,6},{5,7},{10,8},{11,9},{8,1... | collective-permute-start | bytes 6152 | tf_op jit(solution)/shard_map/ppermute | solution.py:484
  11.7 3.3 %collective-permute-start.12 = (s32[4,128]{1,0:T(4,128)S(1)}, s32[4,128]{1,0:T(4,128)S(1)}, u32[]{:S(2)}, u32[]{:S(2)}) collective-permute-start(s32[4,128]{1,0:T(4,128)S(1)} %dynamic_update_slice.50), channel_id=1, source_target_pairs={{4,0},{5,1},{6,2},{7,3},{0,4},{1,5},{2,6},{3,7},{12,8},{13,9},{14,... | collective-permute-start | bytes 6152 | tf_op jit(solution)/shard_map/ppermute | solution.py:484
  15.0 0.0 collective-permute-done.11
  15.0 1.5 %collective-permute-start.13 = (s32[4,128]{1,0:T(4,128)S(1)}, s32[4,128]{1,0:T(4,128)S(1)}, u32[]{:S(2)}, u32[]{:S(2)}) collective-permute-start(s32[4,128]{1,0:T(4,128)S(1)} %dynamic_update_slice.50), channel_id=1, source_target_pairs={{6,0},{7,1},{4,2},{5,3},{2,4},{3,5},{0,6},{1,7},{14,8},{15,9},{12,... | collective-permute-start | bytes 6152 | tf_op jit(solution)/shard_map/ppermute | solution.py:484
  16.6 0.0 collective-permute-done.12
  16.6 2.4 %collective-permute-done.13 = s32[4,128]{1,0:T(4,128)S(1)} collective-permute-done((s32[4,128]{1,0:T(4,128)S(1)}, s32[4,128]{1,0:T(4,128)S(1)}, u32[]{:S(2)}, u32[]{:S(2)}) %collective-permute-start.13) | collective-permute-done | bytes 2080 | tf_op jit(solution)/shard_map/ppermute | solution.py:484
  19.0 0.0 collective-permute-done.7.beside_ref
  19.0 0.8 %pair.1 = (f32[8,128,128]{2,1,0:T(8,128)}, s32[4,4,128]{2,1,0:T(4,128)S(1)}) custom-call(f32[4,128,128]{2,1,0:T(8,128)S(1)} %bitcast.35, f32[4,128,128]{2,1,0:T(8,128)S(1)} %collective-permute-done.7.beside_ref, s32[4,4,128]{2,1,0:T(4,128)S(1)} %constant_dynamic-update-slice_fusion._), custom_call_target="tpu_custom_call", output_to_operand_aliasing={{1}: (2, {})} | custom-call | tf_op jit(solution)/shard_map/pair/pallas_call | solution.py:445
  19.8 0.7 %collective-permute-start.14 = (s32[4,4,128]{2,1,0:T(4,128)S(1)}, s32[4,4,128]{2,1,0:T(4,128)S(1)}, u32[]{:S(2)}, u32[]{:S(2)}) collective-permute-start(s32[4,4,128]{2,1,0:T(4,128)S(1)} %get-tuple-element.177), channel_id=1, source_target_pairs={{8,0},{9,1},{10,2},{11,3},{12,4},{13,5},{14,6},{15,7},{0,8},{1,9},... | collective-permute-start | bytes 24584 | tf_op jit(solution)/shard_map/ppermute | solution.py:484
  20.5 0.0 collective-permute-start.17
  20.5 2.2 %collective-permute-done.14 = s32[4,4,128]{2,1,0:T(4,128)S(1)} collective-permute-done((s32[4,4,128]{2,1,0:T(4,128)S(1)}, s32[4,4,128]{2,1,0:T(4,128)S(1)}, u32[]{:S(2)}, u32[]{:S(2)}) %collective-permute-start.14) | collective-permute-done | bytes 8224 | tf_op jit(solution)/shard_map/ppermute | solution.py:484
  22.7 2.5 %collective-permute-start.15 = (s32[2,4,4,128]{3,2,1,0:T(4,128)S(1)}, s32[2,4,4,128]{3,2,1,0:T(4,128)S(1)}, u32[]{:S(2)}, u32[]{:S(2)}) collective-permute-start(s32[2,4,4,128]{3,2,1,0:T(4,128)S(1)} %bitcast_dynamic-update-slice_fusion.4), channel_id=1, source_target_pairs={{16,0},{17,1},{18,2},{19,3},{20,4},{21,5},{22,6},{23,7},{24,8},{25... | collective-permute-start | bytes 49160 | tf_op jit(solution)/shard_map/ppermute | solution.py:484
  25.2 1.6 %collective-permute-done.15 = s32[2,4,4,128]{3,2,1,0:T(4,128)S(1)} collective-permute-done((s32[2,4,4,128]{3,2,1,0:T(4,128)S(1)}, s32[2,4,4,128]{3,2,1,0:T(4,128)S(1)}, u32[]{:S(2)}, u32[]{:S(2)}) %collective-permute-start.15) | collective-permute-done | bytes 16416 | tf_op jit(solution)/shard_map/ppermute | solution.py:484
  26.8 5.5 %collective-permute-start.16 = (s32[2,2,4,4,128]{4,3,2,1,0:T(4,128)S(1)}, s32[2,2,4,4,128]{4,3,2,1,0:T(4,128)S(1)}, u32[]{:S(2)}, u32[]{:S(2)}) collective-permute-start(s32[2,2,4,4,128]{4,3,2,1,0:T(4,128)S(1)} %bitcast_dynamic-update-slice_fusion.2), channel_id=1, source_target_pairs={{1,0},{0,1},{3,2},{2,3},{5,4},{4,5},{7,6},{6,7},{9,8},{8,9},{11,10... | collective-permute-start | bytes 98312 | tf_op jit(solution)/shard_map/ppermute | solution.py:484
  32.4 1.9 %collective-permute-start.18 = (f32[8,128,128]{2,1,0:T(8,128)}, f32[8,128,128]{2,1,0:T(8,128)}, u32[]{:S(2)}, u32[]{:S(2)}) collective-permute-start(f32[8,128,128]{2,1,0:T(8,128)} %get-tuple-element.309.rest_0_), channel_id=1, source_target_pairs={{0,6},{1,7},{2,0},{3,1},{4,2},{5,3},{6,4},{7,5},{8,14},{9,15},{10,... | collective-permute-start | bytes 1572872 | tf_op jit(solution)/shard_map/ppermute | solution.py:427
  34.3 0.0 collective-permute-done.17.rest_1_
  34.3 0.0 collective-permute-start.19
  34.3 0.0 collective-permute-done.16
  34.3 2.3 %plan.1 = (s32[12]{0:T(128)S(1)}, s32[513]{0:T(1024)S(1)}, s32[40,128]{1,0:T(8,128)S(1)}, bf16[6,128,128]{2,1,0:T(8,128)(2,1)S(1)}) custom-call(s32[2]{0:T(128)S(1)} %pad_add_fusion.me_ref, s32[128,128]{1,0:T(8,128)S(1)} %bitcast.36), custom_call_target="tpu_custom_call" | custom-call | tf_op jit(solution)/shard_map/plan/pallas_call | solution.py:158
  36.6 0.0 collective-permute-done.21.rest_2_.rest_10_
  36.6 0.0 collective-permute-done.20.rest_1_.rest_9_
  36.7 1.9 %pack.1 = (f32[3,128,128]{2,1,0:T(8,128)S(1)}, f32[3,128,128]{2,1,0:T(8,128)S(1)}, f32[6,128,128]{2,1,0:T(8,128)S(1)}) custom-call(s32[12]{0:T(128)S(1)} %get-tuple-element.180.list_ref, f32[16,128,128]{2,1,0:T(8,128)} %bitcast.20.rest_0_.rest_8_, f32[16,128,128]{2,1,0:T(8,128)S(1)} %collective-permute-done.20.rest_1_.rest_9_, ...), custom_call_target="tpu_custom_call" | custom-call | tf_op jit(solution)/shard_map/pack/pallas_call | solution.py:192
  38.6 2.3 %collective-permute-start.24 = (f32[6,128,128]{2,1,0:T(8,128)S(1)}, f32[6,128,128]{2,1,0:T(8,128)S(1)}, u32[]{:S(2)}, u32[]{:S(2)}) collective-permute-start(f32[6,128,128]{2,1,0:T(8,128)S(1)} %get-tuple-element.183), channel_id=1, source_target_pairs={{0,16},{16,0},{32,48},{48,32},{64,80},{80,64},{96,112},{112,96},{1... | collective-permute-start | bytes 1179656 | tf_op jit(solution)/shard_map/ppermute | solution.py:415
  40.9 0.0 collective-permute-start.22
  40.9 0.8 %collective-permute-start.23 = (f32[3,128,128]{2,1,0:T(8,128)S(1)}, f32[3,128,128]{2,1,0:T(8,128)S(1)}, u32[]{:S(2)}, u32[]{:S(2)}) collective-permute-start(f32[3,128,128]{2,1,0:T(8,128)S(1)} %get-tuple-element.182), channel_id=1, source_target_pairs={{0,48},{16,32},{32,80},{48,64},{64,112},{80,96},{96,16},{112,0},{1... | collective-permute-start | bytes 589832 | tf_op jit(solution)/shard_map/ppermute | solution.py:415
  41.7 4.6 %collective-permute-done.18.rest_2_ = f32[8,128,128]{2,1,0:T(8,128)} collective-permute-done((f32[8,128,128]{2,1,0:T(8,128)}, f32[8,128,128]{2,1,0:T(8,128)}, u32[]{:S(2)}, u32[]{:S(2)}) %collective-permute-start.18) | collective-permute-done | bytes 524320 | tf_op jit(solution)/shard_map/ppermute | solution.py:427
  46.3 0.8 %collective-permute-start.25 = (f32[8,128,128]{2,1,0:T(8,128)}, f32[8,128,128]{2,1,0:T(8,128)}, u32[]{:S(2)}, u32[]{:S(2)}) collective-permute-start(f32[8,128,128]{2,1,0:T(8,128)} %get-tuple-element.309.rest_0_), channel_id=1, source_target_pairs={{0,1},{1,0},{2,3},{3,2},{4,5},{5,4},{6,7},{7,6},{8,9},{9,8},{10,11... | collective-permute-start | bytes 1572872 | tf_op jit(solution)/shard_map/ppermute | solution.py:427
  47.1 0.0 collective-permute-done.22.refs_1_.rest_12_
  47.1 0.0 copy-start.2
  47.1 2.6 %collective-permute-start.26 = (f32[8,128,128]{2,1,0:T(8,128)}, f32[8,128,128]{2,1,0:T(8,128)}, u32[]{:S(2)}, u32[]{:S(2)}) collective-permute-start(f32[8,128,128]{2,1,0:T(8,128)} %collective-permute-done.17.rest_1_), channel_id=1, source_target_pairs={{0,1},{1,0},{2,3},{3,2},{4,5},{5,4},{6,7},{7,6},{8,9},{9,8},{10,11... | collective-permute-start | bytes 1572872 | tf_op jit(solution)/shard_map/ppermute | solution.py:427
  49.7 4.3 %collective-permute-done.23.refs_2_.rest_13_ = f32[3,128,128]{2,1,0:T(8,128)S(1)} collective-permute-done((f32[3,128,128]{2,1,0:T(8,128)S(1)}, f32[3,128,128]{2,1,0:T(8,128)S(1)}, u32[]{:S(2)}, u32[]{:S(2)}) %collective-permute-start.23) | collective-permute-done | bytes 196640 | tf_op jit(solution)/shard_map/ppermute | solution.py:415
  53.9 0.0 copy-start.4
  53.9 3.3 %collective-permute-start.27 = (f32[8,128,128]{2,1,0:T(8,128)}, f32[8,128,128]{2,1,0:T(8,128)}, u32[]{:S(2)}, u32[]{:S(2)}) collective-permute-start(f32[8,128,128]{2,1,0:T(8,128)} %collective-permute-done.18.rest_2_), channel_id=1, source_target_pairs={{0,1},{1,0},{2,3},{3,2},{4,5},{5,4},{6,7},{7,6},{8,9},{9,8},{10,11... | collective-permute-start | bytes 1572872 | tf_op jit(solution)/shard_map/ppermute | solution.py:427
  57.2 0.0 collective-permute-done.19.refs_0_
  57.2 0.0 collective-permute-done.24.refs_3_.rest_11_
  57.2 0.0 copy-done.2
  57.2 0.0 copy-done.4
  57.2 0.0 copy-start
  57.2 0.7 %copy-done = f32[6,128,128]{2,1,0:T(8,128)} copy-done((f32[6,128,128]{2,1,0:T(8,128)}, f32[6,128,128]{2,1,0:T(8,128)S(1)}, u32[]{:S(2)}) %copy-start) | copy-done | bytes 393240
  58.0 0.7 %collective-permute-start.28 = (f32[8,128,128]{2,1,0:T(8,128)}, f32[8,128,128]{2,1,0:T(8,128)}, u32[]{:S(2)}, u32[]{:S(2)}) collective-permute-start(f32[8,128,128]{2,1,0:T(8,128)} %hold.1.rest_3_), channel_id=1, source_target_pairs={{0,1},{1,0},{2,3},{3,2},{4,5},{5,4},{6,7},{7,6},{8,9},{9,8},{10,11... | collective-permute-start | bytes 1572872 | tf_op jit(solution)/shard_map/ppermute | solution.py:427
  58.6 1.7 %overflow.1 = s32[1]{0:T(128)} custom-call(s32[128,128]{1,0:T(8,128)S(1)} %bitcast.37, bf16[6,128,128]{2,1,0:T(8,128)(2,1)S(1)} %get-tuple-element.184.maps_ref), custom_call_target="tpu_custom_call" | custom-call | flops 1000000000 | bytes 100000 | tf_op jit(solution)/shard_map/overflow/pallas_call | solution.py:227
  60.4 0.0 collective-permute-done.25.rest_4_
  60.4 0.0 collective-permute-done.27.rest_6_
  60.4 0.0 collective-permute-done.26.rest_5_
  60.4 0.1 collective-permute-done.28.rest_7_
  60.5 0.0 copy-done.1
  60.5 0.0 copy-done.3
  60.5 0.0 copy-done.5
  60.5 3.4 %products.5 = f32[16,128,128]{2,1,0:T(8,128)} custom-call(s32[513]{0:T(1024)S(1)} %get-tuple-element.178.list_ref, f32[8,128,128]{2,1,0:T(8,128)} %get-tuple-element.309.rest_0_, f32[8,128,128]{2,1,0:T(8,128)} %collective-permute-done.17.rest_1_, f32[8,128,128]{2,1,0:T(8,128)} %collective-permute-done.18.rest_2_, f32[8,128,128]{2,1,0:T(8,128)} %hold.1.rest_3_, ...), custom_call_target="tpu_custom_call" | custom-call | flops 100663296 | bytes 1572864 | tf_op jit(solution)/shard_map/products/pallas_call | solution.py:388
  63.9 0.8 %while.12 = (s32[]{:T(128)}, f32[16,128,128]{2,1,0:T(8,128)}, s32[]{:T(128)}, f32[16,128,128]{2,1,0:T(8,128)}, s32[2]{0:T(128)S(1)}, /*index=5*/s32[40,128]{1,0:...) while((s32[]{:T(128)}, f32[16,128,128]{2,1,0:T(8,128)}, ...), condition=%wide.region_1.2_spmd, body=%wide.region_0.1_spmd.sunk | while | flops 100925440 | bytes 33030584 | solution.py:545
  (25 shorter events, 0.3 us)
Async XLA Ops:
  0.0 8.6 %copy-start.6 = (f32[1,1,4,128,128]{4,3,2,1,0:T(8,128)S(1)}, f32[1,1,4,128,128]{4,3,2,1,0:T(8,128)}, u32[]{:S(2)}) copy-start(f32[1,1,4,128,128]{4,3,2,1,0:T(8,128)} %param.7) | copy-start | bytes 786436
  1.6 8.4 %collective-permute-start.9 = (s32[128]{0:T(128)S(1)}, s32[128]{0:T(128)S(1)}, u32[]{:S(2)}, u32[]{:S(2)}) collective-permute-start(s32[128]{0:T(128)S(1)} %get-tuple-element.215), channel_id=1, source_target_pairs={{64,0},{65,1},{66,2},{67,3},{68,4},{69,5},{70,6},{71,7},{72,8},{73... | collective-permute-start | bytes 1544 | tf_op jit(solution)/shard_map/ppermute | solution.py:484
  5.3 3.3 %collective-permute-start.8 = (s32[128]{0:T(128)S(1)}, s32[128]{0:T(128)S(1)}, u32[]{:S(2)}, u32[]{:S(2)}) collective-permute-start(s32[128]{0:T(128)S(1)} %get-tuple-element.215), channel_id=1, source_target_pairs={{32,0},{33,1},{34,2},{35,3},{36,4},{37,5},{38,6},{39,7},{40,8},{41... | collective-permute-start | bytes 1544 | tf_op jit(solution)/shard_map/ppermute | solution.py:484
  5.7 4.2 %collective-permute-start.10 = (s32[128]{0:T(128)S(1)}, s32[128]{0:T(128)S(1)}, u32[]{:S(2)}, u32[]{:S(2)}) collective-permute-start(s32[128]{0:T(128)S(1)} %get-tuple-element.215), channel_id=1, source_target_pairs={{96,0},{97,1},{98,2},{99,3},{100,4},{101,5},{102,6},{103,7},{104,8... | collective-permute-start | bytes 1544 | tf_op jit(solution)/shard_map/ppermute | solution.py:484
  6.1 30.5 %collective-permute-start.21 = (f32[16,128,128]{2,1,0:T(8,128)}, f32[16,128,128]{2,1,0:T(8,128)S(1)}, u32[]{:S(2)}, u32[]{:S(2)}) collective-permute-start(f32[16,128,128]{2,1,0:T(8,128)} %bitcast.20.rest_0_.rest_8_), channel_id=1, source_target_pairs={{0,96},{16,112},{32,0},{48,16},{64,32},{80,48},{96,64},{112,80},{1... | collective-permute-start | bytes 3145736 | tf_op jit(solution)/shard_map/ppermute | solution.py:415
  8.5 28.1 %collective-permute-start.20 = (f32[16,128,128]{2,1,0:T(8,128)}, f32[16,128,128]{2,1,0:T(8,128)S(1)}, u32[]{:S(2)}, u32[]{:S(2)}) collective-permute-start(f32[16,128,128]{2,1,0:T(8,128)} %bitcast.20.rest_0_.rest_8_), channel_id=1, source_target_pairs={{0,32},{16,48},{32,64},{48,80},{64,96},{80,112},{96,0},{112,16},{1... | collective-permute-start | bytes 3145736 | tf_op jit(solution)/shard_map/ppermute | solution.py:415
  8.6 10.3 %collective-permute-start.7 = (f32[4,128,128]{2,1,0:T(8,128)S(1)}, f32[4,128,128]{2,1,0:T(8,128)S(1)}, u32[]{:S(2)}, u32[]{:S(2)}) collective-permute-start(f32[4,128,128]{2,1,0:T(8,128)S(1)} %bitcast.34), channel_id=1, source_target_pairs={{0,8},{1,9},{2,10},{3,11},{4,12},{5,13},{6,14},{7,15},{8,0},{9,1},... | collective-permute-start | bytes 786440 | tf_op jit(solution)/shard_map/ppermute | solution.py:427
  10.0 5.0 %collective-permute-start.11 = (s32[4,128]{1,0:T(4,128)S(1)}, s32[4,128]{1,0:T(4,128)S(1)}, u32[]{:S(2)}, u32[]{:S(2)}) collective-permute-start(s32[4,128]{1,0:T(4,128)S(1)} %dynamic_update_slice.50), channel_id=1, source_target_pairs={{2,0},{3,1},{0,2},{1,3},{6,4},{7,5},{4,6},{5,7},{10,8},{11,9},{8,1... | collective-permute-start | bytes 6152 | tf_op jit(solution)/shard_map/ppermute | solution.py:484
  11.7 4.9 %collective-permute-start.12 = (s32[4,128]{1,0:T(4,128)S(1)}, s32[4,128]{1,0:T(4,128)S(1)}, u32[]{:S(2)}, u32[]{:S(2)}) collective-permute-start(s32[4,128]{1,0:T(4,128)S(1)} %dynamic_update_slice.50), channel_id=1, source_target_pairs={{4,0},{5,1},{6,2},{7,3},{0,4},{1,5},{2,6},{3,7},{12,8},{13,9},{14,... | collective-permute-start | bytes 6152 | tf_op jit(solution)/shard_map/ppermute | solution.py:484
  15.0 3.9 %collective-permute-start.13 = (s32[4,128]{1,0:T(4,128)S(1)}, s32[4,128]{1,0:T(4,128)S(1)}, u32[]{:S(2)}, u32[]{:S(2)}) collective-permute-start(s32[4,128]{1,0:T(4,128)S(1)} %dynamic_update_slice.50), channel_id=1, source_target_pairs={{6,0},{7,1},{4,2},{5,3},{2,4},{3,5},{0,6},{1,7},{14,8},{15,9},{12,... | collective-permute-start | bytes 6152 | tf_op jit(solution)/shard_map/ppermute | solution.py:484
  19.8 2.9 %collective-permute-start.14 = (s32[4,4,128]{2,1,0:T(4,128)S(1)}, s32[4,4,128]{2,1,0:T(4,128)S(1)}, u32[]{:S(2)}, u32[]{:S(2)}) collective-permute-start(s32[4,4,128]{2,1,0:T(4,128)S(1)} %get-tuple-element.177), channel_id=1, source_target_pairs={{8,0},{9,1},{10,2},{11,3},{12,4},{13,5},{14,6},{15,7},{0,8},{1,9},... | collective-permute-start | bytes 24584 | tf_op jit(solution)/shard_map/ppermute | solution.py:484
  20.5 13.8 %collective-permute-start.17 = (f32[8,128,128]{2,1,0:T(8,128)}, f32[8,128,128]{2,1,0:T(8,128)}, u32[]{:S(2)}, u32[]{:S(2)}) collective-permute-start(f32[8,128,128]{2,1,0:T(8,128)} %get-tuple-element.309.rest_0_), channel_id=1, source_target_pairs={{0,2},{1,3},{2,4},{3,5},{4,6},{5,7},{6,0},{7,1},{8,10},{9,11},{10,... | collective-permute-start | bytes 1572872 | tf_op jit(solution)/shard_map/ppermute | solution.py:427
  22.7 4.1 %collective-permute-start.15 = (s32[2,4,4,128]{3,2,1,0:T(4,128)S(1)}, s32[2,4,4,128]{3,2,1,0:T(4,128)S(1)}, u32[]{:S(2)}, u32[]{:S(2)}) collective-permute-start(s32[2,4,4,128]{3,2,1,0:T(4,128)S(1)} %bitcast_dynamic-update-slice_fusion.4), channel_id=1, source_target_pairs={{16,0},{17,1},{18,2},{19,3},{20,4},{21,5},{22,6},{23,7},{24,8},{25... | collective-permute-start | bytes 49160 | tf_op jit(solution)/shard_map/ppermute | solution.py:484
  26.8 7.4 %collective-permute-start.16 = (s32[2,2,4,4,128]{4,3,2,1,0:T(4,128)S(1)}, s32[2,2,4,4,128]{4,3,2,1,0:T(4,128)S(1)}, u32[]{:S(2)}, u32[]{:S(2)}) collective-permute-start(s32[2,2,4,4,128]{4,3,2,1,0:T(4,128)S(1)} %bitcast_dynamic-update-slice_fusion.2), channel_id=1, source_target_pairs={{1,0},{0,1},{3,2},{2,3},{5,4},{4,5},{7,6},{6,7},{9,8},{8,9},{11,10... | collective-permute-start | bytes 98312 | tf_op jit(solution)/shard_map/ppermute | solution.py:484
  32.4 13.9 %collective-permute-start.18 = (f32[8,128,128]{2,1,0:T(8,128)}, f32[8,128,128]{2,1,0:T(8,128)}, u32[]{:S(2)}, u32[]{:S(2)}) collective-permute-start(f32[8,128,128]{2,1,0:T(8,128)} %get-tuple-element.309.rest_0_), channel_id=1, source_target_pairs={{0,6},{1,7},{2,0},{3,1},{4,2},{5,3},{6,4},{7,5},{8,14},{9,15},{10,... | collective-permute-start | bytes 1572872 | tf_op jit(solution)/shard_map/ppermute | solution.py:427
  34.3 22.9 %collective-permute-start.19 = (f32[8,128,128]{2,1,0:T(8,128)}, f32[8,128,128]{2,1,0:T(8,128)}, u32[]{:S(2)}, u32[]{:S(2)}) collective-permute-start(f32[8,128,128]{2,1,0:T(8,128)} %collective-permute-done.17.rest_1_), channel_id=1, source_target_pairs={{0,2},{1,3},{2,4},{3,5},{4,6},{5,7},{6,0},{7,1},{8,10},{9,11},{10,... | collective-permute-start | bytes 1572872 | tf_op jit(solution)/shard_map/ppermute | solution.py:427
  38.6 18.6 %collective-permute-start.24 = (f32[6,128,128]{2,1,0:T(8,128)S(1)}, f32[6,128,128]{2,1,0:T(8,128)S(1)}, u32[]{:S(2)}, u32[]{:S(2)}) collective-permute-start(f32[6,128,128]{2,1,0:T(8,128)S(1)} %get-tuple-element.183), channel_id=1, source_target_pairs={{0,16},{16,0},{32,48},{48,32},{64,80},{80,64},{96,112},{112,96},{1... | collective-permute-start | bytes 1179656 | tf_op jit(solution)/shard_map/ppermute | solution.py:415
  40.9 6.2 %collective-permute-start.22 = (f32[3,128,128]{2,1,0:T(8,128)S(1)}, f32[3,128,128]{2,1,0:T(8,128)S(1)}, u32[]{:S(2)}, u32[]{:S(2)}) collective-permute-start(f32[3,128,128]{2,1,0:T(8,128)S(1)} %get-tuple-element.181), channel_id=1, source_target_pairs={{0,32},{16,48},{32,64},{48,80},{64,96},{80,112},{96,0},{112,16},{1... | collective-permute-start | bytes 589832 | tf_op jit(solution)/shard_map/ppermute | solution.py:415
  40.9 13.0 %collective-permute-start.23 = (f32[3,128,128]{2,1,0:T(8,128)S(1)}, f32[3,128,128]{2,1,0:T(8,128)S(1)}, u32[]{:S(2)}, u32[]{:S(2)}) collective-permute-start(f32[3,128,128]{2,1,0:T(8,128)S(1)} %get-tuple-element.182), channel_id=1, source_target_pairs={{0,48},{16,32},{32,80},{48,64},{64,112},{80,96},{96,16},{112,0},{1... | collective-permute-start | bytes 589832 | tf_op jit(solution)/shard_map/ppermute | solution.py:415
  46.3 14.1 %collective-permute-start.25 = (f32[8,128,128]{2,1,0:T(8,128)}, f32[8,128,128]{2,1,0:T(8,128)}, u32[]{:S(2)}, u32[]{:S(2)}) collective-permute-start(f32[8,128,128]{2,1,0:T(8,128)} %get-tuple-element.309.rest_0_), channel_id=1, source_target_pairs={{0,1},{1,0},{2,3},{3,2},{4,5},{5,4},{6,7},{7,6},{8,9},{9,8},{10,11... | collective-permute-start | bytes 1572872 | tf_op jit(solution)/shard_map/ppermute | solution.py:427
  47.1 10.1 %copy-start.2 = (f32[3,128,128]{2,1,0:T(8,128)}, f32[3,128,128]{2,1,0:T(8,128)S(1)}, u32[]{:S(2)}) copy-start(f32[3,128,128]{2,1,0:T(8,128)S(1)} %collective-permute-done.22.refs_1_.rest_12_) | copy-start | bytes 589828
  47.1 13.3 %collective-permute-start.26 = (f32[8,128,128]{2,1,0:T(8,128)}, f32[8,128,128]{2,1,0:T(8,128)}, u32[]{:S(2)}, u32[]{:S(2)}) collective-permute-start(f32[8,128,128]{2,1,0:T(8,128)} %collective-permute-done.17.rest_1_), channel_id=1, source_target_pairs={{0,1},{1,0},{2,3},{3,2},{4,5},{5,4},{6,7},{7,6},{8,9},{9,8},{10,11... | collective-permute-start | bytes 1572872 | tf_op jit(solution)/shard_map/ppermute | solution.py:427
  53.9 3.3 %copy-start.4 = (f32[3,128,128]{2,1,0:T(8,128)}, f32[3,128,128]{2,1,0:T(8,128)S(1)}, u32[]{:S(2)}) copy-start(f32[3,128,128]{2,1,0:T(8,128)S(1)} %collective-permute-done.23.refs_2_.rest_13_) | copy-start | bytes 589828
  53.9 6.4 %collective-permute-start.27 = (f32[8,128,128]{2,1,0:T(8,128)}, f32[8,128,128]{2,1,0:T(8,128)}, u32[]{:S(2)}, u32[]{:S(2)}) collective-permute-start(f32[8,128,128]{2,1,0:T(8,128)} %collective-permute-done.18.rest_2_), channel_id=1, source_target_pairs={{0,1},{1,0},{2,3},{3,2},{4,5},{5,4},{6,7},{7,6},{8,9},{9,8},{10,11... | collective-permute-start | bytes 1572872 | tf_op jit(solution)/shard_map/ppermute | solution.py:427
  57.2 0.7 %copy-start = (f32[6,128,128]{2,1,0:T(8,128)}, f32[6,128,128]{2,1,0:T(8,128)S(1)}, u32[]{:S(2)}) copy-start(f32[6,128,128]{2,1,0:T(8,128)S(1)} %collective-permute-done.24.refs_3_.rest_11_) | copy-start | bytes 1179652
  58.0 2.5 %collective-permute-start.28 = (f32[8,128,128]{2,1,0:T(8,128)}, f32[8,128,128]{2,1,0:T(8,128)}, u32[]{:S(2)}, u32[]{:S(2)}) collective-permute-start(f32[8,128,128]{2,1,0:T(8,128)} %hold.1.rest_3_), channel_id=1, source_target_pairs={{0,1},{1,0},{2,3},{3,2},{4,5},{5,4},{6,7},{7,6},{8,9},{9,8},{10,11... | collective-permute-start | bytes 1572872 | tf_op jit(solution)/shard_map/ppermute | solution.py:427
  58.6 1.9 %copy-start.1 = (f32[6,128,128]{2,1,0:T(8,128)S(1)}, f32[6,128,128]{2,1,0:T(8,128)}, u32[]{:S(2)}) copy-start(f32[6,128,128]{2,1,0:T(8,128)} %copy-done) | copy-start | bytes 1179652
  58.6 1.9 %copy-start.3 = (f32[3,128,128]{2,1,0:T(8,128)S(1)}, f32[3,128,128]{2,1,0:T(8,128)}, u32[]{:S(2)}) copy-start(f32[3,128,128]{2,1,0:T(8,128)} %copy-done.2) | copy-start | bytes 589828
  58.6 1.9 %copy-start.5 = (f32[3,128,128]{2,1,0:T(8,128)S(1)}, f32[3,128,128]{2,1,0:T(8,128)}, u32[]{:S(2)}) copy-start(f32[3,128,128]{2,1,0:T(8,128)} %copy-done.4) | copy-start | bytes 589828
where the time goes:
time: 64.9 us
  starting transfers between devices  35.6 us (55%)
  waiting for transfers between devices  15.2 us (23%)
  Pallas kernels  10.2 us (16%)
  local copies, waits for them, and re-layouts  1.82 us (3%)
  other arithmetic  0.82 us (1%)
  loops' own time  0.8 us (1%)
    ppermute x9, starting transfers between devices, among(): got = lax.ppermute(held, ('row', *COL), pairs)  19.7 us
    ppermute x8, starting transfers between devices, moved(): return lax.ppermute(block, COL, [(i, there(i)) for i in range(columns)])  10.5 us
    ppermute x9, waiting for transfers between devices, among(): got = lax.ppermute(held, ('row', *COL), pairs)  6.25 us
    ppermute x5, starting transfers between devices, to_row(): return lax.ppermute(block, 'row', [(i, there(i)) for i in range(rows)])  5.44 us
    ppermute x8, waiting for transfers between devices, moved(): return lax.ppermute(block, COL, [(i, there(i)) for i in range(columns)])  4.73 us
    ppermute x5, waiting for transfers between devices, to_row(): return lax.ppermute(block, 'row', [(i, there(i)) for i in range(rows)])  4.27 us
    pallas_call x1, Pallas kernels, products(): pl.pallas_call(functools.partial(kernel, parts), in_specs=[smem if x.ndim...  3.4 us
    pallas_call x1, Pallas kernels, plan(): pl.pallas_call(functools.partial(plan_kernel, sends), in_specs=[smem, vme...  2.35 us
  transfers between devices with their start and end apart: 22, of which 6 were waited for; matrix products, arithmetic and copies ran while one was open for 1% of the time, Pallas kernels for 11%

commit v1 on v0

--- a/solution.py
+++ b/solution.py
@@ -114,7 +114,7 @@
     )
 
 
-def plan_kernel(sends, me_ref, spots_ref, pack_list, product_list, info_ref, maps_ref):
+def plan_kernel(sends, me_ref, spots_ref, pack_list, info_ref, maps_ref):
     row, column = me_ref[0], me_ref[1]
     make_maps(maps_ref)
     held = positions(spots_ref, maps_ref)
@@ -149,7 +149,6 @@
     info_ref[8:16] = b
     info_ref[16:32] = c
     info_ref[32:40] = order
-    extract(entries_of(info_ref, me_ref)[0], product_list)
 
 
 def plan(me, spots, sends):
@@ -158,10 +157,9 @@
     return pl.pallas_call(
         functools.partial(plan_kernel, sends),
         in_specs=[smem, vmem],
-        out_specs=[smem, smem, vmem, vmem],
+        out_specs=[smem, vmem, vmem],
         out_shape=[
             jax.ShapeDtypeStruct((sum(n for n, *_ in sends),), jnp.int32),
-            jax.ShapeDtypeStruct((LIST + 1,), jnp.int32),
             jax.ShapeDtypeStruct((40, 128), jnp.int32),
             jax.ShapeDtypeStruct((6, 128, 128), jnp.bfloat16),
         ],
@@ -201,7 +199,8 @@
     )(listing, *near)
 
 
-def overflow_kernel(spots_ref, maps_ref, over_ref):
+def overflow_kernel(me_ref, info_ref, spots_ref, maps_ref, over_ref, product_list):
+    extract(entries_of(info_ref, me_ref)[0], product_list)
     held = positions(spots_ref, maps_ref)
     a = held[:8].astype(jnp.int32)
     turned = [held[8:40]] + [pltpu.roll(held[8:40], 128 - q, 1) for q in range(1, 16)]
@@ -222,17 +221,21 @@
     over_ref[0] = jnp.max(jnp.where(most > slots.astype(jnp.float32), 1.0, 0.0)).astype(jnp.int32)
 
 
-def overflow(spots, maps):
+def overflow(me, info, spots, maps):
+    smem = pl.BlockSpec(memory_space=pltpu.SMEM)
     vmem = pl.BlockSpec(memory_space=pltpu.VMEM)
     return pl.pallas_call(
         overflow_kernel,
-        in_specs=[vmem] * 2,
-        out_specs=pl.BlockSpec(memory_space=pltpu.SMEM),
-        out_shape=jax.ShapeDtypeStruct((1,), jnp.int32),
+        in_specs=[smem, vmem, vmem, vmem],
+        out_specs=[smem, smem],
+        out_shape=[
+            jax.ShapeDtypeStruct((1,), jnp.int32),
+            jax.ShapeDtypeStruct((LIST + 1,), jnp.int32),
+        ],
         compiler_params=pltpu.CompilerParams(vmem_limit_bytes=16 << 20),
         cost_estimate=pl.CostEstimate(flops=10**9, bytes_accessed=10**5, transcendentals=0),
         name="overflow",
-    )(spots, maps)
+    )(me, info, spots, maps)
 
 
 def halves(x):
@@ -326,15 +329,30 @@
 
 def all_kernel(parts, list_ref, *rest):
     a_refs, b_refs = rest[:A_PARTS], rest[A_PARTS:parts]
-    out_ref, acc, c_sem, _, *buffers = rest[parts:]
+    out_ref, acc, c_sem, touched, *buffers = rest[parts:]
+    slots = acc.shape[0]
+
+    def stored(c):
+        return pltpu.make_async_copy(acc.at[c], out_ref.at[c], c_sem.at[c])
 
     def meanwhile():
+        for c in range(slots):
+            touched[c] = 0
+
+        def mark(n, carry):
+            touched[c_of(list_ref[n])] = 1
+            return carry
+
+        lax.fori_loop(0, list_ref[LIST], mark, 0)
         acc[...] = jnp.zeros_like(acc)
+        for c in range(slots):
+            pl.when(touched[c] == 0)(lambda c=c: stored(c).start())
 
     multiply_listed(list_ref, a_refs, b_refs, acc, *buffers, meanwhile)
-    copy = pltpu.make_async_copy(acc, out_ref, c_sem.at[0])
-    copy.start()
-    copy.wait()
+    for c in range(slots):
+        pl.when(touched[c] == 1)(lambda c=c: stored(c).start())
+    for c in range(slots):
+        stored(c).wait()
 
 
 def add_listed(list_ref, a_refs, b_refs, total_ref, out_ref, acc, c_sem, stage, *buffers):
@@ -515,25 +533,28 @@
     a_ahead = moved(pair, back_z, columns)
 
     sends = [
-        (FAR, 2, lambda i: (i + 2) & 7),
+        (FAR, 2, lambda i: (i - 2) & 7),
         (FAR, 3, lambda i: ((i + 2) & 7) ^ 1),
         (NEAR, 1, lambda i: i ^ 1),
     ]
-    pack_list, product_list, info, maps = plan(me, spots, sends)
+    pack_list, info, maps = plan(me, spots, sends)
     packed = pack(pack_list, near, [n for n, *_ in sends])
 
     far_own, far_other, cross = [
         to_row(block, rows, there) for block, (*_, there) in zip(packed, sends)
     ]
 
-    (a_far,) = held_for([moved(a_behind, on_z, columns)], [far_own, far_other, cross])
+    over, product_list = overflow(me, info, spots, maps)
+    (a_behind,) = held_for([a_behind], [info])
+    a_far = moved(a_behind, on_z, columns)
+    (a_far,) = held_for([a_far], [far_own, far_other, cross, over])
     a_mine = [pair, a_behind, a_ahead, a_far]
     a_parts = a_mine + [moved(block, lambda i: i ^ 1, columns) for block in a_mine]
 
     b_parts = near + [cross, far_own, far_other]
     total = products(all_kernel, [product_list], a_parts, b_parts, None, sc)
 
-    trips = overflow(spots, maps)[0]
+    trips = over[0]
 
     def trip(state):
         done, total = state

time: 64.9 us -> 69.3 us (1.068)
  starting transfers between devices: 35.6 us -> 31.8 us
  waiting for transfers between devices: 15.2 us -> 19 us
  local copies, waits for them, and re-layouts: 1.82 us -> 5.45 us
  Pallas kernels: 10.2 us -> 11 us
    ppermute x5, waiting for transfers between devices: 4.27 us -> 9.75 us  [to_row(): return lax.ppermute(block, 'row', [(i, there(i)) for i in range(rows)])]
    ppermute x8, starting transfers between devices: 10.5 us -> 5.14 us  [moved(): return lax.ppermute(block, COL, [(i, there(i)) for i in range(columns)])]
    unnamed x14 -> x16, local copies, waits for them, and re-layouts: 0.76 us -> 4.39 us
    ppermute x8, waiting for transfers between devices: 4.73 us -> 3.03 us  [moved(): return lax.ppermute(block, COL, [(i, there(i)) for i in range(columns)])]
    ppermute x5, starting transfers between devices: 5.44 us -> 6.97 us  [to_row(): return lax.ppermute(block, 'row', [(i, there(i)) for i in range(rows)])]
    pallas_call x1, Pallas kernels: 1.73 us -> 2.93 us  [overflow(): pl.pallas_call(overflow_kernel, in_specs=[smem, vmem, vmem, vmem], out_sp...]
  transfers between devices with their start and end apart: 22 -> 22, of which waited for: 6 -> 6; matrix products, arithmetic and copies ran while one was open for 1% -> 0% of each run, Pallas kernels for 11% -> 11%
where the time goes in v1:
time: 69.3 us; the launch traced here: 69.2 us
  starting transfers between devices  31.8 us (46%)
  waiting for transfers between devices  19 us (27%)
  Pallas kernels  11 us (16%)
  local copies, waits for them, and re-layouts  5.45 us (8%)
  other arithmetic  0.82 us (1%)
  loops' own time  0.79 us (1%)
    ppermute x9, starting transfers between devices, among(): got = lax.ppermute(held, ('row', *COL), pairs)  19.7 us
    ppermute x5, waiting for transfers between devices, to_row(): return lax.ppermute(block, 'row', [(i, there(i)) for i in range(rows)])  9.75 us
    ppermute x5, starting transfers between devices, to_row(): return lax.ppermute(block, 'row', [(i, there(i)) for i in range(rows)])  6.97 us
    ppermute x9, waiting for transfers between devices, among(): got = lax.ppermute(held, ('row', *COL), pairs)  6.25 us
    ppermute x8, starting transfers between devices, moved(): return lax.ppermute(block, COL, [(i, there(i)) for i in range(columns)])  5.14 us
    unnamed x16, local copies, waits for them, and re-layouts  4.39 us
    pallas_call x1, Pallas kernels, products(): pl.pallas_call(functools.partial(kernel, parts), in_specs=[smem if x.ndim...  3.14 us
    ppermute x8, waiting for transfers between devices, moved(): return lax.ppermute(block, COL, [(i, there(i)) for i in range(columns)])  3.03 us
  transfers between devices with their start and end apart: 22, of which 6 were waited for; matrix products, arithmetic and copies ran while one was open for 0% of the time, Pallas kernels for 11%

profile of v1, /device:TPU:1, one launch (start us, length us, event | category | flops | bytes accessed | tf_op | source)
XLA Modules:
  0.0 69.2 jit_solution(9137719096201129870)
XLA Ops:
  0.0 0.0 copy-start.6
  0.0 0.8 %reshape_squeeze.6 = s32[16]{0:T(128)S(1)} reshape(s32[1,1,2,8]{3,2,1,0:T(2,128)} %param.10) | data formatting | bytes 128 | tf_op jit(solution)/shard_map/reshape;squeeze | solution.py:524
  0.8 0.7 %pad_add_fusion.1 = s32[40]{0:T(128)S(1)} fusion(s32[16]{0:T(128)} %bitcast.38, s32[16]{0:T(128)S(1)} %reshape_squeeze.6, s32[4]{0:T(128)S(1)} %broadcast.5, s32[4]{0:T(128)} %bitcast.39), kind=kLoop, calls=%fused_computation.12 | loop fusion | flops 120 | bytes 320 | tf_op jit(solution)/shard_map/concatenate | solution.py:524
  1.6 3.8 %collective-permute-start.9 = (s32[128]{0:T(128)S(1)}, s32[128]{0:T(128)S(1)}, u32[]{:S(2)}, u32[]{:S(2)}) collective-permute-start(s32[128]{0:T(128)S(1)} %get-tuple-element.217), channel_id=1, source_target_pairs={{64,0},{65,1},{66,2},{67,3},{68,4},{69,5},{70,6},{71,7},{72,8},{73... | collective-permute-start | bytes 1544 | tf_op jit(solution)/shard_map/ppermute | solution.py:502
  5.3 0.4 collective-permute-start.8
  5.7 0.4 collective-permute-start.10
  6.1 2.3 %collective-permute-start.21 = (f32[16,128,128]{2,1,0:T(8,128)}, f32[16,128,128]{2,1,0:T(8,128)S(1)}, u32[]{:S(2)}, u32[]{:S(2)}) collective-permute-start(f32[16,128,128]{2,1,0:T(8,128)} %bitcast.20.rest_0_.rest_8_), channel_id=1, source_target_pairs={{0,96},{16,112},{32,0},{48,16},{64,32},{80,48},{96,64},{112,80},{1... | collective-permute-start | bytes 3145736 | tf_op jit(solution)/shard_map/ppermute | solution.py:433
  8.4 0.1 pad_add_fusion.me_ref
  8.5 0.1 collective-permute-start.20
  8.6 0.0 collective-permute-done.8
  8.6 0.0 copy-done.6
  8.6 1.3 %collective-permute-start.7 = (f32[4,128,128]{2,1,0:T(8,128)S(1)}, f32[4,128,128]{2,1,0:T(8,128)S(1)}, u32[]{:S(2)}, u32[]{:S(2)}) collective-permute-start(f32[4,128,128]{2,1,0:T(8,128)S(1)} %bitcast.34), channel_id=1, source_target_pairs={{0,8},{1,9},{2,10},{3,11},{4,12},{5,13},{6,14},{7,15},{8,0},{9,1},... | collective-permute-start | bytes 786440 | tf_op jit(solution)/shard_map/ppermute | solution.py:445
  9.9 0.0 collective-permute-done.9
  10.0 0.0 collective-permute-done.10
  10.0 1.7 %collective-permute-start.11 = (s32[4,128]{1,0:T(4,128)S(1)}, s32[4,128]{1,0:T(4,128)S(1)}, u32[]{:S(2)}, u32[]{:S(2)}) collective-permute-start(s32[4,128]{1,0:T(4,128)S(1)} %dynamic_update_slice.50), channel_id=1, source_target_pairs={{2,0},{3,1},{0,2},{1,3},{6,4},{7,5},{4,6},{5,7},{10,8},{11,9},{8,1... | collective-permute-start | bytes 6152 | tf_op jit(solution)/shard_map/ppermute | solution.py:502
  11.7 3.3 %collective-permute-start.12 = (s32[4,128]{1,0:T(4,128)S(1)}, s32[4,128]{1,0:T(4,128)S(1)}, u32[]{:S(2)}, u32[]{:S(2)}) collective-permute-start(s32[4,128]{1,0:T(4,128)S(1)} %dynamic_update_slice.50), channel_id=1, source_target_pairs={{4,0},{5,1},{6,2},{7,3},{0,4},{1,5},{2,6},{3,7},{12,8},{13,9},{14,... | collective-permute-start | bytes 6152 | tf_op jit(solution)/shard_map/ppermute | solution.py:502
  15.0 0.0 collective-permute-done.11
  15.0 1.5 %collective-permute-start.13 = (s32[4,128]{1,0:T(4,128)S(1)}, s32[4,128]{1,0:T(4,128)S(1)}, u32[]{:S(2)}, u32[]{:S(2)}) collective-permute-start(s32[4,128]{1,0:T(4,128)S(1)} %dynamic_update_slice.50), channel_id=1, source_target_pairs={{6,0},{7,1},{4,2},{5,3},{2,4},{3,5},{0,6},{1,7},{14,8},{15,9},{12,... | collective-permute-start | bytes 6152 | tf_op jit(solution)/shard_map/ppermute | solution.py:502
  16.6 0.0 collective-permute-done.12
  16.6 2.4 %collective-permute-done.13 = s32[4,128]{1,0:T(4,128)S(1)} collective-permute-done((s32[4,128]{1,0:T(4,128)S(1)}, s32[4,128]{1,0:T(4,128)S(1)}, u32[]{:S(2)}, u32[]{:S(2)}) %collective-permute-start.13) | collective-permute-done | bytes 2080 | tf_op jit(solution)/shard_map/ppermute | solution.py:502
  19.0 0.0 collective-permute-done.7.beside_ref
  19.0 0.9 %pair.1 = (f32[8,128,128]{2,1,0:T(8,128)}, s32[4,4,128]{2,1,0:T(4,128)S(1)}) custom-call(f32[4,128,128]{2,1,0:T(8,128)S(1)} %bitcast.35, f32[4,128,128]{2,1,0:T(8,128)S(1)} %collective-permute-done.7.beside_ref, s32[4,4,128]{2,1,0:T(4,128)S(1)} %constant_dynamic-update-slice_fusion._), custom_call_target="tpu_custom_call", output_to_operand_aliasing={{1}: (2, {})} | custom-call | tf_op jit(solution)/shard_map/pair/pallas_call | solution.py:463
  19.9 0.7 collective-permute-start.14
  20.5 0.0 collective-permute-start.17
  20.5 2.2 %collective-permute-done.14 = s32[4,4,128]{2,1,0:T(4,128)S(1)} collective-permute-done((s32[4,4,128]{2,1,0:T(4,128)S(1)}, s32[4,4,128]{2,1,0:T(4,128)S(1)}, u32[]{:S(2)}, u32[]{:S(2)}) %collective-permute-start.14) | collective-permute-done | bytes 8224 | tf_op jit(solution)/shard_map/ppermute | solution.py:502
  22.7 2.5 %collective-permute-start.15 = (s32[2,4,4,128]{3,2,1,0:T(4,128)S(1)}, s32[2,4,4,128]{3,2,1,0:T(4,128)S(1)}, u32[]{:S(2)}, u32[]{:S(2)}) collective-permute-start(s32[2,4,4,128]{3,2,1,0:T(4,128)S(1)} %bitcast_dynamic-update-slice_fusion.4), channel_id=1, source_target_pairs={{16,0},{17,1},{18,2},{19,3},{20,4},{21,5},{22,6},{23,7},{24,8},{25... | collective-permute-start | bytes 49160 | tf_op jit(solution)/shard_map/ppermute | solution.py:502
  25.2 1.6 %collective-permute-done.15 = s32[2,4,4,128]{3,2,1,0:T(4,128)S(1)} collective-permute-done((s32[2,4,4,128]{3,2,1,0:T(4,128)S(1)}, s32[2,4,4,128]{3,2,1,0:T(4,128)S(1)}, u32[]{:S(2)}, u32[]{:S(2)}) %collective-permute-start.15) | collective-permute-done | bytes 16416 | tf_op jit(solution)/shard_map/ppermute | solution.py:502
  26.8 5.5 %collective-permute-start.16 = (s32[2,2,4,4,128]{4,3,2,1,0:T(4,128)S(1)}, s32[2,2,4,4,128]{4,3,2,1,0:T(4,128)S(1)}, u32[]{:S(2)}, u32[]{:S(2)}) collective-permute-start(s32[2,2,4,4,128]{4,3,2,1,0:T(4,128)S(1)} %bitcast_dynamic-update-slice_fusion.2), channel_id=1, source_target_pairs={{1,0},{0,1},{3,2},{2,3},{5,4},{4,5},{7,6},{6,7},{9,8},{8,9},{11,10... | collective-permute-start | bytes 98312 | tf_op jit(solution)/shard_map/ppermute | solution.py:502
  32.4 1.9 %collective-permute-start.18 = (f32[8,128,128]{2,1,0:T(8,128)}, f32[8,128,128]{2,1,0:T(8,128)}, u32[]{:S(2)}, u32[]{:S(2)}) collective-permute-start(f32[8,128,128]{2,1,0:T(8,128)} %get-tuple-element.311.rest_0_), channel_id=1, source_target_pairs={{0,6},{1,7},{2,0},{3,1},{4,2},{5,3},{6,4},{7,5},{8,14},{9,15},{10,... | collective-permute-start | bytes 1572872 | tf_op jit(solution)/shard_map/ppermute | solution.py:445
  34.3 0.0 collective-permute-done.16
  34.3 1.8 %plan.1 = (s32[12]{0:T(128)S(1)}, s32[40,128]{1,0:T(8,128)S(1)}, bf16[6,128,128]{2,1,0:T(8,128)(2,1)S(1)}) custom-call(s32[2]{0:T(128)S(1)} %pad_add_fusion.me_ref, s32[128,128]{1,0:T(8,128)S(1)} %bitcast.36), custom_call_target="tpu_custom_call" | custom-call | tf_op jit(solution)/shard_map/plan/pallas_call | solution.py:157
  36.1 0.0 collective-permute-done.17.refs_0_
  36.1 0.1 collective-permute-start.19
  36.2 0.0 collective-permute-done.21.rest_2_.rest_10_
  36.2 0.0 collective-permute-done.20.rest_1_.rest_9_
  36.2 1.6 %pack.1 = (f32[3,128,128]{2,1,0:T(8,128)S(1)}, f32[3,128,128]{2,1,0:T(8,128)S(1)}, f32[6,128,128]{2,1,0:T(8,128)S(1)}) custom-call(s32[12]{0:T(128)S(1)} %get-tuple-element.183.list_ref, f32[16,128,128]{2,1,0:T(8,128)} %bitcast.20.rest_0_.rest_8_, f32[16,128,128]{2,1,0:T(8,128)S(1)} %collective-permute-done.20.rest_1_.rest_9_, ...), custom_call_target="tpu_custom_call" | custom-call | tf_op jit(solution)/shard_map/pack/pallas_call | solution.py:190
  37.9 1.8 %collective-permute-start.24 = (f32[6,128,128]{2,1,0:T(8,128)S(1)}, f32[6,128,128]{2,1,0:T(8,128)S(1)}, u32[]{:S(2)}, u32[]{:S(2)}) collective-permute-start(f32[6,128,128]{2,1,0:T(8,128)S(1)} %get-tuple-element.186), channel_id=1, source_target_pairs={{0,16},{16,0},{32,48},{48,32},{64,80},{80,64},{96,112},{112,96},{1... | collective-permute-start | bytes 1179656 | tf_op jit(solution)/shard_map/ppermute | solution.py:433
  39.6 2.8 %collective-permute-start.22 = (f32[3,128,128]{2,1,0:T(8,128)S(1)}, f32[3,128,128]{2,1,0:T(8,128)S(1)}, u32[]{:S(2)}, u32[]{:S(2)}) collective-permute-start(f32[3,128,128]{2,1,0:T(8,128)S(1)} %get-tuple-element.184), channel_id=1, source_target_pairs={{0,96},{16,112},{32,0},{48,16},{64,32},{80,48},{96,64},{112,80},{1... | collective-permute-start | bytes 589832 | tf_op jit(solution)/shard_map/ppermute | solution.py:433
  42.5 0.0 collective-permute-start.23
  42.5 2.9 %overflow.1 = (s32[1]{0:T(128)}, s32[513]{0:T(1024)S(1)}) custom-call(s32[2]{0:T(128)S(1)} %pad_add_fusion.me_ref, s32[40,128]{1,0:T(8,128)S(1)} %get-tuple-element.310.info_ref.refs_1_, s32[128,128]{1,0:T(8,128)S(1)} %bitcast.37, bf16[6,128,128]{2,1,0:T(8,128)(2,1)S(1)} %get-tuple-element.180.maps_ref), custom_call_target="tpu_custom_call" | custom-call | flops 1000000000 | bytes 100000 | tf_op jit(solution)/shard_map/overflow/pallas_call | solution.py:227
  45.4 0.9 %collective-permute-done.18.rest_2_ = f32[8,128,128]{2,1,0:T(8,128)} collective-permute-done((f32[8,128,128]{2,1,0:T(8,128)}, f32[8,128,128]{2,1,0:T(8,128)}, u32[]{:S(2)}, u32[]{:S(2)}) %collective-permute-start.18) | collective-permute-done | bytes 524320 | tf_op jit(solution)/shard_map/ppermute | solution.py:445
  46.3 0.8 %collective-permute-start.25 = (f32[8,128,128]{2,1,0:T(8,128)}, f32[8,128,128]{2,1,0:T(8,128)}, u32[]{:S(2)}, u32[]{:S(2)}) collective-permute-start(f32[8,128,128]{2,1,0:T(8,128)} %get-tuple-element.311.rest_0_), channel_id=1, source_target_pairs={{0,1},{1,0},{2,3},{3,2},{4,5},{5,4},{6,7},{7,6},{8,9},{9,8},{10,11... | collective-permute-start | bytes 1572872 | tf_op jit(solution)/shard_map/ppermute | solution.py:445
  47.1 0.0 collective-permute-done.22.refs_1_.rest_12_
  47.1 0.0 copy-start.2
  47.1 0.5 collective-permute-start.26
  47.6 9.7 %collective-permute-done.23.refs_2_.rest_13_ = f32[3,128,128]{2,1,0:T(8,128)S(1)} collective-permute-done((f32[3,128,128]{2,1,0:T(8,128)S(1)}, f32[3,128,128]{2,1,0:T(8,128)S(1)}, u32[]{:S(2)}, u32[]{:S(2)}) %collective-permute-start.23) | collective-permute-done | bytes 196640 | tf_op jit(solution)/shard_map/ppermute | solution.py:433
  57.3 0.4 collective-permute-start.27
  57.7 0.0 collective-permute-done.19.refs_0_
  57.7 0.0 collective-permute-done.24.refs_3_.rest_11_
  57.8 0.8 %copy-done.7 = f32[8,128,128]{2,1,0:T(8,128)} copy-done((f32[8,128,128]{2,1,0:T(8,128)}, f32[8,128,128]{2,1,0:T(8,128)S(1)}, u32[]{:S(2)}) %copy-start.7) | copy-done | bytes 524312
  58.5 0.0 copy-done.2
  58.6 0.0 copy-done.4
  58.6 0.7 %copy-done = f32[6,128,128]{2,1,0:T(8,128)} copy-done((f32[6,128,128]{2,1,0:T(8,128)}, f32[6,128,128]{2,1,0:T(8,128)S(1)}, u32[]{:S(2)}) %copy-start) | copy-done | bytes 393240
  59.3 0.6 hold.3.rest_3_
  59.9 0.2 collective-permute-start.28
  60.1 0.0 collective-permute-done.25.rest_4_
  60.1 0.0 collective-permute-done.27.rest_6_
  60.1 0.0 collective-permute-done.26.rest_5_
  60.1 2.1 %collective-permute-done.28.rest_7_ = f32[8,128,128]{2,1,0:T(8,128)} collective-permute-done((f32[8,128,128]{2,1,0:T(8,128)}, f32[8,128,128]{2,1,0:T(8,128)}, u32[]{:S(2)}, u32[]{:S(2)}) %collective-permute-start.28) | collective-permute-done | bytes 524320 | tf_op jit(solution)/shard_map/ppermute | solution.py:445
  62.2 1.0 %copy-done.1 = f32[6,128,128]{2,1,0:T(8,128)S(1)} copy-done((f32[6,128,128]{2,1,0:T(8,128)S(1)}, f32[6,128,128]{2,1,0:T(8,128)}, u32[]{:S(2)}) %copy-start.1) | copy-done | bytes 393240
  63.2 0.9 %copy-done.3 = f32[3,128,128]{2,1,0:T(8,128)S(1)} copy-done((f32[3,128,128]{2,1,0:T(8,128)S(1)}, f32[3,128,128]{2,1,0:T(8,128)}, u32[]{:S(2)}) %copy-start.3) | copy-done | bytes 196632
  64.2 0.9 %copy-done.5 = f32[3,128,128]{2,1,0:T(8,128)S(1)} copy-done((f32[3,128,128]{2,1,0:T(8,128)S(1)}, f32[3,128,128]{2,1,0:T(8,128)}, u32[]{:S(2)}) %copy-start.5) | copy-done | bytes 196632
  65.1 3.1 %products.5 = f32[16,128,128]{2,1,0:T(8,128)} custom-call(s32[513]{0:T(1024)S(1)} %get-tuple-element.181.list_ref, f32[8,128,128]{2,1,0:T(8,128)} %get-tuple-element.311.rest_0_, f32[8,128,128]{2,1,0:T(8,128)} %hold.2.rest_1_, f32[8,128,128]{2,1,0:T(8,128)} %collective-permute-done.18.rest_2_, f32[8,128,128]{2,1,0:T(8,128)} %hold.3.rest_3_, ...), custom_call_target="tpu_custom_call" | custom-call | flops 100663296 | bytes 1572864 | tf_op jit(solution)/shard_map/products/pallas_call | solution.py:406
  68.2 0.8 %while.12 = (s32[]{:T(128)}, f32[16,128,128]{2,1,0:T(8,128)}, s32[]{:T(128)}, f32[16,128,128]{2,1,0:T(8,128)}, s32[2]{0:T(128)S(1)}, /*index=5*/s32[40,128]{1,0:...) while((s32[]{:T(128)}, f32[16,128,128]{2,1,0:T(8,128)}, ...), condition=%wide.region_1.2_spmd, body=%wide.region_0.1_spmd.sunk | while | flops 100925440 | bytes 33030584 | solution.py:566
  (28 shorter events, 0.3 us)
Async XLA Ops:
  0.0 8.6 %copy-start.6 = (f32[1,1,4,128,128]{4,3,2,1,0:T(8,128)S(1)}, f32[1,1,4,128,128]{4,3,2,1,0:T(8,128)}, u32[]{:S(2)}) copy-start(f32[1,1,4,128,128]{4,3,2,1,0:T(8,128)} %param.7) | copy-start | bytes 786436
  1.6 8.4 %collective-permute-start.9 = (s32[128]{0:T(128)S(1)}, s32[128]{0:T(128)S(1)}, u32[]{:S(2)}, u32[]{:S(2)}) collective-permute-start(s32[128]{0:T(128)S(1)} %get-tuple-element.217), channel_id=1, source_target_pairs={{64,0},{65,1},{66,2},{67,3},{68,4},{69,5},{70,6},{71,7},{72,8},{73... | collective-permute-start | bytes 1544 | tf_op jit(solution)/shard_map/ppermute | solution.py:502
  5.3 3.3 %collective-permute-start.8 = (s32[128]{0:T(128)S(1)}, s32[128]{0:T(128)S(1)}, u32[]{:S(2)}, u32[]{:S(2)}) collective-permute-start(s32[128]{0:T(128)S(1)} %get-tuple-element.217), channel_id=1, source_target_pairs={{32,0},{33,1},{34,2},{35,3},{36,4},{37,5},{38,6},{39,7},{40,8},{41... | collective-permute-start | bytes 1544 | tf_op jit(solution)/shard_map/ppermute | solution.py:502
  5.7 4.2 %collective-permute-start.10 = (s32[128]{0:T(128)S(1)}, s32[128]{0:T(128)S(1)}, u32[]{:S(2)}, u32[]{:S(2)}) collective-permute-start(s32[128]{0:T(128)S(1)} %get-tuple-element.217), channel_id=1, source_target_pairs={{96,0},{97,1},{98,2},{99,3},{100,4},{101,5},{102,6},{103,7},{104,8... | collective-permute-start | bytes 1544 | tf_op jit(solution)/shard_map/ppermute | solution.py:502
  6.1 30.1 %collective-permute-start.21 = (f32[16,128,128]{2,1,0:T(8,128)}, f32[16,128,128]{2,1,0:T(8,128)S(1)}, u32[]{:S(2)}, u32[]{:S(2)}) collective-permute-start(f32[16,128,128]{2,1,0:T(8,128)} %bitcast.20.rest_0_.rest_8_), channel_id=1, source_target_pairs={{0,96},{16,112},{32,0},{48,16},{64,32},{80,48},{96,64},{112,80},{1... | collective-permute-start | bytes 3145736 | tf_op jit(solution)/shard_map/ppermute | solution.py:433
  8.5 27.7 %collective-permute-start.20 = (f32[16,128,128]{2,1,0:T(8,128)}, f32[16,128,128]{2,1,0:T(8,128)S(1)}, u32[]{:S(2)}, u32[]{:S(2)}) collective-permute-start(f32[16,128,128]{2,1,0:T(8,128)} %bitcast.20.rest_0_.rest_8_), channel_id=1, source_target_pairs={{0,32},{16,48},{32,64},{48,80},{64,96},{80,112},{96,0},{112,16},{1... | collective-permute-start | bytes 3145736 | tf_op jit(solution)/shard_map/ppermute | solution.py:433
  8.6 10.3 %collective-permute-start.7 = (f32[4,128,128]{2,1,0:T(8,128)S(1)}, f32[4,128,128]{2,1,0:T(8,128)S(1)}, u32[]{:S(2)}, u32[]{:S(2)}) collective-permute-start(f32[4,128,128]{2,1,0:T(8,128)S(1)} %bitcast.34), channel_id=1, source_target_pairs={{0,8},{1,9},{2,10},{3,11},{4,12},{5,13},{6,14},{7,15},{8,0},{9,1},... | collective-permute-start | bytes 786440 | tf_op jit(solution)/shard_map/ppermute | solution.py:445
  10.0 5.0 %collective-permute-start.11 = (s32[4,128]{1,0:T(4,128)S(1)}, s32[4,128]{1,0:T(4,128)S(1)}, u32[]{:S(2)}, u32[]{:S(2)}) collective-permute-start(s32[4,128]{1,0:T(4,128)S(1)} %dynamic_update_slice.50), channel_id=1, source_target_pairs={{2,0},{3,1},{0,2},{1,3},{6,4},{7,5},{4,6},{5,7},{10,8},{11,9},{8,1... | collective-permute-start | bytes 6152 | tf_op jit(solution)/shard_map/ppermute | solution.py:502
  11.7 4.9 %collective-permute-start.12 = (s32[4,128]{1,0:T(4,128)S(1)}, s32[4,128]{1,0:T(4,128)S(1)}, u32[]{:S(2)}, u32[]{:S(2)}) collective-permute-start(s32[4,128]{1,0:T(4,128)S(1)} %dynamic_update_slice.50), channel_id=1, source_target_pairs={{4,0},{5,1},{6,2},{7,3},{0,4},{1,5},{2,6},{3,7},{12,8},{13,9},{14,... | collective-permute-start | bytes 6152 | tf_op jit(solution)/shard_map/ppermute | solution.py:502
  15.0 3.9 %collective-permute-start.13 = (s32[4,128]{1,0:T(4,128)S(1)}, s32[4,128]{1,0:T(4,128)S(1)}, u32[]{:S(2)}, u32[]{:S(2)}) collective-permute-start(s32[4,128]{1,0:T(4,128)S(1)} %dynamic_update_slice.50), channel_id=1, source_target_pairs={{6,0},{7,1},{4,2},{5,3},{2,4},{3,5},{0,6},{1,7},{14,8},{15,9},{12,... | collective-permute-start | bytes 6152 | tf_op jit(solution)/shard_map/ppermute | solution.py:502
  19.9 2.9 %collective-permute-start.14 = (s32[4,4,128]{2,1,0:T(4,128)S(1)}, s32[4,4,128]{2,1,0:T(4,128)S(1)}, u32[]{:S(2)}, u32[]{:S(2)}) collective-permute-start(s32[4,4,128]{2,1,0:T(4,128)S(1)} %get-tuple-element.178), channel_id=1, source_target_pairs={{8,0},{9,1},{10,2},{11,3},{12,4},{13,5},{14,6},{15,7},{0,8},{1,9},... | collective-permute-start | bytes 24584 | tf_op jit(solution)/shard_map/ppermute | solution.py:502
  20.5 15.6 %collective-permute-start.17 = (f32[8,128,128]{2,1,0:T(8,128)}, f32[8,128,128]{2,1,0:T(8,128)}, u32[]{:S(2)}, u32[]{:S(2)}) collective-permute-start(f32[8,128,128]{2,1,0:T(8,128)} %get-tuple-element.311.rest_0_), channel_id=1, source_target_pairs={{0,2},{1,3},{2,4},{3,5},{4,6},{5,7},{6,0},{7,1},{8,10},{9,11},{10,... | collective-permute-start | bytes 1572872 | tf_op jit(solution)/shard_map/ppermute | solution.py:445
  22.7 4.1 %collective-permute-start.15 = (s32[2,4,4,128]{3,2,1,0:T(4,128)S(1)}, s32[2,4,4,128]{3,2,1,0:T(4,128)S(1)}, u32[]{:S(2)}, u32[]{:S(2)}) collective-permute-start(s32[2,4,4,128]{3,2,1,0:T(4,128)S(1)} %bitcast_dynamic-update-slice_fusion.4), channel_id=1, source_target_pairs={{16,0},{17,1},{18,2},{19,3},{20,4},{21,5},{22,6},{23,7},{24,8},{25... | collective-permute-start | bytes 49160 | tf_op jit(solution)/shard_map/ppermute | solution.py:502
  26.8 7.4 %collective-permute-start.16 = (s32[2,2,4,4,128]{4,3,2,1,0:T(4,128)S(1)}, s32[2,2,4,4,128]{4,3,2,1,0:T(4,128)S(1)}, u32[]{:S(2)}, u32[]{:S(2)}) collective-permute-start(s32[2,2,4,4,128]{4,3,2,1,0:T(4,128)S(1)} %bitcast_dynamic-update-slice_fusion.2), channel_id=1, source_target_pairs={{1,0},{0,1},{3,2},{2,3},{5,4},{4,5},{7,6},{6,7},{9,8},{8,9},{11,10... | collective-permute-start | bytes 98312 | tf_op jit(solution)/shard_map/ppermute | solution.py:502
  32.4 13.9 %collective-permute-start.18 = (f32[8,128,128]{2,1,0:T(8,128)}, f32[8,128,128]{2,1,0:T(8,128)}, u32[]{:S(2)}, u32[]{:S(2)}) collective-permute-start(f32[8,128,128]{2,1,0:T(8,128)} %get-tuple-element.311.rest_0_), channel_id=1, source_target_pairs={{0,6},{1,7},{2,0},{3,1},{4,2},{5,3},{6,4},{7,5},{8,14},{9,15},{10,... | collective-permute-start | bytes 1572872 | tf_op jit(solution)/shard_map/ppermute | solution.py:445
  36.1 21.6 %collective-permute-start.19 = (f32[8,128,128]{2,1,0:T(8,128)}, f32[8,128,128]{2,1,0:T(8,128)S(1)}, u32[]{:S(2)}, u32[]{:S(2)}) collective-permute-start(f32[8,128,128]{2,1,0:T(8,128)} %hold.2.rest_1_), channel_id=1, source_target_pairs={{0,2},{1,3},{2,4},{3,5},{4,6},{5,7},{6,0},{7,1},{8,10},{9,11},{10,... | collective-permute-start | bytes 1572872 | tf_op jit(solution)/shard_map/ppermute | solution.py:445
  37.9 19.9 %collective-permute-start.24 = (f32[6,128,128]{2,1,0:T(8,128)S(1)}, f32[6,128,128]{2,1,0:T(8,128)S(1)}, u32[]{:S(2)}, u32[]{:S(2)}) collective-permute-start(f32[6,128,128]{2,1,0:T(8,128)S(1)} %get-tuple-element.186), channel_id=1, source_target_pairs={{0,16},{16,0},{32,48},{48,32},{64,80},{80,64},{96,112},{112,96},{1... | collective-permute-start | bytes 1179656 | tf_op jit(solution)/shard_map/ppermute | solution.py:433
  39.6 7.4 %collective-permute-start.22 = (f32[3,128,128]{2,1,0:T(8,128)S(1)}, f32[3,128,128]{2,1,0:T(8,128)S(1)}, u32[]{:S(2)}, u32[]{:S(2)}) collective-permute-start(f32[3,128,128]{2,1,0:T(8,128)S(1)} %get-tuple-element.184), channel_id=1, source_target_pairs={{0,96},{16,112},{32,0},{48,16},{64,32},{80,48},{96,64},{112,80},{1... | collective-permute-start | bytes 589832 | tf_op jit(solution)/shard_map/ppermute | solution.py:433
  42.5 14.9 %collective-permute-start.23 = (f32[3,128,128]{2,1,0:T(8,128)S(1)}, f32[3,128,128]{2,1,0:T(8,128)S(1)}, u32[]{:S(2)}, u32[]{:S(2)}) collective-permute-start(f32[3,128,128]{2,1,0:T(8,128)S(1)} %get-tuple-element.185), channel_id=1, source_target_pairs={{0,48},{16,32},{32,80},{48,64},{64,112},{80,96},{96,16},{112,0},{1... | collective-permute-start | bytes 589832 | tf_op jit(solution)/shard_map/ppermute | solution.py:433
  46.3 13.8 %collective-permute-start.25 = (f32[8,128,128]{2,1,0:T(8,128)}, f32[8,128,128]{2,1,0:T(8,128)}, u32[]{:S(2)}, u32[]{:S(2)}) collective-permute-start(f32[8,128,128]{2,1,0:T(8,128)} %get-tuple-element.311.rest_0_), channel_id=1, source_target_pairs={{0,1},{1,0},{2,3},{3,2},{4,5},{5,4},{6,7},{7,6},{8,9},{9,8},{10,11... | collective-permute-start | bytes 1572872 | tf_op jit(solution)/shard_map/ppermute | solution.py:445
  47.1 11.5 %copy-start.2 = (f32[3,128,128]{2,1,0:T(8,128)}, f32[3,128,128]{2,1,0:T(8,128)S(1)}, u32[]{:S(2)}) copy-start(f32[3,128,128]{2,1,0:T(8,128)S(1)} %collective-permute-done.22.refs_1_.rest_12_) | copy-start | bytes 589828
  47.1 13.0 %collective-permute-start.26 = (f32[8,128,128]{2,1,0:T(8,128)}, f32[8,128,128]{2,1,0:T(8,128)}, u32[]{:S(2)}, u32[]{:S(2)}) collective-permute-start(f32[8,128,128]{2,1,0:T(8,128)} %hold.2.rest_1_), channel_id=1, source_target_pairs={{0,1},{1,0},{2,3},{3,2},{4,5},{5,4},{6,7},{7,6},{8,9},{9,8},{10,11... | collective-permute-start | bytes 1572872 | tf_op jit(solution)/shard_map/ppermute | solution.py:445
  57.3 1.2 %copy-start.4 = (f32[3,128,128]{2,1,0:T(8,128)}, f32[3,128,128]{2,1,0:T(8,128)S(1)}, u32[]{:S(2)}) copy-start(f32[3,128,128]{2,1,0:T(8,128)S(1)} %collective-permute-done.23.refs_2_.rest_13_) | copy-start | bytes 589828
  57.3 2.8 %collective-permute-start.27 = (f32[8,128,128]{2,1,0:T(8,128)}, f32[8,128,128]{2,1,0:T(8,128)}, u32[]{:S(2)}, u32[]{:S(2)}) collective-permute-start(f32[8,128,128]{2,1,0:T(8,128)} %collective-permute-done.18.rest_2_), channel_id=1, source_target_pairs={{0,1},{1,0},{2,3},{3,2},{4,5},{5,4},{6,7},{7,6},{8,9},{9,8},{10,11... | collective-permute-start | bytes 1572872 | tf_op jit(solution)/shard_map/ppermute | solution.py:445
  57.7 0.8 %copy-start.7 = (f32[8,128,128]{2,1,0:T(8,128)}, f32[8,128,128]{2,1,0:T(8,128)S(1)}, u32[]{:S(2)}) copy-start(f32[8,128,128]{2,1,0:T(8,128)S(1)} %collective-permute-done.19.refs_0_) | copy-start | bytes 1572868
  58.5 0.7 %copy-start = (f32[6,128,128]{2,1,0:T(8,128)}, f32[6,128,128]{2,1,0:T(8,128)S(1)}, u32[]{:S(2)}) copy-start(f32[6,128,128]{2,1,0:T(8,128)S(1)} %collective-permute-done.24.refs_3_.rest_11_) | copy-start | bytes 1179652
  59.9 2.3 %collective-permute-start.28 = (f32[8,128,128]{2,1,0:T(8,128)}, f32[8,128,128]{2,1,0:T(8,128)}, u32[]{:S(2)}, u32[]{:S(2)}) collective-permute-start(f32[8,128,128]{2,1,0:T(8,128)} %hold.3.rest_3_), channel_id=1, source_target_pairs={{0,1},{1,0},{2,3},{3,2},{4,5},{5,4},{6,7},{7,6},{8,9},{9,8},{10,11... | collective-permute-start | bytes 1572872 | tf_op jit(solution)/shard_map/ppermute | solution.py:445
  62.2 1.0 %copy-start.1 = (f32[6,128,128]{2,1,0:T(8,128)S(1)}, f32[6,128,128]{2,1,0:T(8,128)}, u32[]{:S(2)}) copy-start(f32[6,128,128]{2,1,0:T(8,128)} %copy-done) | copy-start | bytes 1179652
  63.2 0.9 %copy-start.3 = (f32[3,128,128]{2,1,0:T(8,128)S(1)}, f32[3,128,128]{2,1,0:T(8,128)}, u32[]{:S(2)}) copy-start(f32[3,128,128]{2,1,0:T(8,128)} %copy-done.2) | copy-start | bytes 589828
  64.2 0.9 %copy-start.5 = (f32[3,128,128]{2,1,0:T(8,128)S(1)}, f32[3,128,128]{2,1,0:T(8,128)}, u32[]{:S(2)}) copy-start(f32[3,128,128]{2,1,0:T(8,128)} %copy-done.4) | copy-start | bytes 589828

commit v2 on v1

--- a/solution.py
+++ b/solution.py
@@ -14,7 +14,7 @@
 NEAR = 6
 FAR = 3
 COL = ("x_lo", "z", "core")
-VMEM_LIMIT = 16 << 20
+VMEM_LIMIT = 8 << 20
 A_PARTS = 8
 LIST = 512
 AHEAD = 8
@@ -163,7 +163,7 @@
             jax.ShapeDtypeStruct((40, 128), jnp.int32),
             jax.ShapeDtypeStruct((6, 128, 128), jnp.bfloat16),
         ],
-        compiler_params=pltpu.CompilerParams(vmem_limit_bytes=16 << 20),
+        compiler_params=pltpu.CompilerParams(vmem_limit_bytes=4 << 20),
         name="plan",
     )(me, spots)
 
@@ -194,7 +194,7 @@
         out_specs=[pl.BlockSpec(memory_space=pltpu.VMEM)] * len(sizes),
         scratch_shapes=[pltpu.SemaphoreType.DMA((sum(sizes),))],
         out_shape=[jax.ShapeDtypeStruct((n, size, size), jnp.float32) for n in sizes],
-        compiler_params=pltpu.CompilerParams(vmem_limit_bytes=16 << 20),
+        compiler_params=pltpu.CompilerParams(vmem_limit_bytes=4 << 20),
         name="pack",
     )(listing, *near)
 
@@ -232,7 +232,7 @@
             jax.ShapeDtypeStruct((1,), jnp.int32),
             jax.ShapeDtypeStruct((LIST + 1,), jnp.int32),
         ],
-        compiler_params=pltpu.CompilerParams(vmem_limit_bytes=16 << 20),
+        compiler_params=pltpu.CompilerParams(vmem_limit_bytes=4 << 20),
         cost_estimate=pl.CostEstimate(flops=10**9, bytes_accessed=10**5, transcendentals=0),
         name="overflow",
     )(me, info, spots, maps)
@@ -470,7 +470,7 @@
         ],
         scratch_shapes=[pltpu.SemaphoreType.DMA((2,))],
         input_output_aliases={2: 1},
-        compiler_params=pltpu.CompilerParams(vmem_limit_bytes=16 << 20),
+        compiler_params=pltpu.CompilerParams(vmem_limit_bytes=4 << 20),
         name="pair",
     )(tile, beside, passing)
 
@@ -487,6 +487,7 @@
         out_specs=[anywhere] * len(arrays),
         out_shape=[jax.ShapeDtypeStruct(x.shape, x.dtype) for x in arrays],
         input_output_aliases={i: i for i in range(len(arrays))},
+        compiler_params=pltpu.CompilerParams(vmem_limit_bytes=1 << 20),
         name="hold",
     )(*arrays, *later)
 

time: 69.3 us -> 64.3 us (0.928)
  local copies, waits for them, and re-layouts: 5.45 us -> 1.06 us
  waiting for transfers between devices: 19 us -> 17 us
  starting transfers between devices: 31.8 us -> 33.4 us
    unnamed x16 -> x4, local copies, waits for them, and re-layouts: 4.39 us -> 0.01 us
    ppermute x5, waiting for transfers between devices: 9.75 us -> 8.09 us  [to_row(): return lax.ppermute(block, 'row', [(i, there(i)) for i in range(rows)])]
    ppermute x8, starting transfers between devices: 5.14 us -> 6.06 us  [moved(): return lax.ppermute(block, COL, [(i, there(i)) for i in range(columns)])]
  transfers between devices with their start and end apart: 22 -> 22, of which waited for: 6 -> 7; matrix products, arithmetic and copies ran while one was open for 0% -> 0% of each run, Pallas kernels for 11% -> 12%
where the time goes in v2:
time: 64.3 us; the launch traced here: 64.8 us
  starting transfers between devices  33.4 us (52%)
  waiting for transfers between devices  17 us (26%)
  Pallas kernels  11.4 us (18%)
  local copies, waits for them, and re-layouts  1.06 us (2%)
  other arithmetic  0.82 us (1%)
  loops' own time  0.82 us (1%)
    ppermute x9, starting transfers between devices, among(): got = lax.ppermute(held, ('row', *COL), pairs)  19.7 us
    ppermute x5, waiting for transfers between devices, to_row(): return lax.ppermute(block, 'row', [(i, there(i)) for i in range(rows)])  8.09 us
    ppermute x5, starting transfers between devices, to_row(): return lax.ppermute(block, 'row', [(i, there(i)) for i in range(rows)])  7.62 us
    ppermute x9, waiting for transfers between devices, among(): got = lax.ppermute(held, ('row', *COL), pairs)  6.25 us
    ppermute x8, starting transfers between devices, moved(): return lax.ppermute(block, COL, [(i, there(i)) for i in range(columns)])  6.06 us
    pallas_call x1, Pallas kernels, products(): pl.pallas_call(functools.partial(kernel, parts), in_specs=[smem if x.ndim...  3.74 us
    pallas_call x1, Pallas kernels, overflow(): pl.pallas_call(overflow_kernel, in_specs=[smem, vmem, vmem, vmem], out_sp...  3.29 us
    ppermute x8, waiting for transfers between devices, moved(): return lax.ppermute(block, COL, [(i, there(i)) for i in range(columns)])  2.65 us
  transfers between devices with their start and end apart: 22, of which 7 were waited for; matrix products, arithmetic and copies ran while one was open for 0% of the time, Pallas kernels for 12%

profile of v2, /device:TPU:1, one launch (start us, length us, event | category | flops | bytes accessed | tf_op | source)
XLA Modules:
  0.0 64.8 jit_solution(155571255406680546)
XLA Ops:
  0.0 0.0 copy-start
  0.0 0.8 %reshape_squeeze.6 = s32[16]{0:T(128)S(1)} reshape(s32[1,1,2,8]{3,2,1,0:T(2,128)} %param.10) | data formatting | bytes 128 | tf_op jit(solution)/shard_map/reshape;squeeze | solution.py:525
  0.8 0.7 %pad_add_fusion.1 = s32[40]{0:T(128)S(1)} fusion(s32[16]{0:T(128)} %bitcast.43, s32[16]{0:T(128)S(1)} %reshape_squeeze.6, s32[4]{0:T(128)S(1)} %broadcast.5, s32[4]{0:T(128)} %bitcast.44), kind=kLoop, calls=%fused_computation.12 | loop fusion | flops 120 | bytes 320 | tf_op jit(solution)/shard_map/concatenate | solution.py:525
  1.6 3.8 %collective-permute-start.9 = (s32[128]{0:T(128)S(1)}, s32[128]{0:T(128)S(1)}, u32[]{:S(2)}, u32[]{:S(2)}) collective-permute-start(s32[128]{0:T(128)S(1)} %get-tuple-element.217), channel_id=1, source_target_pairs={{64,0},{65,1},{66,2},{67,3},{68,4},{69,5},{70,6},{71,7},{72,8},{73... | collective-permute-start | bytes 1544 | tf_op jit(solution)/shard_map/ppermute | solution.py:503
  5.3 0.4 collective-permute-start.8
  5.7 0.4 collective-permute-start.10
  6.1 2.3 %collective-permute-start.21 = (f32[16,128,128]{2,1,0:T(8,128)}, f32[16,128,128]{2,1,0:T(8,128)S(1)}, u32[]{:S(2)}, u32[]{:S(2)}) collective-permute-start(f32[16,128,128]{2,1,0:T(8,128)} %bitcast.38), channel_id=1, source_target_pairs={{0,96},{16,112},{32,0},{48,16},{64,32},{80,48},{96,64},{112,80},{1... | collective-permute-start | bytes 3145736 | tf_op jit(solution)/shard_map/ppermute | solution.py:433
  8.4 0.1 pad_add_fusion.me_ref
  8.5 0.1 collective-permute-start.20
  8.6 0.0 collective-permute-done.8
  8.6 0.0 copy-done
  8.6 1.3 %collective-permute-start.7 = (f32[4,128,128]{2,1,0:T(8,128)S(1)}, f32[4,128,128]{2,1,0:T(8,128)S(1)}, u32[]{:S(2)}, u32[]{:S(2)}) collective-permute-start(f32[4,128,128]{2,1,0:T(8,128)S(1)} %bitcast.34), channel_id=1, source_target_pairs={{0,8},{1,9},{2,10},{3,11},{4,12},{5,13},{6,14},{7,15},{8,0},{9,1},... | collective-permute-start | bytes 786440 | tf_op jit(solution)/shard_map/ppermute | solution.py:445
  9.9 0.0 collective-permute-done.9
  10.0 0.0 collective-permute-done.10
  10.0 0.0 copy-start.1
  10.0 1.7 %collective-permute-start.11 = (s32[4,128]{1,0:T(4,128)S(1)}, s32[4,128]{1,0:T(4,128)S(1)}, u32[]{:S(2)}, u32[]{:S(2)}) collective-permute-start(s32[4,128]{1,0:T(4,128)S(1)} %dynamic_update_slice.50), channel_id=1, source_target_pairs={{2,0},{3,1},{0,2},{1,3},{6,4},{7,5},{4,6},{5,7},{10,8},{11,9},{8,1... | collective-permute-start | bytes 6152 | tf_op jit(solution)/shard_map/ppermute | solution.py:503
  11.7 3.3 %collective-permute-start.12 = (s32[4,128]{1,0:T(4,128)S(1)}, s32[4,128]{1,0:T(4,128)S(1)}, u32[]{:S(2)}, u32[]{:S(2)}) collective-permute-start(s32[4,128]{1,0:T(4,128)S(1)} %dynamic_update_slice.50), channel_id=1, source_target_pairs={{4,0},{5,1},{6,2},{7,3},{0,4},{1,5},{2,6},{3,7},{12,8},{13,9},{14,... | collective-permute-start | bytes 6152 | tf_op jit(solution)/shard_map/ppermute | solution.py:503
  15.0 0.0 collective-permute-done.11
  15.0 1.5 %collective-permute-start.13 = (s32[4,128]{1,0:T(4,128)S(1)}, s32[4,128]{1,0:T(4,128)S(1)}, u32[]{:S(2)}, u32[]{:S(2)}) collective-permute-start(s32[4,128]{1,0:T(4,128)S(1)} %dynamic_update_slice.50), channel_id=1, source_target_pairs={{6,0},{7,1},{4,2},{5,3},{2,4},{3,5},{0,6},{1,7},{14,8},{15,9},{12,... | collective-permute-start | bytes 6152 | tf_op jit(solution)/shard_map/ppermute | solution.py:503
  16.6 0.0 collective-permute-done.12
  16.6 2.4 %collective-permute-done.13 = s32[4,128]{1,0:T(4,128)S(1)} collective-permute-done((s32[4,128]{1,0:T(4,128)S(1)}, s32[4,128]{1,0:T(4,128)S(1)}, u32[]{:S(2)}, u32[]{:S(2)}) %collective-permute-start.13) | collective-permute-done | bytes 2080 | tf_op jit(solution)/shard_map/ppermute | solution.py:503
  19.0 0.0 collective-permute-done.7.beside_ref
  19.0 0.9 %pair.1 = (f32[8,128,128]{2,1,0:T(8,128)}, s32[4,4,128]{2,1,0:T(4,128)S(1)}) custom-call(f32[4,128,128]{2,1,0:T(8,128)S(1)} %bitcast.35, f32[4,128,128]{2,1,0:T(8,128)S(1)} %collective-permute-done.7.beside_ref, s32[4,4,128]{2,1,0:T(4,128)S(1)} %constant_dynamic-update-slice_fusion._), custom_call_target="tpu_custom_call", output_to_operand_aliasing={{1}: (2, {})} | custom-call | tf_op jit(solution)/shard_map/pair/pallas_call | solution.py:463
  19.9 0.7 %collective-permute-start.14 = (s32[4,4,128]{2,1,0:T(4,128)S(1)}, s32[4,4,128]{2,1,0:T(4,128)S(1)}, u32[]{:S(2)}, u32[]{:S(2)}) collective-permute-start(s32[4,4,128]{2,1,0:T(4,128)S(1)} %get-tuple-element.178), channel_id=1, source_target_pairs={{8,0},{9,1},{10,2},{11,3},{12,4},{13,5},{14,6},{15,7},{0,8},{1,9},... | collective-permute-start | bytes 24584 | tf_op jit(solution)/shard_map/ppermute | solution.py:503
  20.5 0.0 collective-permute-start.17
  20.5 2.2 %collective-permute-done.14 = s32[4,4,128]{2,1,0:T(4,128)S(1)} collective-permute-done((s32[4,4,128]{2,1,0:T(4,128)S(1)}, s32[4,4,128]{2,1,0:T(4,128)S(1)}, u32[]{:S(2)}, u32[]{:S(2)}) %collective-permute-start.14) | collective-permute-done | bytes 8224 | tf_op jit(solution)/shard_map/ppermute | solution.py:503
  22.8 2.5 %collective-permute-start.15 = (s32[2,4,4,128]{3,2,1,0:T(4,128)S(1)}, s32[2,4,4,128]{3,2,1,0:T(4,128)S(1)}, u32[]{:S(2)}, u32[]{:S(2)}) collective-permute-start(s32[2,4,4,128]{3,2,1,0:T(4,128)S(1)} %bitcast_dynamic-update-slice_fusion.4), channel_id=1, source_target_pairs={{16,0},{17,1},{18,2},{19,3},{20,4},{21,5},{22,6},{23,7},{24,8},{25... | collective-permute-start | bytes 49160 | tf_op jit(solution)/shard_map/ppermute | solution.py:503
  25.2 1.6 %collective-permute-done.15 = s32[2,4,4,128]{3,2,1,0:T(4,128)S(1)} collective-permute-done((s32[2,4,4,128]{3,2,1,0:T(4,128)S(1)}, s32[2,4,4,128]{3,2,1,0:T(4,128)S(1)}, u32[]{:S(2)}, u32[]{:S(2)}) %collective-permute-start.15) | collective-permute-done | bytes 16416 | tf_op jit(solution)/shard_map/ppermute | solution.py:503
  26.9 5.5 %collective-permute-start.16 = (s32[2,2,4,4,128]{4,3,2,1,0:T(4,128)S(1)}, s32[2,2,4,4,128]{4,3,2,1,0:T(4,128)S(1)}, u32[]{:S(2)}, u32[]{:S(2)}) collective-permute-start(s32[2,2,4,4,128]{4,3,2,1,0:T(4,128)S(1)} %bitcast_dynamic-update-slice_fusion.2), channel_id=1, source_target_pairs={{1,0},{0,1},{3,2},{2,3},{5,4},{4,5},{7,6},{6,7},{9,8},{8,9},{11,10... | collective-permute-start | bytes 98312 | tf_op jit(solution)/shard_map/ppermute | solution.py:503
  32.4 1.9 %collective-permute-start.18 = (f32[8,128,128]{2,1,0:T(8,128)}, f32[8,128,128]{2,1,0:T(8,128)}, u32[]{:S(2)}, u32[]{:S(2)}) collective-permute-start(f32[8,128,128]{2,1,0:T(8,128)} %get-tuple-element.311.rest_0_), channel_id=1, source_target_pairs={{0,6},{1,7},{2,0},{3,1},{4,2},{5,3},{6,4},{7,5},{8,14},{9,15},{10,... | collective-permute-start | bytes 1572872 | tf_op jit(solution)/shard_map/ppermute | solution.py:445
  34.3 0.0 collective-permute-done.16
  34.3 1.8 %plan.1 = (s32[12]{0:T(128)S(1)}, s32[40,128]{1,0:T(8,128)S(1)}, bf16[6,128,128]{2,1,0:T(8,128)(2,1)S(1)}) custom-call(s32[2]{0:T(128)S(1)} %pad_add_fusion.me_ref, s32[128,128]{1,0:T(8,128)S(1)} %bitcast.36), custom_call_target="tpu_custom_call" | custom-call | tf_op jit(solution)/shard_map/plan/pallas_call | solution.py:157
  36.1 0.0 collective-permute-done.17.refs_0_
  36.1 0.1 collective-permute-start.19
  36.2 0.0 collective-permute-done.21.rest_2_.rest_10_
  36.2 0.0 collective-permute-done.20.rest_1_.rest_9_
  36.2 0.0 copy-done.1
  36.2 1.1 %pack.1 = (f32[3,128,128]{2,1,0:T(8,128)S(1)}, f32[3,128,128]{2,1,0:T(8,128)S(1)}, f32[6,128,128]{2,1,0:T(8,128)S(1)}) custom-call(s32[12]{0:T(128)S(1)} %get-tuple-element.183.list_ref, f32[16,128,128]{2,1,0:T(8,128)S(1)} %bitcast.42, f32[16,128,128]{2,1,0:T(8,128)S(1)} %collective-permute-done.20.rest_1_.rest_9_, ...), custom_call_target="tpu_custom_call" | custom-call | tf_op jit(solution)/shard_map/pack/pallas_call | solution.py:190
  37.3 2.5 %collective-permute-start.24 = (f32[6,128,128]{2,1,0:T(8,128)S(1)}, f32[6,128,128]{2,1,0:T(8,128)S(1)}, u32[]{:S(2)}, u32[]{:S(2)}) collective-permute-start(f32[6,128,128]{2,1,0:T(8,128)S(1)} %get-tuple-element.186), channel_id=1, source_target_pairs={{0,16},{16,0},{32,48},{48,32},{64,80},{80,64},{96,112},{112,96},{1... | collective-permute-start | bytes 1179656 | tf_op jit(solution)/shard_map/ppermute | solution.py:433
  39.9 2.7 %collective-permute-start.22 = (f32[3,128,128]{2,1,0:T(8,128)S(1)}, f32[3,128,128]{2,1,0:T(8,128)S(1)}, u32[]{:S(2)}, u32[]{:S(2)}) collective-permute-start(f32[3,128,128]{2,1,0:T(8,128)S(1)} %get-tuple-element.184), channel_id=1, source_target_pairs={{0,96},{16,112},{32,0},{48,16},{64,32},{80,48},{96,64},{112,80},{1... | collective-permute-start | bytes 589832 | tf_op jit(solution)/shard_map/ppermute | solution.py:433
  42.6 0.0 collective-permute-start.23
  42.6 3.3 %overflow.1 = (s32[1]{0:T(128)}, s32[513]{0:T(1024)S(1)}) custom-call(s32[2]{0:T(128)S(1)} %pad_add_fusion.me_ref, s32[40,128]{1,0:T(8,128)S(1)} %get-tuple-element.310.info_ref.refs_1_, s32[128,128]{1,0:T(8,128)S(1)} %bitcast.37, bf16[6,128,128]{2,1,0:T(8,128)(2,1)S(1)} %get-tuple-element.180.maps_ref), custom_call_target="tpu_custom_call" | custom-call | flops 1000000000 | bytes 100000 | tf_op jit(solution)/shard_map/overflow/pallas_call | solution.py:227
  45.9 0.4 collective-permute-done.18.rest_2_
  46.3 0.8 %collective-permute-start.25 = (f32[8,128,128]{2,1,0:T(8,128)}, f32[8,128,128]{2,1,0:T(8,128)}, u32[]{:S(2)}, u32[]{:S(2)}) collective-permute-start(f32[8,128,128]{2,1,0:T(8,128)} %get-tuple-element.311.rest_0_), channel_id=1, source_target_pairs={{0,1},{1,0},{2,3},{3,2},{4,5},{5,4},{6,7},{7,6},{8,9},{9,8},{10,11... | collective-permute-start | bytes 1572872 | tf_op jit(solution)/shard_map/ppermute | solution.py:445
  47.1 0.0 collective-permute-done.22.refs_1_.rest_12_
  47.1 0.6 collective-permute-start.26
  47.7 8.1 %collective-permute-done.23.refs_2_.rest_13_ = f32[3,128,128]{2,1,0:T(8,128)S(1)} collective-permute-done((f32[3,128,128]{2,1,0:T(8,128)S(1)}, f32[3,128,128]{2,1,0:T(8,128)S(1)}, u32[]{:S(2)}, u32[]{:S(2)}) %collective-permute-start.23) | collective-permute-done | bytes 196640 | tf_op jit(solution)/shard_map/ppermute | solution.py:433
  55.8 1.3 %collective-permute-start.27 = (f32[8,128,128]{2,1,0:T(8,128)}, f32[8,128,128]{2,1,0:T(8,128)}, u32[]{:S(2)}, u32[]{:S(2)}) collective-permute-start(f32[8,128,128]{2,1,0:T(8,128)} %collective-permute-done.18.rest_2_), channel_id=1, source_target_pairs={{0,1},{1,0},{2,3},{3,2},{4,5},{5,4},{6,7},{7,6},{8,9},{9,8},{10,11... | collective-permute-start | bytes 1572872 | tf_op jit(solution)/shard_map/ppermute | solution.py:445
  57.1 0.0 collective-permute-done.19.refs_0_
  57.1 0.0 collective-permute-done.24.refs_3_.rest_11_
  57.1 0.6 hold.3.rest_3_
  57.8 0.1 collective-permute-start.28
  57.9 0.0 collective-permute-done.25.rest_4_
  57.9 1.1 %collective-permute-done.27.rest_6_ = f32[8,128,128]{2,1,0:T(8,128)} collective-permute-done((f32[8,128,128]{2,1,0:T(8,128)}, f32[8,128,128]{2,1,0:T(8,128)}, u32[]{:S(2)}, u32[]{:S(2)}) %collective-permute-start.27) | collective-permute-done | bytes 524320 | tf_op jit(solution)/shard_map/ppermute | solution.py:445
  59.0 0.0 collective-permute-done.26.rest_5_
  59.0 1.1 %collective-permute-done.28.rest_7_ = f32[8,128,128]{2,1,0:T(8,128)} collective-permute-done((f32[8,128,128]{2,1,0:T(8,128)}, f32[8,128,128]{2,1,0:T(8,128)}, u32[]{:S(2)}, u32[]{:S(2)}) %collective-permute-start.28) | collective-permute-done | bytes 524320 | tf_op jit(solution)/shard_map/ppermute | solution.py:445
  60.1 3.7 %products.5 = f32[16,128,128]{2,1,0:T(8,128)} custom-call(s32[513]{0:T(1024)S(1)} %get-tuple-element.181.list_ref, f32[8,128,128]{2,1,0:T(8,128)} %get-tuple-element.311.rest_0_, f32[8,128,128]{2,1,0:T(8,128)} %hold.2.rest_1_, f32[8,128,128]{2,1,0:T(8,128)} %collective-permute-done.18.rest_2_, f32[8,128,128]{2,1,0:T(8,128)} %hold.3.rest_3_, ...), custom_call_target="tpu_custom_call" | custom-call | flops 100663296 | bytes 1572864 | tf_op jit(solution)/shard_map/products/pallas_call | solution.py:406
  63.8 0.8 %while.12 = (s32[]{:T(128)}, f32[16,128,128]{2,1,0:T(8,128)}, s32[]{:T(128)}, f32[16,128,128]{2,1,0:T(8,128)}, s32[2]{0:T(128)S(1)}, /*index=5*/s32[40,128]{1,0:...) while((s32[]{:T(128)}, f32[16,128,128]{2,1,0:T(8,128)}, ...), condition=%wide.region_1.2_spmd, body=%wide.region_0.1_spmd.sunk | while | flops 100925440 | bytes 33030584 | solution.py:567
  (22 shorter events, 0.3 us)
Async XLA Ops:
  0.0 8.6 %copy-start = (f32[1,1,4,128,128]{4,3,2,1,0:T(8,128)S(1)}, f32[1,1,4,128,128]{4,3,2,1,0:T(8,128)}, u32[]{:S(2)}) copy-start(f32[1,1,4,128,128]{4,3,2,1,0:T(8,128)} %param.7) | copy-start | bytes 786436
  1.6 8.4 %collective-permute-start.9 = (s32[128]{0:T(128)S(1)}, s32[128]{0:T(128)S(1)}, u32[]{:S(2)}, u32[]{:S(2)}) collective-permute-start(s32[128]{0:T(128)S(1)} %get-tuple-element.217), channel_id=1, source_target_pairs={{64,0},{65,1},{66,2},{67,3},{68,4},{69,5},{70,6},{71,7},{72,8},{73... | collective-permute-start | bytes 1544 | tf_op jit(solution)/shard_map/ppermute | solution.py:503
  5.3 3.3 %collective-permute-start.8 = (s32[128]{0:T(128)S(1)}, s32[128]{0:T(128)S(1)}, u32[]{:S(2)}, u32[]{:S(2)}) collective-permute-start(s32[128]{0:T(128)S(1)} %get-tuple-element.217), channel_id=1, source_target_pairs={{32,0},{33,1},{34,2},{35,3},{36,4},{37,5},{38,6},{39,7},{40,8},{41... | collective-permute-start | bytes 1544 | tf_op jit(solution)/shard_map/ppermute | solution.py:503
  5.7 4.2 %collective-permute-start.10 = (s32[128]{0:T(128)S(1)}, s32[128]{0:T(128)S(1)}, u32[]{:S(2)}, u32[]{:S(2)}) collective-permute-start(s32[128]{0:T(128)S(1)} %get-tuple-element.217), channel_id=1, source_target_pairs={{96,0},{97,1},{98,2},{99,3},{100,4},{101,5},{102,6},{103,7},{104,8... | collective-permute-start | bytes 1544 | tf_op jit(solution)/shard_map/ppermute | solution.py:503
  6.1 30.1 %collective-permute-start.21 = (f32[16,128,128]{2,1,0:T(8,128)}, f32[16,128,128]{2,1,0:T(8,128)S(1)}, u32[]{:S(2)}, u32[]{:S(2)}) collective-permute-start(f32[16,128,128]{2,1,0:T(8,128)} %bitcast.38), channel_id=1, source_target_pairs={{0,96},{16,112},{32,0},{48,16},{64,32},{80,48},{96,64},{112,80},{1... | collective-permute-start | bytes 3145736 | tf_op jit(solution)/shard_map/ppermute | solution.py:433
  8.5 27.7 %collective-permute-start.20 = (f32[16,128,128]{2,1,0:T(8,128)}, f32[16,128,128]{2,1,0:T(8,128)S(1)}, u32[]{:S(2)}, u32[]{:S(2)}) collective-permute-start(f32[16,128,128]{2,1,0:T(8,128)} %bitcast.39), channel_id=1, source_target_pairs={{0,32},{16,48},{32,64},{48,80},{64,96},{80,112},{96,0},{112,16},{1... | collective-permute-start | bytes 3145736 | tf_op jit(solution)/shard_map/ppermute | solution.py:433
  8.6 10.4 %collective-permute-start.7 = (f32[4,128,128]{2,1,0:T(8,128)S(1)}, f32[4,128,128]{2,1,0:T(8,128)S(1)}, u32[]{:S(2)}, u32[]{:S(2)}) collective-permute-start(f32[4,128,128]{2,1,0:T(8,128)S(1)} %bitcast.34), channel_id=1, source_target_pairs={{0,8},{1,9},{2,10},{3,11},{4,12},{5,13},{6,14},{7,15},{8,0},{9,1},... | collective-permute-start | bytes 786440 | tf_op jit(solution)/shard_map/ppermute | solution.py:445
  10.0 26.2 %copy-start.1 = (f32[1,1,2,8,128,128]{5,4,3,2,1,0:T(8,128)S(1)}, f32[1,1,2,8,128,128]{5,4,3,2,1,0:T(8,128)}, u32[]{:S(2)}) copy-start(f32[1,1,2,8,128,128]{5,4,3,2,1,0:T(8,128)} %param.9) | copy-start | bytes 3145732
  10.0 5.0 %collective-permute-start.11 = (s32[4,128]{1,0:T(4,128)S(1)}, s32[4,128]{1,0:T(4,128)S(1)}, u32[]{:S(2)}, u32[]{:S(2)}) collective-permute-start(s32[4,128]{1,0:T(4,128)S(1)} %dynamic_update_slice.50), channel_id=1, source_target_pairs={{2,0},{3,1},{0,2},{1,3},{6,4},{7,5},{4,6},{5,7},{10,8},{11,9},{8,1... | collective-permute-start | bytes 6152 | tf_op jit(solution)/shard_map/ppermute | solution.py:503
  11.7 4.9 %collective-permute-start.12 = (s32[4,128]{1,0:T(4,128)S(1)}, s32[4,128]{1,0:T(4,128)S(1)}, u32[]{:S(2)}, u32[]{:S(2)}) collective-permute-start(s32[4,128]{1,0:T(4,128)S(1)} %dynamic_update_slice.50), channel_id=1, source_target_pairs={{4,0},{5,1},{6,2},{7,3},{0,4},{1,5},{2,6},{3,7},{12,8},{13,9},{14,... | collective-permute-start | bytes 6152 | tf_op jit(solution)/shard_map/ppermute | solution.py:503
  15.0 3.9 %collective-permute-start.13 = (s32[4,128]{1,0:T(4,128)S(1)}, s32[4,128]{1,0:T(4,128)S(1)}, u32[]{:S(2)}, u32[]{:S(2)}) collective-permute-start(s32[4,128]{1,0:T(4,128)S(1)} %dynamic_update_slice.50), channel_id=1, source_target_pairs={{6,0},{7,1},{4,2},{5,3},{2,4},{3,5},{0,6},{1,7},{14,8},{15,9},{12,... | collective-permute-start | bytes 6152 | tf_op jit(solution)/shard_map/ppermute | solution.py:503
  19.9 2.9 %collective-permute-start.14 = (s32[4,4,128]{2,1,0:T(4,128)S(1)}, s32[4,4,128]{2,1,0:T(4,128)S(1)}, u32[]{:S(2)}, u32[]{:S(2)}) collective-permute-start(s32[4,4,128]{2,1,0:T(4,128)S(1)} %get-tuple-element.178), channel_id=1, source_target_pairs={{8,0},{9,1},{10,2},{11,3},{12,4},{13,5},{14,6},{15,7},{0,8},{1,9},... | collective-permute-start | bytes 24584 | tf_op jit(solution)/shard_map/ppermute | solution.py:503
  20.5 15.6 %collective-permute-start.17 = (f32[8,128,128]{2,1,0:T(8,128)}, f32[8,128,128]{2,1,0:T(8,128)}, u32[]{:S(2)}, u32[]{:S(2)}) collective-permute-start(f32[8,128,128]{2,1,0:T(8,128)} %get-tuple-element.311.rest_0_), channel_id=1, source_target_pairs={{0,2},{1,3},{2,4},{3,5},{4,6},{5,7},{6,0},{7,1},{8,10},{9,11},{10,... | collective-permute-start | bytes 1572872 | tf_op jit(solution)/shard_map/ppermute | solution.py:445
  22.8 4.1 %collective-permute-start.15 = (s32[2,4,4,128]{3,2,1,0:T(4,128)S(1)}, s32[2,4,4,128]{3,2,1,0:T(4,128)S(1)}, u32[]{:S(2)}, u32[]{:S(2)}) collective-permute-start(s32[2,4,4,128]{3,2,1,0:T(4,128)S(1)} %bitcast_dynamic-update-slice_fusion.4), channel_id=1, source_target_pairs={{16,0},{17,1},{18,2},{19,3},{20,4},{21,5},{22,6},{23,7},{24,8},{25... | collective-permute-start | bytes 49160 | tf_op jit(solution)/shard_map/ppermute | solution.py:503
  26.9 7.4 %collective-permute-start.16 = (s32[2,2,4,4,128]{4,3,2,1,0:T(4,128)S(1)}, s32[2,2,4,4,128]{4,3,2,1,0:T(4,128)S(1)}, u32[]{:S(2)}, u32[]{:S(2)}) collective-permute-start(s32[2,2,4,4,128]{4,3,2,1,0:T(4,128)S(1)} %bitcast_dynamic-update-slice_fusion.2), channel_id=1, source_target_pairs={{1,0},{0,1},{3,2},{2,3},{5,4},{4,5},{7,6},{6,7},{9,8},{8,9},{11,10... | collective-permute-start | bytes 98312 | tf_op jit(solution)/shard_map/ppermute | solution.py:503
  32.4 13.9 %collective-permute-start.18 = (f32[8,128,128]{2,1,0:T(8,128)}, f32[8,128,128]{2,1,0:T(8,128)}, u32[]{:S(2)}, u32[]{:S(2)}) collective-permute-start(f32[8,128,128]{2,1,0:T(8,128)} %get-tuple-element.311.rest_0_), channel_id=1, source_target_pairs={{0,6},{1,7},{2,0},{3,1},{4,2},{5,3},{6,4},{7,5},{8,14},{9,15},{10,... | collective-permute-start | bytes 1572872 | tf_op jit(solution)/shard_map/ppermute | solution.py:445
  36.1 21.0 %collective-permute-start.19 = (f32[8,128,128]{2,1,0:T(8,128)}, f32[8,128,128]{2,1,0:T(8,128)}, u32[]{:S(2)}, u32[]{:S(2)}) collective-permute-start(f32[8,128,128]{2,1,0:T(8,128)} %hold.2.rest_1_), channel_id=1, source_target_pairs={{0,2},{1,3},{2,4},{3,5},{4,6},{5,7},{6,0},{7,1},{8,10},{9,11},{10,... | collective-permute-start | bytes 1572872 | tf_op jit(solution)/shard_map/ppermute | solution.py:445
  37.3 19.8 %collective-permute-start.24 = (f32[6,128,128]{2,1,0:T(8,128)S(1)}, f32[6,128,128]{2,1,0:T(8,128)S(1)}, u32[]{:S(2)}, u32[]{:S(2)}) collective-permute-start(f32[6,128,128]{2,1,0:T(8,128)S(1)} %get-tuple-element.186), channel_id=1, source_target_pairs={{0,16},{16,0},{32,48},{48,32},{64,80},{80,64},{96,112},{112,96},{1... | collective-permute-start | bytes 1179656 | tf_op jit(solution)/shard_map/ppermute | solution.py:433
  39.9 7.2 %collective-permute-start.22 = (f32[3,128,128]{2,1,0:T(8,128)S(1)}, f32[3,128,128]{2,1,0:T(8,128)S(1)}, u32[]{:S(2)}, u32[]{:S(2)}) collective-permute-start(f32[3,128,128]{2,1,0:T(8,128)S(1)} %get-tuple-element.184), channel_id=1, source_target_pairs={{0,96},{16,112},{32,0},{48,16},{64,32},{80,48},{96,64},{112,80},{1... | collective-permute-start | bytes 589832 | tf_op jit(solution)/shard_map/ppermute | solution.py:433
  42.6 13.2 %collective-permute-start.23 = (f32[3,128,128]{2,1,0:T(8,128)S(1)}, f32[3,128,128]{2,1,0:T(8,128)S(1)}, u32[]{:S(2)}, u32[]{:S(2)}) collective-permute-start(f32[3,128,128]{2,1,0:T(8,128)S(1)} %get-tuple-element.185), channel_id=1, source_target_pairs={{0,48},{16,32},{32,80},{48,64},{64,112},{80,96},{96,16},{112,0},{1... | collective-permute-start | bytes 589832 | tf_op jit(solution)/shard_map/ppermute | solution.py:433
  46.3 11.5 %collective-permute-start.25 = (f32[8,128,128]{2,1,0:T(8,128)}, f32[8,128,128]{2,1,0:T(8,128)}, u32[]{:S(2)}, u32[]{:S(2)}) collective-permute-start(f32[8,128,128]{2,1,0:T(8,128)} %get-tuple-element.311.rest_0_), channel_id=1, source_target_pairs={{0,1},{1,0},{2,3},{3,2},{4,5},{5,4},{6,7},{7,6},{8,9},{9,8},{10,11... | collective-permute-start | bytes 1572872 | tf_op jit(solution)/shard_map/ppermute | solution.py:445
  47.1 11.9 %collective-permute-start.26 = (f32[8,128,128]{2,1,0:T(8,128)}, f32[8,128,128]{2,1,0:T(8,128)}, u32[]{:S(2)}, u32[]{:S(2)}) collective-permute-start(f32[8,128,128]{2,1,0:T(8,128)} %hold.2.rest_1_), channel_id=1, source_target_pairs={{0,1},{1,0},{2,3},{3,2},{4,5},{5,4},{6,7},{7,6},{8,9},{9,8},{10,11... | collective-permute-start | bytes 1572872 | tf_op jit(solution)/shard_map/ppermute | solution.py:445
  55.8 3.2 %collective-permute-start.27 = (f32[8,128,128]{2,1,0:T(8,128)}, f32[8,128,128]{2,1,0:T(8,128)}, u32[]{:S(2)}, u32[]{:S(2)}) collective-permute-start(f32[8,128,128]{2,1,0:T(8,128)} %collective-permute-done.18.rest_2_), channel_id=1, source_target_pairs={{0,1},{1,0},{2,3},{3,2},{4,5},{5,4},{6,7},{7,6},{8,9},{9,8},{10,11... | collective-permute-start | bytes 1572872 | tf_op jit(solution)/shard_map/ppermute | solution.py:445
  57.8 2.3 %collective-permute-start.28 = (f32[8,128,128]{2,1,0:T(8,128)}, f32[8,128,128]{2,1,0:T(8,128)}, u32[]{:S(2)}, u32[]{:S(2)}) collective-permute-start(f32[8,128,128]{2,1,0:T(8,128)} %hold.3.rest_3_), channel_id=1, source_target_pairs={{0,1},{1,0},{2,3},{3,2},{4,5},{5,4},{6,7},{7,6},{8,9},{9,8},{10,11... | collective-permute-start | bytes 1572872 | tf_op jit(solution)/shard_map/ppermute | solution.py:445

commit v3 on v2

--- a/solution.py
+++ b/solution.py
@@ -199,7 +199,13 @@
     )(listing, *near)
 
 
-def overflow_kernel(me_ref, info_ref, spots_ref, maps_ref, over_ref, product_list):
+def overflow_kernel(
+    me_ref, info_ref, spots_ref, maps_ref, over_ref, product_list, zeros_ref, zero, sem
+):
+    zero[...] = jnp.zeros_like(zero)
+    stores = [pltpu.make_async_copy(zero, zeros_ref.at[c], sem.at[c]) for c in range(sem.shape[0])]
+    for store in stores:
+        store.start()
     extract(entries_of(info_ref, me_ref)[0], product_list)
     held = positions(spots_ref, maps_ref)
     a = held[:8].astype(jnp.int32)
@@ -219,19 +225,23 @@
     *_, way = lane_facts(most.shape)
     slots = jnp.where(way == 0, 128, jnp.where(way == 1, NEAR, FAR))
     over_ref[0] = jnp.max(jnp.where(most > slots.astype(jnp.float32), 1.0, 0.0)).astype(jnp.int32)
-
-
-def overflow(me, info, spots, maps):
+    for store in stores:
+        store.wait()
+
+
+def overflow(me, info, spots, maps, slots, size):
     smem = pl.BlockSpec(memory_space=pltpu.SMEM)
     vmem = pl.BlockSpec(memory_space=pltpu.VMEM)
     return pl.pallas_call(
         overflow_kernel,
         in_specs=[smem, vmem, vmem, vmem],
-        out_specs=[smem, smem],
+        out_specs=[smem, smem, pl.BlockSpec(memory_space=pltpu.HBM)],
         out_shape=[
             jax.ShapeDtypeStruct((1,), jnp.int32),
             jax.ShapeDtypeStruct((LIST + 1,), jnp.int32),
+            jax.ShapeDtypeStruct((slots, size, size), jnp.float32),
         ],
+        scratch_shapes=[pltpu.VMEM((size, size), jnp.float32), pltpu.SemaphoreType.DMA((slots,))],
         compiler_params=pltpu.CompilerParams(vmem_limit_bytes=4 << 20),
         cost_estimate=pl.CostEstimate(flops=10**9, bytes_accessed=10**5, transcendentals=0),
         name="overflow",
@@ -329,7 +339,7 @@
 
 def all_kernel(parts, list_ref, *rest):
     a_refs, b_refs = rest[:A_PARTS], rest[A_PARTS:parts]
-    out_ref, acc, c_sem, touched, *buffers = rest[parts:]
+    _, out_ref, acc, c_sem, touched, *buffers = rest[parts:]
     slots = acc.shape[0]
 
     def stored(c):
@@ -345,14 +355,12 @@
 
         lax.fori_loop(0, list_ref[LIST], mark, 0)
         acc[...] = jnp.zeros_like(acc)
-        for c in range(slots):
-            pl.when(touched[c] == 0)(lambda c=c: stored(c).start())
 
     multiply_listed(list_ref, a_refs, b_refs, acc, *buffers, meanwhile)
     for c in range(slots):
         pl.when(touched[c] == 1)(lambda c=c: stored(c).start())
     for c in range(slots):
-        stored(c).wait()
+        pl.when(touched[c] == 1)(lambda c=c: stored(c).wait())
 
 
 def add_listed(list_ref, a_refs, b_refs, total_ref, out_ref, acc, c_sem, stage, *buffers):
@@ -524,9 +532,9 @@
     blank = jnp.full((8 - sa,), -1, jnp.int32)
     mine = jnp.concatenate([a_index[0, 0], blank, b_index[0, 0].reshape(-1), c_index[0, 0]])
     spots = among(jnp.pad(mine, (0, 128 - mine.shape[0])), (5, 6), rows, columns)
-    spots = among(spots, (1, 2), rows, columns)
     tile = a_blocks[0, 0]
     pair, spots = paired(tile, moved(tile, lambda i: i ^ 8, columns), spots)
+    spots = among(spots, (1, 2), rows, columns)
     spots = among(spots, (3,), rows, columns)
     spots = among(spots, (4,), rows, columns)
     spots = among(spots, (0,), rows, columns).reshape(rows * columns, 128)
@@ -534,26 +542,26 @@
     a_ahead = moved(pair, back_z, columns)
 
     sends = [
+        (FAR, 3, lambda i: ((i + 2) & 7) ^ 1),
         (FAR, 2, lambda i: (i - 2) & 7),
-        (FAR, 3, lambda i: ((i + 2) & 7) ^ 1),
         (NEAR, 1, lambda i: i ^ 1),
     ]
     pack_list, info, maps = plan(me, spots, sends)
     packed = pack(pack_list, near, [n for n, *_ in sends])
 
-    far_own, far_other, cross = [
+    far_other, far_own, cross = [
         to_row(block, rows, there) for block, (*_, there) in zip(packed, sends)
     ]
 
-    over, product_list = overflow(me, info, spots, maps)
+    over, product_list, zeros = overflow(me, info, spots, maps, sc, size)
     (a_behind,) = held_for([a_behind], [info])
     a_far = moved(a_behind, on_z, columns)
-    (a_far,) = held_for([a_far], [far_own, far_other, cross, over])
+    (a_far,) = held_for([a_far], [far_other, far_own, cross, over])
     a_mine = [pair, a_behind, a_ahead, a_far]
     a_parts = a_mine + [moved(block, lambda i: i ^ 1, columns) for block in a_mine]
 
     b_parts = near + [cross, far_own, far_other]
-    total = products(all_kernel, [product_list], a_parts, b_parts, None, sc)
+    total = products(all_kernel, [product_list], a_parts, b_parts, zeros, sc)
 
     trips = over[0]
 

time: 64.3 us -> 64.8 us (level); the launches traced: 64.8 us -> 63.7 us
  Pallas kernels: 11.4 us -> 9.98 us
    ppermute x9, starting transfers between devices: 19.7 us -> 17.8 us  [among(): got = lax.ppermute(held, ('row', *COL), pairs)]
    ppermute x8, starting transfers between devices: 6.06 us -> 7.93 us  [moved(): return lax.ppermute(block, COL, [(i, there(i)) for i in range(columns)])]
    ppermute x9, waiting for transfers between devices: 6.25 us -> 7.51 us  [among(): got = lax.ppermute(held, ('row', *COL), pairs)]
    pallas_call x1, Pallas kernels: 3.74 us -> 2.72 us  [products(): pl.pallas_call(functools.partial(kernel, parts), in_specs=[smem if x.ndim...]
    ppermute x5, waiting for transfers between devices: 8.09 us -> 7.19 us  [to_row(): return lax.ppermute(block, 'row', [(i, there(i)) for i in range(rows)])]
  transfers between devices with their start and end apart: 22 -> 22, of which waited for: 7 -> 9; matrix products, arithmetic and copies ran while one was open for 0% -> 3% of each run, Pallas kernels for 12% -> 11%
where the time goes in v3:
time: 64.8 us; the launch traced here: 63.7 us
  starting transfers between devices  33.5 us (52%)
  waiting for transfers between devices  17.2 us (27%)
  Pallas kernels  9.98 us (15%)
  local copies, waits for them, and re-layouts  1.02 us (2%)
  other arithmetic  0.82 us (1%)
  loops' own time  0.82 us (1%)
    ppermute x9, starting transfers between devices, among(): got = lax.ppermute(held, ('row', *COL), pairs)  17.8 us
    ppermute x8, starting transfers between devices, moved(): return lax.ppermute(block, COL, [(i, there(i)) for i in range(columns)])  7.93 us
    ppermute x5, starting transfers between devices, to_row(): return lax.ppermute(block, 'row', [(i, there(i)) for i in range(rows)])  7.85 us
    ppermute x9, waiting for transfers between devices, among(): got = lax.ppermute(held, ('row', *COL), pairs)  7.51 us
    ppermute x5, waiting for transfers between devices, to_row(): return lax.ppermute(block, 'row', [(i, there(i)) for i in range(rows)])  7.19 us
    pallas_call x1, Pallas kernels, overflow(): pl.pallas_call(overflow_kernel, in_specs=[smem, vmem, vmem, vmem], out_sp...  2.97 us
    pallas_call x1, Pallas kernels, products(): pl.pallas_call(functools.partial(kernel, parts), in_specs=[smem if x.ndim...  2.72 us
    ppermute x8, waiting for transfers between devices, moved(): return lax.ppermute(block, COL, [(i, there(i)) for i in range(columns)])  2.53 us
  transfers between devices with their start and end apart: 22, of which 9 were waited for; matrix products, arithmetic and copies ran while one was open for 3% of the time, Pallas kernels for 11%

profile of v3, /device:TPU:1, one launch (start us, length us, event | category | flops | bytes accessed | tf_op | source)
XLA Modules:
  0.0 63.7 jit_solution(11240493375660193980)
XLA Ops:
  0.0 0.0 copy-start
  0.0 2.0 %collective-permute-start.7 = (f32[4,128,128]{2,1,0:T(8,128)}, f32[4,128,128]{2,1,0:T(8,128)S(1)}, u32[]{:S(2)}, u32[]{:S(2)}) collective-permute-start(f32[4,128,128]{2,1,0:T(8,128)} %bitcast.34), channel_id=1, source_target_pairs={{0,8},{1,9},{2,10},{3,11},{4,12},{5,13},{6,14},{7,15},{8,0},{9,1},... | collective-permute-start | bytes 786440 | tf_op jit(solution)/shard_map/ppermute | solution.py:453
  2.0 0.8 %reshape_squeeze.6 = s32[16]{0:T(128)S(1)} reshape(s32[1,1,2,8]{3,2,1,0:T(2,128)} %param.10) | data formatting | bytes 128 | tf_op jit(solution)/shard_map/reshape;squeeze | solution.py:533
  2.8 0.7 %pad_add_fusion.1 = s32[40]{0:T(128)S(1)} fusion(s32[16]{0:T(128)} %bitcast.43, s32[16]{0:T(128)S(1)} %reshape_squeeze.6, s32[4]{0:T(128)S(1)} %broadcast.5, s32[4]{0:T(128)} %bitcast.44), kind=kLoop, calls=%fused_computation.12 | loop fusion | flops 120 | bytes 320 | tf_op jit(solution)/shard_map/concatenate | solution.py:533
  3.6 2.9 %collective-permute-start.9 = (s32[128]{0:T(128)S(1)}, s32[128]{0:T(128)S(1)}, u32[]{:S(2)}, u32[]{:S(2)}) collective-permute-start(s32[128]{0:T(128)S(1)} %get-tuple-element.219), channel_id=1, source_target_pairs={{64,0},{65,1},{66,2},{67,3},{68,4},{69,5},{70,6},{71,7},{72,8},{73... | collective-permute-start | bytes 1544 | tf_op jit(solution)/shard_map/ppermute | solution.py:511
  6.5 0.4 collective-permute-start.8
  6.9 0.4 collective-permute-start.10
  7.3 0.1 pad_add_fusion.me_ref
  7.4 2.3 %collective-permute-start.21 = (f32[16,128,128]{2,1,0:T(8,128)}, f32[16,128,128]{2,1,0:T(8,128)S(1)}, u32[]{:S(2)}, u32[]{:S(2)}) collective-permute-start(f32[16,128,128]{2,1,0:T(8,128)} %bitcast.38), channel_id=1, source_target_pairs={{0,96},{16,112},{32,0},{48,16},{64,32},{80,48},{96,64},{112,80},{1... | collective-permute-start | bytes 3145736 | tf_op jit(solution)/shard_map/ppermute | solution.py:441
  9.7 0.0 collective-permute-done.8
  9.8 0.1 collective-permute-start.20
  9.9 0.0 collective-permute-done.9
  9.9 0.6 collective-permute-done.10
  10.5 0.0 copy-start.1
  10.5 0.0 collective-permute-done.7.beside_ref
  10.5 0.0 copy-done
  10.6 0.9 %pair.1 = (f32[8,128,128]{2,1,0:T(8,128)}, s32[4,128]{1,0:T(4,128)S(1)}) custom-call(f32[4,128,128]{2,1,0:T(8,128)S(1)} %bitcast.35, f32[4,128,128]{2,1,0:T(8,128)S(1)} %collective-permute-done.7.beside_ref, s32[4,128]{1,0:T(4,128)S(1)} %dynamic_update_slice.50._), custom_call_target="tpu_custom_call", output_to_operand_aliasing={{1}: (2, {})} | custom-call | tf_op jit(solution)/shard_map/pair/pallas_call | solution.py:471
  11.4 3.8 %collective-permute-start.13 = (s32[4,128]{1,0:T(4,128)S(1)}, s32[4,128]{1,0:T(4,128)S(1)}, u32[]{:S(2)}, u32[]{:S(2)}) collective-permute-start(s32[4,128]{1,0:T(4,128)S(1)} %get-tuple-element.179), channel_id=1, source_target_pairs={{6,0},{7,1},{4,2},{5,3},{2,4},{3,5},{0,6},{1,7},{14,8},{15,9},{12,... | collective-permute-start | bytes 6152 | tf_op jit(solution)/shard_map/ppermute | solution.py:511
  15.3 0.0 collective-permute-start.11
  15.3 1.3 %collective-permute-start.12 = (s32[4,128]{1,0:T(4,128)S(1)}, s32[4,128]{1,0:T(4,128)S(1)}, u32[]{:S(2)}, u32[]{:S(2)}) collective-permute-start(s32[4,128]{1,0:T(4,128)S(1)} %get-tuple-element.179), channel_id=1, source_target_pairs={{4,0},{5,1},{6,2},{7,3},{0,4},{1,5},{2,6},{3,7},{12,8},{13,9},{14,... | collective-permute-start | bytes 6152 | tf_op jit(solution)/shard_map/ppermute | solution.py:511
  16.5 1.4 %collective-permute-done.11 = s32[4,128]{1,0:T(4,128)S(1)} collective-permute-done((s32[4,128]{1,0:T(4,128)S(1)}, s32[4,128]{1,0:T(4,128)S(1)}, u32[]{:S(2)}, u32[]{:S(2)}) %collective-permute-start.11) | collective-permute-done | bytes 2080 | tf_op jit(solution)/shard_map/ppermute | solution.py:511
  18.0 0.0 collective-permute-start.17
  18.0 1.3 %collective-permute-done.12 = s32[4,128]{1,0:T(4,128)S(1)} collective-permute-done((s32[4,128]{1,0:T(4,128)S(1)}, s32[4,128]{1,0:T(4,128)S(1)}, u32[]{:S(2)}, u32[]{:S(2)}) %collective-permute-start.12) | collective-permute-done | bytes 2080 | tf_op jit(solution)/shard_map/ppermute | solution.py:511
  19.3 0.0 collective-permute-done.13
  19.3 0.3 collective-permute-start.14
  19.6 2.5 %collective-permute-done.14 = s32[4,4,128]{2,1,0:T(4,128)S(1)} collective-permute-done((s32[4,4,128]{2,1,0:T(4,128)S(1)}, s32[4,4,128]{2,1,0:T(4,128)S(1)}, u32[]{:S(2)}, u32[]{:S(2)}) %collective-permute-start.14) | collective-permute-done | bytes 8224 | tf_op jit(solution)/shard_map/ppermute | solution.py:511
  22.2 2.5 %collective-permute-start.15 = (s32[2,4,4,128]{3,2,1,0:T(4,128)S(1)}, s32[2,4,4,128]{3,2,1,0:T(4,128)S(1)}, u32[]{:S(2)}, u32[]{:S(2)}) collective-permute-start(s32[2,4,4,128]{3,2,1,0:T(4,128)S(1)} %bitcast_dynamic-update-slice_fusion.4), channel_id=1, source_target_pairs={{16,0},{17,1},{18,2},{19,3},{20,4},{21,5},{22,6},{23,7},{24,8},{25... | collective-permute-start | bytes 49160 | tf_op jit(solution)/shard_map/ppermute | solution.py:511
  24.7 1.6 %collective-permute-done.15 = s32[2,4,4,128]{3,2,1,0:T(4,128)S(1)} collective-permute-done((s32[2,4,4,128]{3,2,1,0:T(4,128)S(1)}, s32[2,4,4,128]{3,2,1,0:T(4,128)S(1)}, u32[]{:S(2)}, u32[]{:S(2)}) %collective-permute-start.15) | collective-permute-done | bytes 16416 | tf_op jit(solution)/shard_map/ppermute | solution.py:511
  26.3 6.1 %collective-permute-start.16 = (s32[2,2,4,4,128]{4,3,2,1,0:T(4,128)S(1)}, s32[2,2,4,4,128]{4,3,2,1,0:T(4,128)S(1)}, u32[]{:S(2)}, u32[]{:S(2)}) collective-permute-start(s32[2,2,4,4,128]{4,3,2,1,0:T(4,128)S(1)} %bitcast_dynamic-update-slice_fusion.2), channel_id=1, source_target_pairs={{1,0},{0,1},{3,2},{2,3},{5,4},{4,5},{7,6},{6,7},{9,8},{8,9},{11,10... | collective-permute-start | bytes 98312 | tf_op jit(solution)/shard_map/ppermute | solution.py:511
  32.5 1.4 %collective-permute-start.18 = (f32[8,128,128]{2,1,0:T(8,128)}, f32[8,128,128]{2,1,0:T(8,128)}, u32[]{:S(2)}, u32[]{:S(2)}) collective-permute-start(f32[8,128,128]{2,1,0:T(8,128)} %get-tuple-element.313.rest_0_), channel_id=1, source_target_pairs={{0,6},{1,7},{2,0},{3,1},{4,2},{5,3},{6,4},{7,5},{8,14},{9,15},{10,... | collective-permute-start | bytes 1572872 | tf_op jit(solution)/shard_map/ppermute | solution.py:453
  33.9 0.0 collective-permute-done.16
  33.9 1.8 %plan.1 = (s32[12]{0:T(128)S(1)}, s32[40,128]{1,0:T(8,128)S(1)}, bf16[6,128,128]{2,1,0:T(8,128)(2,1)S(1)}) custom-call(s32[2]{0:T(128)S(1)} %pad_add_fusion.me_ref, s32[128,128]{1,0:T(8,128)S(1)} %bitcast.36), custom_call_target="tpu_custom_call" | custom-call | tf_op jit(solution)/shard_map/plan/pallas_call | solution.py:157
  35.7 0.0 collective-permute-done.17.refs_0_
  35.7 1.1 %collective-permute-start.19 = (f32[8,128,128]{2,1,0:T(8,128)}, f32[8,128,128]{2,1,0:T(8,128)}, u32[]{:S(2)}, u32[]{:S(2)}) collective-permute-start(f32[8,128,128]{2,1,0:T(8,128)} %hold.2.rest_1_), channel_id=1, source_target_pairs={{0,2},{1,3},{2,4},{3,5},{4,6},{5,7},{6,0},{7,1},{8,10},{9,11},{10,... | collective-permute-start | bytes 1572872 | tf_op jit(solution)/shard_map/ppermute | solution.py:453
  36.8 0.0 collective-permute-done.21.rest_2_.rest_10_
  36.8 0.0 collective-permute-done.20.rest_1_.rest_9_
  36.8 0.0 copy-done.1
  36.8 1.0 %pack.1 = (f32[3,128,128]{2,1,0:T(8,128)S(1)}, f32[3,128,128]{2,1,0:T(8,128)S(1)}, f32[6,128,128]{2,1,0:T(8,128)S(1)}) custom-call(s32[12]{0:T(128)S(1)} %get-tuple-element.184.list_ref, f32[16,128,128]{2,1,0:T(8,128)S(1)} %bitcast.42, f32[16,128,128]{2,1,0:T(8,128)S(1)} %collective-permute-done.20.rest_1_.rest_9_, ...), custom_call_target="tpu_custom_call" | custom-call | tf_op jit(solution)/shard_map/pack/pallas_call | solution.py:190
  37.8 2.3 %collective-permute-start.24 = (f32[6,128,128]{2,1,0:T(8,128)S(1)}, f32[6,128,128]{2,1,0:T(8,128)S(1)}, u32[]{:S(2)}, u32[]{:S(2)}) collective-permute-start(f32[6,128,128]{2,1,0:T(8,128)S(1)} %get-tuple-element.187), channel_id=1, source_target_pairs={{0,16},{16,0},{32,48},{48,32},{64,80},{80,64},{96,112},{112,96},{1... | collective-permute-start | bytes 1179656 | tf_op jit(solution)/shard_map/ppermute | solution.py:441
  40.2 0.2 collective-permute-start.22
  40.4 2.9 %collective-permute-start.23 = (f32[3,128,128]{2,1,0:T(8,128)S(1)}, f32[3,128,128]{2,1,0:T(8,128)S(1)}, u32[]{:S(2)}, u32[]{:S(2)}) collective-permute-start(f32[3,128,128]{2,1,0:T(8,128)S(1)} %get-tuple-element.186), channel_id=1, source_target_pairs={{0,96},{16,112},{32,0},{48,16},{64,32},{80,48},{96,64},{112,80},{1... | collective-permute-start | bytes 589832 | tf_op jit(solution)/shard_map/ppermute | solution.py:441
  43.3 3.0 %overflow.1 = (s32[1]{0:T(128)}, s32[513]{0:T(1024)S(1)}, f32[16,128,128]{2,1,0:T(8,128)}) custom-call(s32[2]{0:T(128)S(1)} %pad_add_fusion.me_ref, s32[40,128]{1,0:T(8,128)S(1)} %get-tuple-element.312.info_ref.refs_1_, s32[128,128]{1,0:T(8,128)S(1)} %bitcast.37, bf16[6,128,128]{2,1,0:T(8,128)(2,1)S(1)} %get-tuple-element.181.maps_ref), custom_call_target="tpu_custom_call" | custom-call | flops 1000000000 | bytes 100000 | tf_op jit(solution)/shard_map/overflow/pallas_call | solution.py:235
  46.3 0.4 collective-permute-done.18.rest_2_
  46.6 1.2 %collective-permute-start.25 = (f32[8,128,128]{2,1,0:T(8,128)}, f32[8,128,128]{2,1,0:T(8,128)}, u32[]{:S(2)}, u32[]{:S(2)}) collective-permute-start(f32[8,128,128]{2,1,0:T(8,128)} %get-tuple-element.313.rest_0_), channel_id=1, source_target_pairs={{0,1},{1,0},{2,3},{3,2},{4,5},{5,4},{6,7},{7,6},{8,9},{9,8},{10,11... | collective-permute-start | bytes 1572872 | tf_op jit(solution)/shard_map/ppermute | solution.py:453
  47.8 7.2 %collective-permute-done.22.refs_1_.rest_13_ = f32[3,128,128]{2,1,0:T(8,128)S(1)} collective-permute-done((f32[3,128,128]{2,1,0:T(8,128)S(1)}, f32[3,128,128]{2,1,0:T(8,128)S(1)}, u32[]{:S(2)}, u32[]{:S(2)}) %collective-permute-start.22) | collective-permute-done | bytes 196640 | tf_op jit(solution)/shard_map/ppermute | solution.py:441
  55.0 1.6 %collective-permute-start.26 = (f32[8,128,128]{2,1,0:T(8,128)}, f32[8,128,128]{2,1,0:T(8,128)}, u32[]{:S(2)}, u32[]{:S(2)}) collective-permute-start(f32[8,128,128]{2,1,0:T(8,128)} %hold.2.rest_1_), channel_id=1, source_target_pairs={{0,1},{1,0},{2,3},{3,2},{4,5},{5,4},{6,7},{7,6},{8,9},{9,8},{10,11... | collective-permute-start | bytes 1572872 | tf_op jit(solution)/shard_map/ppermute | solution.py:453
  56.6 0.0 collective-permute-done.23.refs_2_.rest_12_
  56.6 0.0 collective-permute-start.27
  56.6 0.0 collective-permute-done.19.refs_0_
  56.6 0.0 collective-permute-done.24.refs_3_.rest_11_
  56.6 0.6 hold.3.rest_3_
  57.3 0.6 collective-permute-start.28
  57.9 0.0 collective-permute-done.25.rest_4_
  57.9 1.4 %collective-permute-done.27.rest_6_ = f32[8,128,128]{2,1,0:T(8,128)} collective-permute-done((f32[8,128,128]{2,1,0:T(8,128)}, f32[8,128,128]{2,1,0:T(8,128)}, u32[]{:S(2)}, u32[]{:S(2)}) %collective-permute-start.27) | collective-permute-done | bytes 524320 | tf_op jit(solution)/shard_map/ppermute | solution.py:453
  59.3 0.0 collective-permute-done.26.rest_5_
  59.3 0.7 %collective-permute-done.28.rest_7_ = f32[8,128,128]{2,1,0:T(8,128)} collective-permute-done((f32[8,128,128]{2,1,0:T(8,128)}, f32[8,128,128]{2,1,0:T(8,128)}, u32[]{:S(2)}, u32[]{:S(2)}) %collective-permute-start.28) | collective-permute-done | bytes 524320 | tf_op jit(solution)/shard_map/ppermute | solution.py:453
  60.0 2.7 %products.5 = f32[16,128,128]{2,1,0:T(8,128)} custom-call(s32[513]{0:T(1024)S(1)} %get-tuple-element.182.list_ref, f32[8,128,128]{2,1,0:T(8,128)} %get-tuple-element.313.rest_0_, f32[8,128,128]{2,1,0:T(8,128)} %hold.2.rest_1_, f32[8,128,128]{2,1,0:T(8,128)} %collective-permute-done.18.rest_2_, ...), custom_call_target="tpu_custom_call", output_to_operand_aliasing={{}: (15, {})} | custom-call | flops 100663296 | bytes 1572864 | tf_op jit(solution)/shard_map/products/pallas_call | solution.py:414
  62.7 0.8 %while.12 = (s32[]{:T(128)}, f32[16,128,128]{2,1,0:T(8,128)}, s32[]{:T(128)}, f32[16,128,128]{2,1,0:T(8,128)}, s32[2]{0:T(128)S(1)}, /*index=5*/s32[40,128]{1,0:...) while((s32[]{:T(128)}, f32[16,128,128]{2,1,0:T(8,128)}, ...), condition=%wide.region_1.2_spmd, body=%wide.region_0.1_spmd.sunk | while | flops 100925440 | bytes 33030584 | solution.py:575
  (22 shorter events, 0.3 us)
Async XLA Ops:
  0.0 10.5 %copy-start = (f32[1,1,4,128,128]{4,3,2,1,0:T(8,128)S(1)}, f32[1,1,4,128,128]{4,3,2,1,0:T(8,128)}, u32[]{:S(2)}) copy-start(f32[1,1,4,128,128]{4,3,2,1,0:T(8,128)} %param.7) | copy-start | bytes 786436
  0.0 10.5 %collective-permute-start.7 = (f32[4,128,128]{2,1,0:T(8,128)}, f32[4,128,128]{2,1,0:T(8,128)S(1)}, u32[]{:S(2)}, u32[]{:S(2)}) collective-permute-start(f32[4,128,128]{2,1,0:T(8,128)} %bitcast.34), channel_id=1, source_target_pairs={{0,8},{1,9},{2,10},{3,11},{4,12},{5,13},{6,14},{7,15},{8,0},{9,1},... | collective-permute-start | bytes 786440 | tf_op jit(solution)/shard_map/ppermute | solution.py:453
  3.6 6.3 %collective-permute-start.9 = (s32[128]{0:T(128)S(1)}, s32[128]{0:T(128)S(1)}, u32[]{:S(2)}, u32[]{:S(2)}) collective-permute-start(s32[128]{0:T(128)S(1)} %get-tuple-element.219), channel_id=1, source_target_pairs={{64,0},{65,1},{66,2},{67,3},{68,4},{69,5},{70,6},{71,7},{72,8},{73... | collective-permute-start | bytes 1544 | tf_op jit(solution)/shard_map/ppermute | solution.py:511
  6.5 3.2 %collective-permute-start.8 = (s32[128]{0:T(128)S(1)}, s32[128]{0:T(128)S(1)}, u32[]{:S(2)}, u32[]{:S(2)}) collective-permute-start(s32[128]{0:T(128)S(1)} %get-tuple-element.219), channel_id=1, source_target_pairs={{32,0},{33,1},{34,2},{35,3},{36,4},{37,5},{38,6},{39,7},{40,8},{41... | collective-permute-start | bytes 1544 | tf_op jit(solution)/shard_map/ppermute | solution.py:511
  6.9 3.6 %collective-permute-start.10 = (s32[128]{0:T(128)S(1)}, s32[128]{0:T(128)S(1)}, u32[]{:S(2)}, u32[]{:S(2)}) collective-permute-start(s32[128]{0:T(128)S(1)} %get-tuple-element.219), channel_id=1, source_target_pairs={{96,0},{97,1},{98,2},{99,3},{100,4},{101,5},{102,6},{103,7},{104,8... | collective-permute-start | bytes 1544 | tf_op jit(solution)/shard_map/ppermute | solution.py:511
  7.4 29.4 %collective-permute-start.21 = (f32[16,128,128]{2,1,0:T(8,128)}, f32[16,128,128]{2,1,0:T(8,128)S(1)}, u32[]{:S(2)}, u32[]{:S(2)}) collective-permute-start(f32[16,128,128]{2,1,0:T(8,128)} %bitcast.38), channel_id=1, source_target_pairs={{0,96},{16,112},{32,0},{48,16},{64,32},{80,48},{96,64},{112,80},{1... | collective-permute-start | bytes 3145736 | tf_op jit(solution)/shard_map/ppermute | solution.py:441
  9.8 27.1 %collective-permute-start.20 = (f32[16,128,128]{2,1,0:T(8,128)}, f32[16,128,128]{2,1,0:T(8,128)S(1)}, u32[]{:S(2)}, u32[]{:S(2)}) collective-permute-start(f32[16,128,128]{2,1,0:T(8,128)} %bitcast.39), channel_id=1, source_target_pairs={{0,32},{16,48},{32,64},{48,80},{64,96},{80,112},{96,0},{112,16},{1... | collective-permute-start | bytes 3145736 | tf_op jit(solution)/shard_map/ppermute | solution.py:441
  10.5 26.3 %copy-start.1 = (f32[1,1,2,8,128,128]{5,4,3,2,1,0:T(8,128)S(1)}, f32[1,1,2,8,128,128]{5,4,3,2,1,0:T(8,128)}, u32[]{:S(2)}) copy-start(f32[1,1,2,8,128,128]{5,4,3,2,1,0:T(8,128)} %param.9) | copy-start | bytes 3145732
  11.4 7.9 %collective-permute-start.13 = (s32[4,128]{1,0:T(4,128)S(1)}, s32[4,128]{1,0:T(4,128)S(1)}, u32[]{:S(2)}, u32[]{:S(2)}) collective-permute-start(s32[4,128]{1,0:T(4,128)S(1)} %get-tuple-element.179), channel_id=1, source_target_pairs={{6,0},{7,1},{4,2},{5,3},{2,4},{3,5},{0,6},{1,7},{14,8},{15,9},{12,... | collective-permute-start | bytes 6152 | tf_op jit(solution)/shard_map/ppermute | solution.py:511
  15.3 2.7 %collective-permute-start.11 = (s32[4,128]{1,0:T(4,128)S(1)}, s32[4,128]{1,0:T(4,128)S(1)}, u32[]{:S(2)}, u32[]{:S(2)}) collective-permute-start(s32[4,128]{1,0:T(4,128)S(1)} %get-tuple-element.179), channel_id=1, source_target_pairs={{2,0},{3,1},{0,2},{1,3},{6,4},{7,5},{4,6},{5,7},{10,8},{11,9},{8,1... | collective-permute-start | bytes 6152 | tf_op jit(solution)/shard_map/ppermute | solution.py:511
  15.3 4.0 %collective-permute-start.12 = (s32[4,128]{1,0:T(4,128)S(1)}, s32[4,128]{1,0:T(4,128)S(1)}, u32[]{:S(2)}, u32[]{:S(2)}) collective-permute-start(s32[4,128]{1,0:T(4,128)S(1)} %get-tuple-element.179), channel_id=1, source_target_pairs={{4,0},{5,1},{6,2},{7,3},{0,4},{1,5},{2,6},{3,7},{12,8},{13,9},{14,... | collective-permute-start | bytes 6152 | tf_op jit(solution)/shard_map/ppermute | solution.py:511
  18.0 17.7 %collective-permute-start.17 = (f32[8,128,128]{2,1,0:T(8,128)}, f32[8,128,128]{2,1,0:T(8,128)}, u32[]{:S(2)}, u32[]{:S(2)}) collective-permute-start(f32[8,128,128]{2,1,0:T(8,128)} %get-tuple-element.313.rest_0_), channel_id=1, source_target_pairs={{0,2},{1,3},{2,4},{3,5},{4,6},{5,7},{6,0},{7,1},{8,10},{9,11},{10,... | collective-permute-start | bytes 1572872 | tf_op jit(solution)/shard_map/ppermute | solution.py:453
  19.3 2.9 %collective-permute-start.14 = (s32[4,4,128]{2,1,0:T(4,128)S(1)}, s32[4,4,128]{2,1,0:T(4,128)S(1)}, u32[]{:S(2)}, u32[]{:S(2)}) collective-permute-start(s32[4,4,128]{2,1,0:T(4,128)S(1)} %constant_dynamic-update-slice_fusion), channel_id=1, source_target_pairs={{8,0},{9,1},{10,2},{11,3},{12,4},{13,5},{14,6},{15,7},{0,8},{1,9},... | collective-permute-start | bytes 24584 | tf_op jit(solution)/shard_map/ppermute | solution.py:511
  22.2 4.1 %collective-permute-start.15 = (s32[2,4,4,128]{3,2,1,0:T(4,128)S(1)}, s32[2,4,4,128]{3,2,1,0:T(4,128)S(1)}, u32[]{:S(2)}, u32[]{:S(2)}) collective-permute-start(s32[2,4,4,128]{3,2,1,0:T(4,128)S(1)} %bitcast_dynamic-update-slice_fusion.4), channel_id=1, source_target_pairs={{16,0},{17,1},{18,2},{19,3},{20,4},{21,5},{22,6},{23,7},{24,8},{25... | collective-permute-start | bytes 49160 | tf_op jit(solution)/shard_map/ppermute | solution.py:511
  26.3 7.6 %collective-permute-start.16 = (s32[2,2,4,4,128]{4,3,2,1,0:T(4,128)S(1)}, s32[2,2,4,4,128]{4,3,2,1,0:T(4,128)S(1)}, u32[]{:S(2)}, u32[]{:S(2)}) collective-permute-start(s32[2,2,4,4,128]{4,3,2,1,0:T(4,128)S(1)} %bitcast_dynamic-update-slice_fusion.2), channel_id=1, source_target_pairs={{1,0},{0,1},{3,2},{2,3},{5,4},{4,5},{7,6},{6,7},{9,8},{8,9},{11,10... | collective-permute-start | bytes 98312 | tf_op jit(solution)/shard_map/ppermute | solution.py:511
  32.5 14.2 %collective-permute-start.18 = (f32[8,128,128]{2,1,0:T(8,128)}, f32[8,128,128]{2,1,0:T(8,128)}, u32[]{:S(2)}, u32[]{:S(2)}) collective-permute-start(f32[8,128,128]{2,1,0:T(8,128)} %get-tuple-element.313.rest_0_), channel_id=1, source_target_pairs={{0,6},{1,7},{2,0},{3,1},{4,2},{5,3},{6,4},{7,5},{8,14},{9,15},{10,... | collective-permute-start | bytes 1572872 | tf_op jit(solution)/shard_map/ppermute | solution.py:453
  35.7 20.9 %collective-permute-start.19 = (f32[8,128,128]{2,1,0:T(8,128)}, f32[8,128,128]{2,1,0:T(8,128)}, u32[]{:S(2)}, u32[]{:S(2)}) collective-permute-start(f32[8,128,128]{2,1,0:T(8,128)} %hold.2.rest_1_), channel_id=1, source_target_pairs={{0,2},{1,3},{2,4},{3,5},{4,6},{5,7},{6,0},{7,1},{8,10},{9,11},{10,... | collective-permute-start | bytes 1572872 | tf_op jit(solution)/shard_map/ppermute | solution.py:453
  37.8 18.8 %collective-permute-start.24 = (f32[6,128,128]{2,1,0:T(8,128)S(1)}, f32[6,128,128]{2,1,0:T(8,128)S(1)}, u32[]{:S(2)}, u32[]{:S(2)}) collective-permute-start(f32[6,128,128]{2,1,0:T(8,128)S(1)} %get-tuple-element.187), channel_id=1, source_target_pairs={{0,16},{16,0},{32,48},{48,32},{64,80},{80,64},{96,112},{112,96},{1... | collective-permute-start | bytes 1179656 | tf_op jit(solution)/shard_map/ppermute | solution.py:441
  40.2 14.8 %collective-permute-start.22 = (f32[3,128,128]{2,1,0:T(8,128)S(1)}, f32[3,128,128]{2,1,0:T(8,128)S(1)}, u32[]{:S(2)}, u32[]{:S(2)}) collective-permute-start(f32[3,128,128]{2,1,0:T(8,128)S(1)} %get-tuple-element.185), channel_id=1, source_target_pairs={{0,48},{16,32},{32,80},{48,64},{64,112},{80,96},{96,16},{112,0},{1... | collective-permute-start | bytes 589832 | tf_op jit(solution)/shard_map/ppermute | solution.py:441
  40.4 16.2 %collective-permute-start.23 = (f32[3,128,128]{2,1,0:T(8,128)S(1)}, f32[3,128,128]{2,1,0:T(8,128)S(1)}, u32[]{:S(2)}, u32[]{:S(2)}) collective-permute-start(f32[3,128,128]{2,1,0:T(8,128)S(1)} %get-tuple-element.186), channel_id=1, source_target_pairs={{0,96},{16,112},{32,0},{48,16},{64,32},{80,48},{96,64},{112,80},{1... | collective-permute-start | bytes 589832 | tf_op jit(solution)/shard_map/ppermute | solution.py:441
  46.6 11.2 %collective-permute-start.25 = (f32[8,128,128]{2,1,0:T(8,128)}, f32[8,128,128]{2,1,0:T(8,128)}, u32[]{:S(2)}, u32[]{:S(2)}) collective-permute-start(f32[8,128,128]{2,1,0:T(8,128)} %get-tuple-element.313.rest_0_), channel_id=1, source_target_pairs={{0,1},{1,0},{2,3},{3,2},{4,5},{5,4},{6,7},{7,6},{8,9},{9,8},{10,11... | collective-permute-start | bytes 1572872 | tf_op jit(solution)/shard_map/ppermute | solution.py:453
  55.0 4.2 %collective-permute-start.26 = (f32[8,128,128]{2,1,0:T(8,128)}, f32[8,128,128]{2,1,0:T(8,128)}, u32[]{:S(2)}, u32[]{:S(2)}) collective-permute-start(f32[8,128,128]{2,1,0:T(8,128)} %hold.2.rest_1_), channel_id=1, source_target_pairs={{0,1},{1,0},{2,3},{3,2},{4,5},{5,4},{6,7},{7,6},{8,9},{9,8},{10,11... | collective-permute-start | bytes 1572872 | tf_op jit(solution)/shard_map/ppermute | solution.py:453
  56.6 2.6 %collective-permute-start.27 = (f32[8,128,128]{2,1,0:T(8,128)}, f32[8,128,128]{2,1,0:T(8,128)}, u32[]{:S(2)}, u32[]{:S(2)}) collective-permute-start(f32[8,128,128]{2,1,0:T(8,128)} %collective-permute-done.18.rest_2_), channel_id=1, source_target_pairs={{0,1},{1,0},{2,3},{3,2},{4,5},{5,4},{6,7},{7,6},{8,9},{9,8},{10,11... | collective-permute-start | bytes 1572872 | tf_op jit(solution)/shard_map/ppermute | solution.py:453
  57.3 2.7 %collective-permute-start.28 = (f32[8,128,128]{2,1,0:T(8,128)}, f32[8,128,128]{2,1,0:T(8,128)}, u32[]{:S(2)}, u32[]{:S(2)}) collective-permute-start(f32[8,128,128]{2,1,0:T(8,128)} %hold.3.rest_3_), channel_id=1, source_target_pairs={{0,1},{1,0},{2,3},{3,2},{4,5},{5,4},{6,7},{7,6},{8,9},{9,8},{10,11... | collective-permute-start | bytes 1572872 | tf_op jit(solution)/shard_map/ppermute | solution.py:453

commit v4 on v3

--- a/solution.py
+++ b/solution.py
@@ -114,6 +114,36 @@
     )
 
 
+def list_sends(sends, row, order, turn, pack_list):
+    r, p, owner, _ = lane_facts(order.shape)
+    t = lax.broadcasted_iota(jnp.int32, order.shape, 0)
+    steps = ((owner >> 1) - (row >> 1)) & 3
+    part = jnp.where(steps == 0, 0, jnp.where(steps == 3, 1, 2))
+    word = (part * 16 + (p & 1) * 8 + t).astype(jnp.float32)
+    n = 0
+    for slots, which, there in sends:
+        for e in range(slots):
+            hit = (order == which * 128 + turn * slots + e) & (r == there(row))
+            pack_list[n] = jnp.max(jnp.where(hit, word, -1.0)).astype(jnp.int32)
+            n += 1
+
+
+def relist_kernel(sends, me_ref, turn_ref, info_ref, pack_list):
+    list_sends(sends, me_ref[0], info_ref[32:40], turn_ref[0], pack_list)
+
+
+def relist(me, turn, info, sends):
+    smem = pl.BlockSpec(memory_space=pltpu.SMEM)
+    return pl.pallas_call(
+        functools.partial(relist_kernel, sends),
+        in_specs=[smem, smem, pl.BlockSpec(memory_space=pltpu.VMEM)],
+        out_specs=smem,
+        out_shape=jax.ShapeDtypeStruct((sum(n for n, *_ in sends),), jnp.int32),
+        compiler_params=pltpu.CompilerParams(vmem_limit_bytes=4 << 20),
+        name="relist",
+    )(me, turn, info)
+
+
 def plan_kernel(sends, me_ref, spots_ref, pack_list, info_ref, maps_ref):
     row, column = me_ref[0], me_ref[1]
     make_maps(maps_ref)
@@ -135,16 +165,7 @@
     rank = (upto - alike + matmul(flags, maps_ref[4])).astype(jnp.int32)
     order = jnp.where(need, way * 128 + rank, -1)
 
-    steps = ((owner >> 1) - (row >> 1)) & 3
-    part = jnp.where(steps == 0, 0, jnp.where(steps == 3, 1, 2))
-    word = (part * 16 + (p & 1) * 8 + t).astype(jnp.float32)
-    n = 0
-    for slots, which, there in sends:
-        for e in range(slots):
-            hit = (order == which * 128 + e) & (r == there(row))
-            pack_list[n] = jnp.max(jnp.where(hit, word, -1.0)).astype(jnp.int32)
-            n += 1
-
+    list_sends(sends, row, order, 0, pack_list)
     info_ref[0:8] = a
     info_ref[8:16] = b
     info_ref[16:32] = c
@@ -224,7 +245,9 @@
         most = jnp.maximum(most, jnp.sum(alike[q * 8 : q * 8 + 8], axis=0, keepdims=True))
     *_, way = lane_facts(most.shape)
     slots = jnp.where(way == 0, 128, jnp.where(way == 1, NEAR, FAR))
-    over_ref[0] = jnp.max(jnp.where(most > slots.astype(jnp.float32), 1.0, 0.0)).astype(jnp.int32)
+    slots = slots.astype(jnp.float32)
+    turns = sum(jnp.where(most > k * slots, 1.0, 0.0) for k in range(1, 17))
+    over_ref[0] = jnp.max(turns).astype(jnp.int32)
     for store in stores:
         store.wait()
 
@@ -273,7 +296,7 @@
     list_ref[LIST] = n
 
 
-def entries_of(info_ref, me_ref):
+def entries_of(info_ref, me_ref, turn=1):
     row, column = me_ref[0], me_ref[1]
     b, c, order = info_ref[8:16], info_ref[16:32], info_ref[32:40]
     r, p, owner, way = lane_facts(b.shape)
@@ -281,7 +304,10 @@
     rank = order & 127
     steps = ((owner >> 1) - (row >> 1)) & 3
     part = jnp.where(steps == 0, 0, jnp.where(steps == 3, 1, 2))
-    sent = (way > 0) & (rank < jnp.where(way == 1, NEAR, FAR))
+    slots = jnp.where(way == 1, NEAR, FAR)
+    sent = (way > 0) & (rank < slots)
+    at = rank - turn * slots
+    later = (way > 0) & (at >= 0) & (at < slots)
     along = ((p >> 1) - (column >> 1)) & 3
     beside = ((p ^ column) >> 3) & 1
     a_part = jnp.where(along == 0, 0, jnp.where(along == 3, 1, jnp.where(along == 1, 2, 3)))
@@ -299,9 +325,9 @@
             code(a_slot, part, (p & 1) * 8 + t, c_slot),
             code(a_slot, 2 + way, rank, c_slot),
         )
-        elsewhere = code(a_slot, owner ^ row, (p & 1) * 8 + t, c_slot)
+        in_turn = code(a_slot, (way - 1) & 3, at, c_slot)
         found[0].append(jnp.where(live & ((way == 0) | sent), at_hand, -1).astype(jnp.float32))
-        found[1].append(jnp.where(live & (way > 0) & ~sent, elsewhere, -1).astype(jnp.float32))
+        found[1].append(jnp.where(live & later, in_turn, -1).astype(jnp.float32))
     return [jnp.concatenate(x) for x in found]
 
 
@@ -397,10 +423,10 @@
     touched(3, lambda c: stored(c).wait())
 
 
-def rest_kernel(parts, me_ref, info_ref, *rest):
+def rest_kernel(parts, me_ref, turn_ref, info_ref, *rest):
     a_refs, b_refs = rest[:A_PARTS], rest[A_PARTS:parts]
     total_ref, out_ref, rest_list, *buffers = rest[parts:]
-    extract(entries_of(info_ref, me_ref)[1], rest_list)
+    extract(entries_of(info_ref, me_ref, turn_ref[0])[1], rest_list)
     add_listed(rest_list, a_refs, b_refs, total_ref, out_ref, *buffers)
 
 
@@ -532,9 +558,9 @@
     blank = jnp.full((8 - sa,), -1, jnp.int32)
     mine = jnp.concatenate([a_index[0, 0], blank, b_index[0, 0].reshape(-1), c_index[0, 0]])
     spots = among(jnp.pad(mine, (0, 128 - mine.shape[0])), (5, 6), rows, columns)
+    spots = among(spots, (1, 2), rows, columns)
     tile = a_blocks[0, 0]
     pair, spots = paired(tile, moved(tile, lambda i: i ^ 8, columns), spots)
-    spots = among(spots, (1, 2), rows, columns)
     spots = among(spots, (3,), rows, columns)
     spots = among(spots, (4,), rows, columns)
     spots = among(spots, (0,), rows, columns).reshape(rows * columns, 128)
@@ -563,16 +589,21 @@
     b_parts = near + [cross, far_own, far_other]
     total = products(all_kernel, [product_list], a_parts, b_parts, zeros, sc)
 
-    trips = over[0]
-
-    def trip(state):
-        done, total = state
-        sent = jnp.where(done >= 0, own, 0)
-        whole = [own] + [to_row(sent, rows, lambda i, n=n: i ^ n) for n in range(1, rows)]
-        rest = products(rest_kernel, [me, info], a_parts, whole, total, sc, own_list=True)
-        return done + 1, rest
-
-    _, total = lax.while_loop(lambda state: state[0] < trips, trip, (jnp.int32(0), total))
+    turns = over[0]
+
+    def again(state):
+        turn, total = state
+        listing = relist(me, turn[None], info, sends)
+        packed = pack(listing, near, [n for n, *_ in sends])
+        far_other, far_own, cross = [
+            to_row(block, rows, there) for block, (*_, there) in zip(packed, sends)
+        ]
+        blocks = [cross, far_own, far_other]
+        leading = [me, turn[None], info]
+        total = products(rest_kernel, leading, a_parts, blocks, total, sc, own_list=True)
+        return turn + 1, total
+
+    _, total = lax.while_loop(lambda state: state[0] <= turns, again, (jnp.int32(1), total))
     return total[None, None]
 
 

time: 64.8 us -> 63.5 us (0.980); the launches traced: 63.7 us -> 63.7 us
  Pallas kernels: 9.98 us -> 11.5 us
  waiting for transfers between devices: 17.2 us -> 15.8 us
    ppermute x8, starting transfers between devices: 7.93 us -> 5.53 us  [moved(): return lax.ppermute(block, COL, [(i, there(i)) for i in range(columns)])]
    ppermute x9, starting transfers between devices: 17.8 us -> 20.1 us  [among(): got = lax.ppermute(held, ('row', *COL), pairs)]
    ppermute x9, waiting for transfers between devices: 7.51 us -> 6.25 us  [among(): got = lax.ppermute(held, ('row', *COL), pairs)]
  transfers between devices with their start and end apart: 22 -> 22, of which waited for: 9 -> 7; matrix products, arithmetic and copies ran while one was open for 3% -> 0% of each run, Pallas kernels for 11% -> 13%
where the time goes in v4:
time: 63.5 us; the launch traced here: 63.7 us
  starting transfers between devices  33.8 us (53%)
  waiting for transfers between devices  15.8 us (25%)
  Pallas kernels  11.5 us (18%)
  local copies, waits for them, and re-layouts  1.06 us (2%)
  other arithmetic  0.82 us (1%)
    ppermute x9, starting transfers between devices, among(): got = lax.ppermute(held, ('row', *COL), pairs)  20.1 us
    ppermute x5, starting transfers between devices, to_row(): return lax.ppermute(block, 'row', [(i, there(i)) for i in range(rows)])  8.2 us
    ppermute x5, waiting for transfers between devices, to_row(): return lax.ppermute(block, 'row', [(i, there(i)) for i in range(rows)])  7.33 us
    ppermute x9, waiting for transfers between devices, among(): got = lax.ppermute(held, ('row', *COL), pairs)  6.25 us
    ppermute x8, starting transfers between devices, moved(): return lax.ppermute(block, COL, [(i, there(i)) for i in range(columns)])  5.53 us
    pallas_call x1, Pallas kernels, overflow(): pl.pallas_call(overflow_kernel, in_specs=[smem, vmem, vmem, vmem], out_sp...  3.35 us
    pallas_call x1, Pallas kernels, products(): pl.pallas_call(functools.partial(kernel, parts), in_specs=[smem if x.ndim...  3.3 us
    ppermute x8, waiting for transfers between devices, moved(): return lax.ppermute(block, COL, [(i, there(i)) for i in range(columns)])  2.21 us
  transfers between devices with their start and end apart: 22, of which 7 were waited for; matrix products, arithmetic and copies ran while one was open for 0% of the time, Pallas kernels for 13%

profile of v4, /device:TPU:1, one launch (start us, length us, event | category | flops | bytes accessed | tf_op | source)
XLA Modules:
  0.0 63.7 jit_solution(14989474539944732190)
XLA Ops:
  0.0 0.0 copy-start
  0.0 0.8 %reshape_squeeze.6 = s32[16]{0:T(128)S(1)} reshape(s32[1,1,2,8]{3,2,1,0:T(2,128)} %param.10) | data formatting | bytes 128 | tf_op jit(solution)/shard_map/reshape;squeeze | solution.py:559
  0.8 0.7 %pad_add_fusion.1 = s32[40]{0:T(128)S(1)} fusion(s32[16]{0:T(128)} %bitcast.46, s32[16]{0:T(128)S(1)} %reshape_squeeze.6, s32[4]{0:T(128)S(1)} %broadcast.5, s32[4]{0:T(128)} %bitcast.47), kind=kLoop, calls=%fused_computation.11 | loop fusion | flops 120 | bytes 320 | tf_op jit(solution)/shard_map/concatenate | solution.py:559
  1.6 2.2 %collective-permute-start.4 = (s32[128]{0:T(128)S(1)}, s32[128]{0:T(128)S(1)}, u32[]{:S(2)}, u32[]{:S(2)}) collective-permute-start(s32[128]{0:T(128)S(1)} %get-tuple-element.146), channel_id=1, source_target_pairs={{32,0},{33,1},{34,2},{35,3},{36,4},{37,5},{38,6},{39,7},{40,8},{41... | collective-permute-start | bytes 1544 | tf_op jit(solution)/shard_map/ppermute | solution.py:537
  3.7 2.6 %collective-permute-start.5 = (s32[128]{0:T(128)S(1)}, s32[128]{0:T(128)S(1)}, u32[]{:S(2)}, u32[]{:S(2)}) collective-permute-start(s32[128]{0:T(128)S(1)} %get-tuple-element.146), channel_id=1, source_target_pairs={{64,0},{65,1},{66,2},{67,3},{68,4},{69,5},{70,6},{71,7},{72,8},{73... | collective-permute-start | bytes 1544 | tf_op jit(solution)/shard_map/ppermute | solution.py:537
  6.3 0.0 collective-permute-start.6
  6.3 0.0 collective-permute-start.16
  6.4 0.0 copy-start.1
  6.4 0.1 pad_add_fusion.me_ref
  6.5 2.7 %collective-permute-start.17 = (f32[16,128,128]{2,1,0:T(8,128)}, f32[16,128,128]{2,1,0:T(8,128)}, u32[]{:S(2)}, u32[]{:S(2)}) collective-permute-start(f32[16,128,128]{2,1,0:T(8,128)} %bitcast.42), channel_id=1, source_target_pairs={{0,96},{16,112},{32,0},{48,16},{64,32},{80,48},{96,64},{112,80},{1... | collective-permute-start | bytes 3145736 | tf_op jit(solution)/shard_map/ppermute | solution.py:467
  9.2 0.0 collective-permute-done.4
  9.3 0.0 copy-done
  9.3 1.3 %collective-permute-start.3 = (f32[4,128,128]{2,1,0:T(8,128)S(1)}, f32[4,128,128]{2,1,0:T(8,128)S(1)}, u32[]{:S(2)}, u32[]{:S(2)}) collective-permute-start(f32[4,128,128]{2,1,0:T(8,128)S(1)} %bitcast.37), channel_id=1, source_target_pairs={{0,8},{1,9},{2,10},{3,11},{4,12},{5,13},{6,14},{7,15},{8,0},{9,1},... | collective-permute-start | bytes 786440 | tf_op jit(solution)/shard_map/ppermute | solution.py:479
  10.5 0.0 collective-permute-done.5
  10.6 0.0 collective-permute-done.6
  10.6 1.7 %collective-permute-start.7 = (s32[4,128]{1,0:T(4,128)S(1)}, s32[4,128]{1,0:T(4,128)S(1)}, u32[]{:S(2)}, u32[]{:S(2)}) collective-permute-start(s32[4,128]{1,0:T(4,128)S(1)} %dynamic_update_slice.50), channel_id=1, source_target_pairs={{2,0},{3,1},{0,2},{1,3},{6,4},{7,5},{4,6},{5,7},{10,8},{11,9},{8,1... | collective-permute-start | bytes 6152 | tf_op jit(solution)/shard_map/ppermute | solution.py:537
  12.3 3.3 %collective-permute-start.8 = (s32[4,128]{1,0:T(4,128)S(1)}, s32[4,128]{1,0:T(4,128)S(1)}, u32[]{:S(2)}, u32[]{:S(2)}) collective-permute-start(s32[4,128]{1,0:T(4,128)S(1)} %dynamic_update_slice.50), channel_id=1, source_target_pairs={{4,0},{5,1},{6,2},{7,3},{0,4},{1,5},{2,6},{3,7},{12,8},{13,9},{14,... | collective-permute-start | bytes 6152 | tf_op jit(solution)/shard_map/ppermute | solution.py:537
  15.6 0.0 collective-permute-done.7
  15.6 1.6 %collective-permute-start.9 = (s32[4,128]{1,0:T(4,128)S(1)}, s32[4,128]{1,0:T(4,128)S(1)}, u32[]{:S(2)}, u32[]{:S(2)}) collective-permute-start(s32[4,128]{1,0:T(4,128)S(1)} %dynamic_update_slice.50), channel_id=1, source_target_pairs={{6,0},{7,1},{4,2},{5,3},{2,4},{3,5},{0,6},{1,7},{14,8},{15,9},{12,... | collective-permute-start | bytes 6152 | tf_op jit(solution)/shard_map/ppermute | solution.py:537
  17.3 0.0 collective-permute-done.8
  17.3 2.3 %collective-permute-done.9 = s32[4,128]{1,0:T(4,128)S(1)} collective-permute-done((s32[4,128]{1,0:T(4,128)S(1)}, s32[4,128]{1,0:T(4,128)S(1)}, u32[]{:S(2)}, u32[]{:S(2)}) %collective-permute-start.9) | collective-permute-done | bytes 2080 | tf_op jit(solution)/shard_map/ppermute | solution.py:537
  19.6 0.0 collective-permute-done.3.beside_ref
  19.6 0.9 %pair.1 = (f32[8,128,128]{2,1,0:T(8,128)}, s32[4,4,128]{2,1,0:T(4,128)S(1)}) custom-call(f32[4,128,128]{2,1,0:T(8,128)S(1)} %bitcast.38, f32[4,128,128]{2,1,0:T(8,128)S(1)} %collective-permute-done.3.beside_ref, s32[4,4,128]{2,1,0:T(4,128)S(1)} %constant_dynamic-update-slice_fusion._), custom_call_target="tpu_custom_call", output_to_operand_aliasing={{1}: (2, {})} | custom-call | tf_op jit(solution)/shard_map/pair/pallas_call | solution.py:497
  20.5 0.7 %collective-permute-start.10 = (s32[4,4,128]{2,1,0:T(4,128)S(1)}, s32[4,4,128]{2,1,0:T(4,128)S(1)}, u32[]{:S(2)}, u32[]{:S(2)}) collective-permute-start(s32[4,4,128]{2,1,0:T(4,128)S(1)} %get-tuple-element.102), channel_id=1, source_target_pairs={{8,0},{9,1},{10,2},{11,3},{12,4},{13,5},{14,6},{15,7},{0,8},{1,9},... | collective-permute-start | bytes 24584 | tf_op jit(solution)/shard_map/ppermute | solution.py:537
  21.1 0.0 collective-permute-start.13
  21.1 2.3 %collective-permute-done.10 = s32[4,4,128]{2,1,0:T(4,128)S(1)} collective-permute-done((s32[4,4,128]{2,1,0:T(4,128)S(1)}, s32[4,4,128]{2,1,0:T(4,128)S(1)}, u32[]{:S(2)}, u32[]{:S(2)}) %collective-permute-start.10) | collective-permute-done | bytes 8224 | tf_op jit(solution)/shard_map/ppermute | solution.py:537
  23.5 2.5 %collective-permute-start.11 = (s32[2,4,4,128]{3,2,1,0:T(4,128)S(1)}, s32[2,4,4,128]{3,2,1,0:T(4,128)S(1)}, u32[]{:S(2)}, u32[]{:S(2)}) collective-permute-start(s32[2,4,4,128]{3,2,1,0:T(4,128)S(1)} %bitcast_dynamic-update-slice_fusion.4), channel_id=1, source_target_pairs={{16,0},{17,1},{18,2},{19,3},{20,4},{21,5},{22,6},{23,7},{24,8},{25... | collective-permute-start | bytes 49160 | tf_op jit(solution)/shard_map/ppermute | solution.py:537
  25.9 1.6 %collective-permute-done.11 = s32[2,4,4,128]{3,2,1,0:T(4,128)S(1)} collective-permute-done((s32[2,4,4,128]{3,2,1,0:T(4,128)S(1)}, s32[2,4,4,128]{3,2,1,0:T(4,128)S(1)}, u32[]{:S(2)}, u32[]{:S(2)}) %collective-permute-start.11) | collective-permute-done | bytes 16416 | tf_op jit(solution)/shard_map/ppermute | solution.py:537
  27.6 5.6 %collective-permute-start.12 = (s32[2,2,4,4,128]{4,3,2,1,0:T(4,128)S(1)}, s32[2,2,4,4,128]{4,3,2,1,0:T(4,128)S(1)}, u32[]{:S(2)}, u32[]{:S(2)}) collective-permute-start(s32[2,2,4,4,128]{4,3,2,1,0:T(4,128)S(1)} %bitcast_dynamic-update-slice_fusion.2), channel_id=1, source_target_pairs={{1,0},{0,1},{3,2},{2,3},{5,4},{4,5},{7,6},{6,7},{9,8},{8,9},{11,10... | collective-permute-start | bytes 98312 | tf_op jit(solution)/shard_map/ppermute | solution.py:537
  33.2 1.9 %collective-permute-start.14 = (f32[8,128,128]{2,1,0:T(8,128)}, f32[8,128,128]{2,1,0:T(8,128)}, u32[]{:S(2)}, u32[]{:S(2)}) collective-permute-start(f32[8,128,128]{2,1,0:T(8,128)} %get-tuple-element.260.rest_0_), channel_id=1, source_target_pairs={{0,6},{1,7},{2,0},{3,1},{4,2},{5,3},{6,4},{7,5},{8,14},{9,15},{10,... | collective-permute-start | bytes 1572872 | tf_op jit(solution)/shard_map/ppermute | solution.py:479
  35.1 0.0 collective-permute-done.12
  35.1 1.8 %plan.1 = (s32[12]{0:T(128)S(1)}, s32[40,128]{1,0:T(8,128)S(1)}, bf16[6,128,128]{2,1,0:T(8,128)(2,1)S(1)}) custom-call(s32[2]{0:T(128)S(1)} %pad_add_fusion.me_ref, s32[128,128]{1,0:T(8,128)S(1)} %bitcast.39), custom_call_target="tpu_custom_call" | custom-call | tf_op jit(solution)/shard_map/plan/pallas_call | solution.py:178
  36.9 0.0 collective-permute-done.13.refs_0_
  36.9 0.1 collective-permute-start.15
  37.0 0.0 collective-permute-done.16.rest_1_.rest_9_
  37.0 0.0 collective-permute-done.17.rest_2_.rest_10_
  37.0 0.0 copy-done.1
  37.0 1.6 %pack.2 = (f32[3,128,128]{2,1,0:T(8,128)S(1)}, f32[3,128,128]{2,1,0:T(8,128)S(1)}, f32[6,128,128]{2,1,0:T(8,128)S(1)}) custom-call(s32[12]{0:T(128)S(1)} %get-tuple-element.107.list_ref, f32[16,128,128]{2,1,0:T(8,128)S(1)} %bitcast.43, f32[16,128,128]{2,1,0:T(8,128)S(1)} %collective-permute-done.16.rest_1_.rest_9_, ...), custom_call_target="tpu_custom_call" | custom-call | tf_op jit(solution)/shard_map/pack/pallas_call | solution.py:211
  38.6 2.0 %collective-permute-start.20 = (f32[6,128,128]{2,1,0:T(8,128)S(1)}, f32[6,128,128]{2,1,0:T(8,128)S(1)}, u32[]{:S(2)}, u32[]{:S(2)}) collective-permute-start(f32[6,128,128]{2,1,0:T(8,128)S(1)} %get-tuple-element.110), channel_id=1, source_target_pairs={{0,16},{16,0},{32,48},{48,32},{64,80},{80,64},{96,112},{112,96},{1... | collective-permute-start | bytes 1179656 | tf_op jit(solution)/shard_map/ppermute | solution.py:467
  40.7 0.0 collective-permute-start.18
  40.7 3.4 %collective-permute-start.19 = (f32[3,128,128]{2,1,0:T(8,128)S(1)}, f32[3,128,128]{2,1,0:T(8,128)S(1)}, u32[]{:S(2)}, u32[]{:S(2)}) collective-permute-start(f32[3,128,128]{2,1,0:T(8,128)S(1)} %get-tuple-element.109), channel_id=1, source_target_pairs={{0,96},{16,112},{32,0},{48,16},{64,32},{80,48},{96,64},{112,80},{1... | collective-permute-start | bytes 589832 | tf_op jit(solution)/shard_map/ppermute | solution.py:467
  44.0 3.4 %overflow.1 = (s32[1]{0:T(128)}, s32[513]{0:T(1024)S(1)}, f32[16,128,128]{2,1,0:T(8,128)}) custom-call(s32[2]{0:T(128)S(1)} %pad_add_fusion.me_ref, s32[40,128]{1,0:T(8,128)S(1)} %get-tuple-element.256.info_ref.refs_1_, s32[128,128]{1,0:T(8,128)S(1)} %bitcast.40, bf16[6,128,128]{2,1,0:T(8,128)(2,1)S(1)} %get-tuple-element.104.maps_ref), custom_call_target="tpu_custom_call" | custom-call | flops 1000000000 | bytes 100000 | tf_op jit(solution)/shard_map/overflow/pallas_call | solution.py:258
  47.4 0.0 collective-permute-done.14.rest_2_
  47.4 0.5 collective-permute-start.21
  47.9 7.3 %collective-permute-done.18.refs_1_.rest_13_ = f32[3,128,128]{2,1,0:T(8,128)S(1)} collective-permute-done((f32[3,128,128]{2,1,0:T(8,128)S(1)}, f32[3,128,128]{2,1,0:T(8,128)S(1)}, u32[]{:S(2)}, u32[]{:S(2)}) %collective-permute-start.18) | collective-permute-done | bytes 196640 | tf_op jit(solution)/shard_map/ppermute | solution.py:467
  55.2 1.2 %collective-permute-start.22 = (f32[8,128,128]{2,1,0:T(8,128)S(1)}, f32[8,128,128]{2,1,0:T(8,128)}, u32[]{:S(2)}, u32[]{:S(2)}) collective-permute-start(f32[8,128,128]{2,1,0:T(8,128)S(1)} %hold.2.rest_1_), channel_id=1, source_target_pairs={{0,1},{1,0},{2,3},{3,2},{4,5},{5,4},{6,7},{7,6},{8,9},{9,8},{10,11... | collective-permute-start | bytes 1572872 | tf_op jit(solution)/shard_map/ppermute | solution.py:479
  56.4 0.0 collective-permute-done.19.refs_2_.rest_12_
  56.4 0.0 collective-permute-start.23
  56.4 0.0 collective-permute-done.15.refs_0_
  56.4 0.0 collective-permute-done.20.refs_3_.rest_11_
  56.4 0.6 hold.3.rest_3_
  57.0 0.6 collective-permute-start.24
  57.6 0.0 collective-permute-done.21.rest_4_
  57.6 1.2 %collective-permute-done.22.rest_5_ = f32[8,128,128]{2,1,0:T(8,128)} collective-permute-done((f32[8,128,128]{2,1,0:T(8,128)S(1)}, f32[8,128,128]{2,1,0:T(8,128)}, u32[]{:S(2)}, u32[]{:S(2)}) %collective-permute-start.22) | collective-permute-done | bytes 524320 | tf_op jit(solution)/shard_map/ppermute | solution.py:479
  58.8 0.3 collective-permute-done.23.rest_6_
  59.0 0.7 %collective-permute-done.24.rest_7_ = f32[8,128,128]{2,1,0:T(8,128)} collective-permute-done((f32[8,128,128]{2,1,0:T(8,128)}, f32[8,128,128]{2,1,0:T(8,128)}, u32[]{:S(2)}, u32[]{:S(2)}) %collective-permute-start.24) | collective-permute-done | bytes 524320 | tf_op jit(solution)/shard_map/ppermute | solution.py:479
  59.8 3.3 %products.2 = f32[16,128,128]{2,1,0:T(8,128)} custom-call(s32[513]{0:T(1024)S(1)} %get-tuple-element.105.list_ref, f32[8,128,128]{2,1,0:T(8,128)} %get-tuple-element.260.rest_0_, f32[8,128,128]{2,1,0:T(8,128)S(1)} %hold.2.rest_1_, f32[8,128,128]{2,1,0:T(8,128)} %collective-permute-done.14.rest_2_, ...), custom_call_target="tpu_custom_call", output_to_operand_aliasing={{}: (15, {})} | custom-call | flops 100663296 | bytes 1572864 | tf_op jit(solution)/shard_map/products/pallas_call | solution.py:440
  63.1 0.6 while.10
  (22 shorter events, 0.2 us)
Async XLA Ops:
  0.0 9.3 %copy-start = (f32[1,1,4,128,128]{4,3,2,1,0:T(8,128)S(1)}, f32[1,1,4,128,128]{4,3,2,1,0:T(8,128)}, u32[]{:S(2)}) copy-start(f32[1,1,4,128,128]{4,3,2,1,0:T(8,128)} %param.7) | copy-start | bytes 786436
  1.6 7.7 %collective-permute-start.4 = (s32[128]{0:T(128)S(1)}, s32[128]{0:T(128)S(1)}, u32[]{:S(2)}, u32[]{:S(2)}) collective-permute-start(s32[128]{0:T(128)S(1)} %get-tuple-element.146), channel_id=1, source_target_pairs={{32,0},{33,1},{34,2},{35,3},{36,4},{37,5},{38,6},{39,7},{40,8},{41... | collective-permute-start | bytes 1544 | tf_op jit(solution)/shard_map/ppermute | solution.py:537
  3.7 6.8 %collective-permute-start.5 = (s32[128]{0:T(128)S(1)}, s32[128]{0:T(128)S(1)}, u32[]{:S(2)}, u32[]{:S(2)}) collective-permute-start(s32[128]{0:T(128)S(1)} %get-tuple-element.146), channel_id=1, source_target_pairs={{64,0},{65,1},{66,2},{67,3},{68,4},{69,5},{70,6},{71,7},{72,8},{73... | collective-permute-start | bytes 1544 | tf_op jit(solution)/shard_map/ppermute | solution.py:537
  6.3 4.2 %collective-permute-start.6 = (s32[128]{0:T(128)S(1)}, s32[128]{0:T(128)S(1)}, u32[]{:S(2)}, u32[]{:S(2)}) collective-permute-start(s32[128]{0:T(128)S(1)} %get-tuple-element.146), channel_id=1, source_target_pairs={{96,0},{97,1},{98,2},{99,3},{100,4},{101,5},{102,6},{103,7},{104,8... | collective-permute-start | bytes 1544 | tf_op jit(solution)/shard_map/ppermute | solution.py:537
  6.3 30.7 %collective-permute-start.16 = (f32[16,128,128]{2,1,0:T(8,128)}, f32[16,128,128]{2,1,0:T(8,128)S(1)}, u32[]{:S(2)}, u32[]{:S(2)}) collective-permute-start(f32[16,128,128]{2,1,0:T(8,128)} %bitcast.41), channel_id=1, source_target_pairs={{0,32},{16,48},{32,64},{48,80},{64,96},{80,112},{96,0},{112,16},{1... | collective-permute-start | bytes 3145736 | tf_op jit(solution)/shard_map/ppermute | solution.py:467
  6.4 30.7 %copy-start.1 = (f32[1,1,2,8,128,128]{5,4,3,2,1,0:T(8,128)S(1)}, f32[1,1,2,8,128,128]{5,4,3,2,1,0:T(8,128)}, u32[]{:S(2)}) copy-start(f32[1,1,2,8,128,128]{5,4,3,2,1,0:T(8,128)} %param.9) | copy-start | bytes 3145732
  6.5 30.5 %collective-permute-start.17 = (f32[16,128,128]{2,1,0:T(8,128)}, f32[16,128,128]{2,1,0:T(8,128)}, u32[]{:S(2)}, u32[]{:S(2)}) collective-permute-start(f32[16,128,128]{2,1,0:T(8,128)} %bitcast.42), channel_id=1, source_target_pairs={{0,96},{16,112},{32,0},{48,16},{64,32},{80,48},{96,64},{112,80},{1... | collective-permute-start | bytes 3145736 | tf_op jit(solution)/shard_map/ppermute | solution.py:467
  9.3 10.3 %collective-permute-start.3 = (f32[4,128,128]{2,1,0:T(8,128)S(1)}, f32[4,128,128]{2,1,0:T(8,128)S(1)}, u32[]{:S(2)}, u32[]{:S(2)}) collective-permute-start(f32[4,128,128]{2,1,0:T(8,128)S(1)} %bitcast.37), channel_id=1, source_target_pairs={{0,8},{1,9},{2,10},{3,11},{4,12},{5,13},{6,14},{7,15},{8,0},{9,1},... | collective-permute-start | bytes 786440 | tf_op jit(solution)/shard_map/ppermute | solution.py:479
  10.6 5.0 %collective-permute-start.7 = (s32[4,128]{1,0:T(4,128)S(1)}, s32[4,128]{1,0:T(4,128)S(1)}, u32[]{:S(2)}, u32[]{:S(2)}) collective-permute-start(s32[4,128]{1,0:T(4,128)S(1)} %dynamic_update_slice.50), channel_id=1, source_target_pairs={{2,0},{3,1},{0,2},{1,3},{6,4},{7,5},{4,6},{5,7},{10,8},{11,9},{8,1... | collective-permute-start | bytes 6152 | tf_op jit(solution)/shard_map/ppermute | solution.py:537
  12.3 5.0 %collective-permute-start.8 = (s32[4,128]{1,0:T(4,128)S(1)}, s32[4,128]{1,0:T(4,128)S(1)}, u32[]{:S(2)}, u32[]{:S(2)}) collective-permute-start(s32[4,128]{1,0:T(4,128)S(1)} %dynamic_update_slice.50), channel_id=1, source_target_pairs={{4,0},{5,1},{6,2},{7,3},{0,4},{1,5},{2,6},{3,7},{12,8},{13,9},{14,... | collective-permute-start | bytes 6152 | tf_op jit(solution)/shard_map/ppermute | solution.py:537
  15.6 3.9 %collective-permute-start.9 = (s32[4,128]{1,0:T(4,128)S(1)}, s32[4,128]{1,0:T(4,128)S(1)}, u32[]{:S(2)}, u32[]{:S(2)}) collective-permute-start(s32[4,128]{1,0:T(4,128)S(1)} %dynamic_update_slice.50), channel_id=1, source_target_pairs={{6,0},{7,1},{4,2},{5,3},{2,4},{3,5},{0,6},{1,7},{14,8},{15,9},{12,... | collective-permute-start | bytes 6152 | tf_op jit(solution)/shard_map/ppermute | solution.py:537
  20.5 3.0 %collective-permute-start.10 = (s32[4,4,128]{2,1,0:T(4,128)S(1)}, s32[4,4,128]{2,1,0:T(4,128)S(1)}, u32[]{:S(2)}, u32[]{:S(2)}) collective-permute-start(s32[4,4,128]{2,1,0:T(4,128)S(1)} %get-tuple-element.102), channel_id=1, source_target_pairs={{8,0},{9,1},{10,2},{11,3},{12,4},{13,5},{14,6},{15,7},{0,8},{1,9},... | collective-permute-start | bytes 24584 | tf_op jit(solution)/shard_map/ppermute | solution.py:537
  21.1 15.8 %collective-permute-start.13 = (f32[8,128,128]{2,1,0:T(8,128)}, f32[8,128,128]{2,1,0:T(8,128)S(1)}, u32[]{:S(2)}, u32[]{:S(2)}) collective-permute-start(f32[8,128,128]{2,1,0:T(8,128)} %get-tuple-element.260.rest_0_), channel_id=1, source_target_pairs={{0,2},{1,3},{2,4},{3,5},{4,6},{5,7},{6,0},{7,1},{8,10},{9,11},{10,... | collective-permute-start | bytes 1572872 | tf_op jit(solution)/shard_map/ppermute | solution.py:479
  23.5 4.1 %collective-permute-start.11 = (s32[2,4,4,128]{3,2,1,0:T(4,128)S(1)}, s32[2,4,4,128]{3,2,1,0:T(4,128)S(1)}, u32[]{:S(2)}, u32[]{:S(2)}) collective-permute-start(s32[2,4,4,128]{3,2,1,0:T(4,128)S(1)} %bitcast_dynamic-update-slice_fusion.4), channel_id=1, source_target_pairs={{16,0},{17,1},{18,2},{19,3},{20,4},{21,5},{22,6},{23,7},{24,8},{25... | collective-permute-start | bytes 49160 | tf_op jit(solution)/shard_map/ppermute | solution.py:537
  27.6 7.5 %collective-permute-start.12 = (s32[2,2,4,4,128]{4,3,2,1,0:T(4,128)S(1)}, s32[2,2,4,4,128]{4,3,2,1,0:T(4,128)S(1)}, u32[]{:S(2)}, u32[]{:S(2)}) collective-permute-start(s32[2,2,4,4,128]{4,3,2,1,0:T(4,128)S(1)} %bitcast_dynamic-update-slice_fusion.2), channel_id=1, source_target_pairs={{1,0},{0,1},{3,2},{2,3},{5,4},{4,5},{7,6},{6,7},{9,8},{8,9},{11,10... | collective-permute-start | bytes 98312 | tf_op jit(solution)/shard_map/ppermute | solution.py:537
  33.2 14.2 %collective-permute-start.14 = (f32[8,128,128]{2,1,0:T(8,128)}, f32[8,128,128]{2,1,0:T(8,128)}, u32[]{:S(2)}, u32[]{:S(2)}) collective-permute-start(f32[8,128,128]{2,1,0:T(8,128)} %get-tuple-element.260.rest_0_), channel_id=1, source_target_pairs={{0,6},{1,7},{2,0},{3,1},{4,2},{5,3},{6,4},{7,5},{8,14},{9,15},{10,... | collective-permute-start | bytes 1572872 | tf_op jit(solution)/shard_map/ppermute | solution.py:479
  36.9 19.5 %collective-permute-start.15 = (f32[8,128,128]{2,1,0:T(8,128)S(1)}, f32[8,128,128]{2,1,0:T(8,128)}, u32[]{:S(2)}, u32[]{:S(2)}) collective-permute-start(f32[8,128,128]{2,1,0:T(8,128)S(1)} %hold.2.rest_1_), channel_id=1, source_target_pairs={{0,2},{1,3},{2,4},{3,5},{4,6},{5,7},{6,0},{7,1},{8,10},{9,11},{10,... | collective-permute-start | bytes 1572872 | tf_op jit(solution)/shard_map/ppermute | solution.py:479
  38.6 17.8 %collective-permute-start.20 = (f32[6,128,128]{2,1,0:T(8,128)S(1)}, f32[6,128,128]{2,1,0:T(8,128)S(1)}, u32[]{:S(2)}, u32[]{:S(2)}) collective-permute-start(f32[6,128,128]{2,1,0:T(8,128)S(1)} %get-tuple-element.110), channel_id=1, source_target_pairs={{0,16},{16,0},{32,48},{48,32},{64,80},{80,64},{96,112},{112,96},{1... | collective-permute-start | bytes 1179656 | tf_op jit(solution)/shard_map/ppermute | solution.py:467
  40.7 14.6 %collective-permute-start.18 = (f32[3,128,128]{2,1,0:T(8,128)S(1)}, f32[3,128,128]{2,1,0:T(8,128)S(1)}, u32[]{:S(2)}, u32[]{:S(2)}) collective-permute-start(f32[3,128,128]{2,1,0:T(8,128)S(1)} %get-tuple-element.108), channel_id=1, source_target_pairs={{0,48},{16,32},{32,80},{48,64},{64,112},{80,96},{96,16},{112,0},{1... | collective-permute-start | bytes 589832 | tf_op jit(solution)/shard_map/ppermute | solution.py:467
  40.7 15.8 %collective-permute-start.19 = (f32[3,128,128]{2,1,0:T(8,128)S(1)}, f32[3,128,128]{2,1,0:T(8,128)S(1)}, u32[]{:S(2)}, u32[]{:S(2)}) collective-permute-start(f32[3,128,128]{2,1,0:T(8,128)S(1)} %get-tuple-element.109), channel_id=1, source_target_pairs={{0,96},{16,112},{32,0},{48,16},{64,32},{80,48},{96,64},{112,80},{1... | collective-permute-start | bytes 589832 | tf_op jit(solution)/shard_map/ppermute | solution.py:467
  47.4 10.2 %collective-permute-start.21 = (f32[8,128,128]{2,1,0:T(8,128)}, f32[8,128,128]{2,1,0:T(8,128)}, u32[]{:S(2)}, u32[]{:S(2)}) collective-permute-start(f32[8,128,128]{2,1,0:T(8,128)} %get-tuple-element.260.rest_0_), channel_id=1, source_target_pairs={{0,1},{1,0},{2,3},{3,2},{4,5},{5,4},{6,7},{7,6},{8,9},{9,8},{10,11... | collective-permute-start | bytes 1572872 | tf_op jit(solution)/shard_map/ppermute | solution.py:479
  55.2 3.5 %collective-permute-start.22 = (f32[8,128,128]{2,1,0:T(8,128)S(1)}, f32[8,128,128]{2,1,0:T(8,128)}, u32[]{:S(2)}, u32[]{:S(2)}) collective-permute-start(f32[8,128,128]{2,1,0:T(8,128)S(1)} %hold.2.rest_1_), channel_id=1, source_target_pairs={{0,1},{1,0},{2,3},{3,2},{4,5},{5,4},{6,7},{7,6},{8,9},{9,8},{10,11... | collective-permute-start | bytes 1572872 | tf_op jit(solution)/shard_map/ppermute | solution.py:479
  56.4 2.6 %collective-permute-start.23 = (f32[8,128,128]{2,1,0:T(8,128)}, f32[8,128,128]{2,1,0:T(8,128)}, u32[]{:S(2)}, u32[]{:S(2)}) collective-permute-start(f32[8,128,128]{2,1,0:T(8,128)} %collective-permute-done.14.rest_2_), channel_id=1, source_target_pairs={{0,1},{1,0},{2,3},{3,2},{4,5},{5,4},{6,7},{7,6},{8,9},{9,8},{10,11... | collective-permute-start | bytes 1572872 | tf_op jit(solution)/shard_map/ppermute | solution.py:479
  57.0 2.8 %collective-permute-start.24 = (f32[8,128,128]{2,1,0:T(8,128)}, f32[8,128,128]{2,1,0:T(8,128)}, u32[]{:S(2)}, u32[]{:S(2)}) collective-permute-start(f32[8,128,128]{2,1,0:T(8,128)} %hold.3.rest_3_), channel_id=1, source_target_pairs={{0,1},{1,0},{2,3},{3,2},{4,5},{5,4},{6,7},{7,6},{8,9},{9,8},{10,11... | collective-permute-start | bytes 1572872 | tf_op jit(solution)/shard_map/ppermute | solution.py:479
